TPU v7x, 512 devices: a whole 4x8x8 slice. The times are simulated.
512 devices in a mesh: dom: 128 (over y, z, core), feat: 4 (over x).
Axes of the slice: x: 4, y: 8, z: 8, core: 2. Of those that a mesh axis runs over, the one named last changes fastest.
Arguments:
- x_t: bfloat16 [128, 65536], P('feat', 'dom'), may hold values from -24 to 24
- w_self: bfloat16 [128, 256], P('feat'), may hold values from -0.5 to 0.5
- w_neigh: bfloat16 [128, 256], P('feat'), may hold values from -0.5 to 0.5
- in_adj: bfloat16 [1536, 128, 128], P('dom'), may hold values from 0 to 0.046875
- in_rows: int32 [1536], P('dom'), may hold values from 0 to 3
- in_cols: int32 [1536], P('dom'), may hold values from 0 to 3
- bnd_adj: bfloat16 [1536, 128, 128], P('dom'), may hold values from 0 to 0.046875
- bnd_send: int32 [1536], P('dom'), may hold values from 0 to 3
- bnd_rows: int32 [1536], P('dom'), may hold values from 0 to 3
- grad_out: bfloat16 [256, 65536], P('feat', 'dom'), may hold values from -6 to 6
Outputs:
- y_t: bfloat16 [256, 65536], P('feat', 'dom')
- grad_x: float32 [128, 65536], P('feat', 'dom')
- grad_ws: float32 [128, 256], P('feat')
- grad_wn: float32 [128, 256], P('feat')
Inputs may be any that keep to these rules, and one draw needn't show every extreme that they name: `in_rows`: a tile index within one partition. `in_cols`: a tile index within one partition. `bnd_send`: a tile index within the sending partition. `bnd_rows`: a tile index within the receiving partition.
All inputs are finite; a program needn't handle non-finite values.
Results may differ from a plain program's by a relative error of at most 0.0054.
Values may be sent and summed in bfloat16 or wider, within the bound.
No kernel may reach another device: no remote copies, remote signals or barrier semaphores. Data moves between devices by JAX's collectives and lax.ppermute only.
A program may use at most 64 MiB of HBM per device.

v0:
```python
import math

import jax
import jax.numpy as jnp
from jax import lax
from jax.sharding import PartitionSpec as P

F_HID = 256
TILE = 128
ROUNDS = 3
BT = 4


HIGHEST = lax.Precision.HIGHEST
epsilon = 1e-05


def from_partner(x, axis, stride):
    return lax.ppermute(x, axis, [(i, i ^ 1 << stride) for i in range(lax.axis_size(axis))])


def segment_onehot(targets, extent):
    return (targets[None, :] == jnp.arange(extent, dtype=jnp.int32)[:, None]).astype(jnp.float32)


def tile_apply(source, weights, take_from, put_into, flipped):
    picked = source[:, take_from, :]
    if flipped:
        product = jnp.einsum("fki,kij->fkj", picked, weights, preferred_element_type=jnp.float32)
    else:
        product = jnp.einsum("fkj,kij->fki", picked, weights, preferred_element_type=jnp.float32)
    return jnp.einsum(
        "fki,tk->fti", product, segment_onehot(put_into, source.shape[1]), precision=HIGHEST
    )


def normalize(pre_act, active, cotangent, squares, aligned):
    rscale = lax.rsqrt(squares / F_HID + epsilon)
    output = (active * rscale).astype(jnp.bfloat16)
    grad_act = rscale * cotangent - active * rscale**3 * (aligned / F_HID)
    gate_value = jax.nn.sigmoid(pre_act)
    grad_pre = (grad_act * gate_value * (1.0 + pre_act * (1.0 - gate_value))).astype(jnp.bfloat16)
    return (output, grad_pre)


def shards(x_t, w_self, w_neigh, in_adj, in_rows, in_cols, bnd_adj, bnd_send, bnd_rows, grad_out):
    feature_rows, local_nodes = x_t.shape
    tile_count = local_nodes // TILE
    levels = lax.axis_size("dom").bit_length() - 1
    swap_bits = [(number + 1) * levels // ROUNDS - 1 for number in range(ROUNDS)]
    blocks = x_t.reshape(feature_rows, tile_count, TILE)
    outgoing = [
        blocks[:, bnd_send[number * BT : (number + 1) * BT], :].reshape(feature_rows, BT * TILE)
        for number in range(ROUNDS)
    ]
    incoming = [
        from_partner(parcel_piece, "dom", bit_index)
        for bit_index, parcel_piece in zip(swap_bits, outgoing)
    ]
    inner_sum = tile_apply(blocks, in_adj, in_cols, in_rows, False)
    received = jnp.concatenate(incoming, axis=1).reshape(feature_rows, ROUNDS * BT, TILE)
    product = jnp.einsum("fsj,sij->fsi", received, bnd_adj, preferred_element_type=jnp.float32)
    outer_sum = jnp.einsum(
        "fsi,ts->fti", product, segment_onehot(bnd_rows, tile_count), precision=HIGHEST
    )
    aggregate = (inner_sum + outer_sum).reshape(feature_rows, local_nodes).astype(jnp.bfloat16)
    contract_first = (((0,), (0,)), ((), ()))
    partial_z = lax.dot_general(w_self, x_t, contract_first, preferred_element_type=jnp.float32)
    partial_z = partial_z + lax.dot_general(
        w_neigh, aggregate, contract_first, preferred_element_type=jnp.float32
    )
    hidden_part = lax.psum_scatter(partial_z, "feat", scatter_dimension=0, tiled=True)
    active = jax.nn.silu(hidden_part)
    cotangent = grad_out.astype(jnp.float32)
    squares, aligned = lax.psum(
        (jnp.sum(active * active, axis=0), jnp.sum(cotangent * active, axis=0)), "feat"
    )
    y_local, grad_local = normalize(hidden_part, active, cotangent, squares, aligned)
    grad_piece = lax.all_gather(grad_local, "feat", axis=0, tiled=True)
    self_acc = jnp.dot(w_self, grad_piece, preferred_element_type=jnp.float32)
    agg_acc = jnp.dot(w_neigh, grad_piece, preferred_element_type=jnp.float32)
    contract_last = (((1,), (1,)), ((), ()))
    wself_term = lax.dot_general(x_t, grad_piece, contract_last, preferred_element_type=jnp.float32)
    wneigh_term = lax.dot_general(
        aggregate, grad_piece, contract_last, preferred_element_type=jnp.float32
    )
    carry = (self_acc, agg_acc, wself_term, wneigh_term)
    self_part, agg_grad, wself_grad, wneigh_grad = carry
    grad_blocks = agg_grad.astype(jnp.bfloat16).reshape(feature_rows, tile_count, TILE)
    back_inner = tile_apply(grad_blocks, in_adj, in_rows, in_cols, True)
    returning = jnp.einsum(
        "fsi,sij->fsj", grad_blocks[:, bnd_rows, :], bnd_adj, preferred_element_type=jnp.float32
    )
    returning = returning.reshape(feature_rows, ROUNDS * BT * TILE)
    sendback = [
        returning[:, number * BT * TILE : (number + 1) * BT * TILE] for number in range(ROUNDS)
    ]
    backward_in = [
        from_partner(parcel_piece.astype(jnp.bfloat16), "dom", bit_index).astype(parcel_piece.dtype)
        for bit_index, parcel_piece in zip(swap_bits, sendback)
    ]
    back_tiles = jnp.concatenate(backward_in, axis=1).reshape(feature_rows, ROUNDS * BT, TILE)
    back_outer = jnp.einsum(
        "fsj,ts->ftj", back_tiles, segment_onehot(bnd_send, tile_count), precision=HIGHEST
    )
    grad_x = self_part + (back_inner + back_outer).reshape(feature_rows, local_nodes)
    summed_ws, summed_wn = lax.psum((wself_grad, wneigh_grad), "dom")
    norm_scale = 1.0 / math.sqrt(lax.axis_size("dom") * local_nodes)
    return (y_local, grad_x, summed_ws * norm_scale, summed_wn * norm_scale)


def solution(mesh):
    in_specs = (
        P("feat", "dom"),
        P("feat", None),
        P("feat", None),
        P("dom", None, None),
        P("dom"),
        P("dom"),
        P("dom", None, None),
        P("dom"),
        P("dom"),
        P("feat", "dom"),
    )
    out_specs = (P("feat", "dom"), P("feat", "dom"), P("feat", None), P("feat", None))
    return jax.shard_map(shards, mesh=mesh, in_specs=in_specs, out_specs=out_specs, check_vma=False)
```

profile of v0, /device:TPU:1, one launch (start us, length us, event | category | flops | bytes accessed | tf_op | source)
XLA Modules:
  0.0 289.3 jit_solution(13019496403652784779)
XLA Ops:
  7.2 0.0 copy-start
  7.2 0.0 reduce-scatter.2.cloned.1.call-start
  7.2 0.8 compare_select_fusion.4
  8.1 0.8 copy_bitcast_fusion.5
  8.8 0.6 gather_fusion.1
  9.4 4.8 %collective-permute-start = (bf16[32,512]{1,0:T(8,128)(2,1)S(1)}, bf16[32,512]{1,0:T(8,128)(2,1)S(1)}, u32[]{:S(2)}, u32[]{:S(2)}) collective-permute-start(bf16[32,512]{1,0:T(8,128)(2,1)S(1)} %copy_bitcast_fusion.3), channel_id=1, source_target_pairs={{0,8},{4,12},{8,0},{12,4},{16,24},{20,28},{24,16},{28,20},{32,40},... | collective-permute-start | bytes 98312 | tf_op jit(solution)/shard_map/ppermute | solution.py:19
  14.3 0.6 gather_fusion.2
  14.8 9.7 %collective-permute-start.1 = (bf16[32,512]{1,0:T(8,128)(2,1)S(1)}, bf16[32,512]{1,0:T(8,128)(2,1)S(1)}, u32[]{:S(2)}, u32[]{:S(2)}) collective-permute-start(bf16[32,512]{1,0:T(8,128)(2,1)S(1)} %copy_bitcast_fusion.2), channel_id=1, source_target_pairs={{0,32},{4,36},{8,40},{12,44},{16,48},{20,52},{24,56},{28,60},{32,0... | collective-permute-start | bytes 98312 | tf_op jit(solution)/shard_map/ppermute | solution.py:19
  24.6 0.6 gather_fusion.3
  25.1 0.0 copy-start.11
  25.2 0.0 copy-start.3
  25.2 0.0 copy-start.6
  25.2 7.5 %collective-permute-start.2 = (bf16[32,512]{1,0:T(8,128)(2,1)S(1)}, bf16[32,512]{1,0:T(8,128)(2,1)S(1)}, u32[]{:S(2)}, u32[]{:S(2)}) collective-permute-start(bf16[32,512]{1,0:T(8,128)(2,1)S(1)} %copy_bitcast_fusion.1), channel_id=1, source_target_pairs={{0,256},{4,260},{8,264},{12,268},{16,272},{20,276},{24,280},{28,28... | collective-permute-start | bytes 98312 | tf_op jit(solution)/shard_map/ppermute | solution.py:19
  32.7 0.0 copy-done.11
  32.7 0.0 copy-start.1
  32.7 0.6 gather_fusion
  33.3 0.2 fusion.39
  33.5 0.1 copy-done.1
  33.7 0.3 convolution_bitcast_fusion.3
  34.0 0.3 copy-done.10
  34.3 0.3 fusion.8
  34.7 0.0 copy-start.9
  34.7 0.0 collective-permute-done
  34.7 0.0 collective-permute-done.1
  34.7 0.0 collective-permute-done.2
  34.7 0.0 copy-done
  34.7 0.3 convolution_bitcast_fusion.2
  35.0 0.3 copy-done.9
  35.3 0.3 fusion.3
  35.7 0.4 copy-done.5
  36.0 1.1 fusion
  37.1 0.0 reduce-scatter.2.cloned.1.call-update
  37.1 0.0 all-reduce.4.cloned.1.call-start
  37.2 23.9 %reduce-scatter.2.cloned.1.call-done = f32[64,512]{1,0:T(8,128)} async-done(((f32[256,512]{1,0:T(8,128)}), f32[64,512]{1,0:T(8,128)}) %reduce-scatter.2.cloned.1.call-update) | async-done | bytes 131088 | tf_op jit(solution)/shard_map/reduce_scatter | solution.py:72
  61.1 0.0 copy-done.4
  61.1 1.0 fusion.14
  62.2 6.1 %all-reduce.1 = (f32[512]{0:T(512)S(1)}, f32[512]{0:T(512)S(1)}) all-reduce(f32[512]{0:T(512)S(1)} %get-tuple-element.5, f32[512]{0:T(512)S(1)} %get-tuple-element.4), channel_id=1, replica_groups=mesh['dom'=128,'feat'=4] {'feat'}, use_global_device_ids=true, to_apply=%region_2.3 | all-reduce | flops 1024 | bytes 8192 | tf_op jit(solution)/shard_map/psum | solution.py:75
  68.3 0.0 copy-done.2
  68.3 0.7 fusion.13
  69.0 9.4 %all_gather.3 = bf16[256,512]{1,0:T(8,128)(2,1)S(1)} all-gather(bf16[64,512]{1,0:T(8,128)(2,1)S(1)} %get-tuple-element.10), channel_id=1, replica_groups=mesh['dom'=128,'feat'=4] {'feat'}, dimensions={0}, use_global_device_ids=true | all-gather | bytes 327680 | tf_op jit(solution)/shard_map/all_gather | solution.py:79
  78.3 0.8 fusion.21
  79.1 0.8 convolution_bitcast_fusion.5
  80.0 0.1 fusion.4
  80.1 0.6 gather_fusion.5
  80.7 0.2 fusion.1
  80.9 4.2 %collective-permute-start.3 = (bf16[32,512]{1,0:T(8,128)(2,1)S(1)}, bf16[32,512]{1,0:T(8,128)(2,1)S(1)}, u32[]{:S(2)}, u32[]{:S(2)}) collective-permute-start(bf16[32,512]{1,0:T(8,128)(2,1)S(1)} %get-tuple-element.12), channel_id=1, source_target_pairs={{0,8},{4,12},{8,0},{12,4},{16,24},{20,28},{24,16},{28,20},{32,40},... | collective-permute-start | bytes 98312 | tf_op jit(solution)/shard_map/ppermute | solution.py:19
  85.1 7.1 %collective-permute-start.5 = (bf16[32,512]{1,0:T(8,128)(2,1)S(1)}, bf16[32,512]{1,0:T(8,128)(2,1)S(1)}, u32[]{:S(2)}, u32[]{:S(2)}) collective-permute-start(bf16[32,512]{1,0:T(8,128)(2,1)S(1)} %get-tuple-element.13), channel_id=1, source_target_pairs={{0,256},{4,260},{8,264},{12,268},{16,272},{20,276},{24,280},{28,28... | collective-permute-start | bytes 98312 | tf_op jit(solution)/shard_map/ppermute | solution.py:19
  92.2 6.9 %collective-permute-start.4 = (bf16[32,512]{1,0:T(8,128)(2,1)S(1)}, bf16[32,512]{1,0:T(8,128)(2,1)S(1)}, u32[]{:S(2)}, u32[]{:S(2)}) collective-permute-start(bf16[32,512]{1,0:T(8,128)(2,1)S(1)} %get-tuple-element.14), channel_id=1, source_target_pairs={{0,32},{4,36},{8,40},{12,44},{16,48},{20,52},{24,56},{28,60},{32,0... | collective-permute-start | bytes 98312 | tf_op jit(solution)/shard_map/ppermute | solution.py:19
  99.1 0.6 gather_fusion.4
  99.6 0.2 convolution_bitcast_fusion.1
  99.9 0.0 all-reduce.4.cloned.1.call-update
  99.9 0.3 fusion.5
  100.2 178.6 %all-reduce.4.cloned.1.call-done = (f32[32,256]{1,0:T(8,128)}, f32[32,256]{1,0:T(8,128)}) async-done(((f32[32,256]{1,0:T(8,128)}, f32[32,256]{1,0:T(8,128)}), (f32[32,256]{1,0:T(8,128)}, f32[32,256]{1,0:T(8,128)})) %all-reduce.4.cloned.1.call-update) | async-done | bytes 65552 | tf_op jit(solution)/shard_map/psum | solution.py:107
  278.9 1.4 broadcast_multiply_fusion.1
  280.2 0.0 copy-done.7
  280.2 0.6 broadcast_multiply_fusion
  280.9 0.0 collective-permute-done.3
  280.9 0.0 collective-permute-done.5
  280.9 0.0 collective-permute-done.4
  280.9 0.0 copy-start.8
  280.9 0.1 reshape.54
  281.0 0.6 copy-done.8
  281.5 0.1 convolution_add_fusion
  281.7 0.8 fusion.2
  (24 shorter events, 0.1 us)
Async XLA Ops:
  7.2 27.6 %copy-start = (bf16[12,128,128]{2,1,0:T(8,128)(2,1)S(1)}, bf16[12,128,128]{2,1,0:T(8,128)(2,1)}, u32[]{:S(2)}) copy-start(bf16[12,128,128]{2,1,0:T(8,128)(2,1)} %param.16) | copy-start | bytes 1179652
  7.2 53.9 %reduce-scatter.2.cloned.1.call-start = ((), (), s32[]{:S(2)}) async-start(), calls=%async_computation.1 | async-start | bytes 655360 | tf_op jit(solution)/shard_map/reduce_scatter | solution.py:72
  9.4 25.3 %collective-permute-start = (bf16[32,512]{1,0:T(8,128)(2,1)S(1)}, bf16[32,512]{1,0:T(8,128)(2,1)S(1)}, u32[]{:S(2)}, u32[]{:S(2)}) collective-permute-start(bf16[32,512]{1,0:T(8,128)(2,1)S(1)} %copy_bitcast_fusion.3), channel_id=1, source_target_pairs={{0,8},{4,12},{8,0},{12,4},{16,24},{20,28},{24,16},{28,20},{32,40},... | collective-permute-start | bytes 98312 | tf_op jit(solution)/shard_map/ppermute | solution.py:19
  14.8 19.9 %collective-permute-start.1 = (bf16[32,512]{1,0:T(8,128)(2,1)S(1)}, bf16[32,512]{1,0:T(8,128)(2,1)S(1)}, u32[]{:S(2)}, u32[]{:S(2)}) collective-permute-start(bf16[32,512]{1,0:T(8,128)(2,1)S(1)} %copy_bitcast_fusion.2), channel_id=1, source_target_pairs={{0,32},{4,36},{8,40},{12,44},{16,48},{20,52},{24,56},{28,60},{32,0... | collective-permute-start | bytes 98312 | tf_op jit(solution)/shard_map/ppermute | solution.py:19
  25.1 7.5 %copy-start.11 = (s32[12]{0:T(128)S(1)}, s32[12]{0:T(128)}, u32[]{:S(2)}) copy-start(s32[12]{0:T(128)} %param.15) | copy-start | bytes 148
  25.2 8.1 %copy-start.3 = (bf16[32,512]{1,0:T(8,128)(2,1)S(1)}, bf16[32,512]{1,0:T(8,128)(2,1)}, u32[]{:S(2)}) copy-start(bf16[32,512]{1,0:T(8,128)(2,1)} %param.10) | copy-start | bytes 98308
  25.2 8.1 %copy-start.6 = (bf16[32,256]{1,0:T(8,128)(2,1)S(1)}, bf16[32,256]{1,0:T(8,128)(2,1)}, u32[]{:S(2)}) copy-start(bf16[32,256]{1,0:T(8,128)(2,1)} %param.11) | copy-start | bytes 49156
  25.2 9.5 %collective-permute-start.2 = (bf16[32,512]{1,0:T(8,128)(2,1)S(1)}, bf16[32,512]{1,0:T(8,128)(2,1)S(1)}, u32[]{:S(2)}, u32[]{:S(2)}) collective-permute-start(bf16[32,512]{1,0:T(8,128)(2,1)S(1)} %copy_bitcast_fusion.1), channel_id=1, source_target_pairs={{0,256},{4,260},{8,264},{12,268},{16,272},{20,276},{24,280},{28,28... | collective-permute-start | bytes 98312 | tf_op jit(solution)/shard_map/ppermute | solution.py:19
  32.7 1.0 copy-start.1
  33.7 0.7 copy-start.10
  34.7 0.7 copy-start.9
  35.3 0.7 copy-start.5
  37.1 24.0 %copy-start.4 = (bf16[64,512]{1,0:T(8,128)(2,1)S(1)}, bf16[64,512]{1,0:T(8,128)(2,1)}, u32[]{:S(2)}) copy-start(bf16[64,512]{1,0:T(8,128)(2,1)} %param.19) | copy-start | bytes 196612
  37.1 241.7 %all-reduce.4.cloned.1.call-start = ((), (), s32[]{:S(2)}) async-start(), calls=%async_computation.2 | async-start | bytes 131072 | tf_op jit(solution)/shard_map/psum | solution.py:107
  61.1 7.2 %copy-start.2 = (f32[64,512]{1,0:T(8,128)S(1)}, f32[64,512]{1,0:T(8,128)}, u32[]{:S(2)}) copy-start(f32[64,512]{1,0:T(8,128)} %reduce-scatter.2.cloned.1.call-done) | copy-start | bytes 393220
  80.9 199.9 %collective-permute-start.3 = (bf16[32,512]{1,0:T(8,128)(2,1)S(1)}, bf16[32,512]{1,0:T(8,128)(2,1)S(1)}, u32[]{:S(2)}, u32[]{:S(2)}) collective-permute-start(bf16[32,512]{1,0:T(8,128)(2,1)S(1)} %get-tuple-element.12), channel_id=1, source_target_pairs={{0,8},{4,12},{8,0},{12,4},{16,24},{20,28},{24,16},{28,20},{32,40},... | collective-permute-start | bytes 98312 | tf_op jit(solution)/shard_map/ppermute | solution.py:19
  85.1 195.8 %collective-permute-start.5 = (bf16[32,512]{1,0:T(8,128)(2,1)S(1)}, bf16[32,512]{1,0:T(8,128)(2,1)S(1)}, u32[]{:S(2)}, u32[]{:S(2)}) collective-permute-start(bf16[32,512]{1,0:T(8,128)(2,1)S(1)} %get-tuple-element.13), channel_id=1, source_target_pairs={{0,256},{4,260},{8,264},{12,268},{16,272},{20,276},{24,280},{28,28... | collective-permute-start | bytes 98312 | tf_op jit(solution)/shard_map/ppermute | solution.py:19
  92.2 188.7 %collective-permute-start.4 = (bf16[32,512]{1,0:T(8,128)(2,1)S(1)}, bf16[32,512]{1,0:T(8,128)(2,1)S(1)}, u32[]{:S(2)}, u32[]{:S(2)}) collective-permute-start(bf16[32,512]{1,0:T(8,128)(2,1)S(1)} %get-tuple-element.14), channel_id=1, source_target_pairs={{0,32},{4,36},{8,40},{12,44},{16,48},{20,52},{24,56},{28,60},{32,0... | collective-permute-start | bytes 98312 | tf_op jit(solution)/shard_map/ppermute | solution.py:19
  278.8 1.4 copy-start.7
  280.9 0.7 copy-start.8
Sparse Core Ops, SparseCore 0:
  37.3 23.7 reduce-scatter.1
  100.0 178.7 all-reduce.3
where the time goes:
time: 290 us; the launch traced here: 289 us
  waiting for transfers between devices  203 us (70%)
  starting transfers between devices  40.2 us (14%)
  blocking collectives  15.4 us (5%)
  between operations  14.4 us (5%)
  local copies, waits for them, and re-layouts  6.09 us (2%)
  matrix products  5.96 us (2%)
  other arithmetic  4.67 us (2%)
    psum x1, waiting for transfers between devices, shards(): summed_ws, summed_wn = lax.psum((wself_grad, wneigh_grad), 'dom')  179 us
    ppermute x6, starting transfers between devices, from_partner(): lax.ppermute(x, axis, [(i, i ^ 1 << stride) for i in range(lax.axis_size(...  40.1 us
    reduce_scatter x1, waiting for transfers between devices, shards(): lax.psum_scatter(partial_z, 'feat', scatter_dimension=0, tiled=True)  23.9 us
    all_gather x1, blocking collectives, shards(): grad_piece = lax.all_gather(grad_local, 'feat', axis=0, tiled=True)  9.36 us
    psum x1, blocking collectives, shards(): lax.psum((jnp.sum(active * active, axis=0), jnp.sum(cotangent * active, a...  6.09 us
  transfers between devices with their start and end apart: 8, of which 2 were waited for; matrix products, arithmetic and copies ran while one was open for 2% of the time, Pallas kernels for 0%

commit v1 on v0

v1 whole, which is shorter than its diff:
```python
import math

import jax
import jax.numpy as jnp
from jax import lax
from jax.experimental import pallas as pl
from jax.experimental.pallas import tpu as pltpu
from jax.sharding import Mesh
from jax.sharding import PartitionSpec as P

F_IN = 128
F_HID = 256
TILE = 128
TILES = 4
ROUNDS = 3
BT = 4
KIN = 12
NODES = 65536
NF = 4
FR = F_IN // NF
HR = F_HID // NF
LOCAL = TILES * TILE
EPS = 1e-05

AXES = ("y2", "yl", "z2", "z1", "z0", "c", "f")
SIZES = (2, 4, 2, 2, 2, 2, 4)
DOM = AXES[:6]
Y = ("y2", "yl")
ZC = ("z2", "z1", "z0", "c")
PAIRS = ("z0", "z2", "y2")

R_AGG, R_X, R_G, R_W = 0, FR, 2 * FR, 2 * FR + HR
ROWS = R_W + FR

SMEM = pl.BlockSpec(memory_space=pltpu.SMEM)
VMEM = pl.BlockSpec(memory_space=pltpu.VMEM)
f32, bf16 = jnp.float32, jnp.bfloat16


def lanes(tile):
    return pl.ds(pl.multiple_of(tile * TILE, TILE), TILE)


def pick_kernel(send, x, *outs):
    for r in range(ROUNDS):
        for b in range(BT):
            outs[r][:, b * TILE : (b + 1) * TILE] = x[:, lanes(send[r * BT + b])]


def agg_kernel(rows, cols, brows, x, r0, r1, r2, adj, badj, g, ws, wn, out, acc):
    nt = (((1,), (1,)), ((), ()))
    acc[...] = jnp.zeros_like(acc)
    for k in range(KIN):
        acc[rows[k]] += lax.dot_general(
            x[:, lanes(cols[k])], adj[k], nt, preferred_element_type=f32
        )
    got = (r0, r1, r2)
    for s in range(ROUNDS * BT):
        b = s % BT
        acc[brows[s]] += lax.dot_general(
            got[s // BT][:, b * TILE : (b + 1) * TILE], badj[s], nt, preferred_element_type=f32
        )
    for i in range(NF):
        for t in range(TILES):
            out[i, R_AGG : R_AGG + FR, t * TILE : (t + 1) * TILE] = acc[t].astype(bf16)
        out[i, R_X : R_X + FR, :] = x[...]
        out[i, R_G : R_G + HR, :] = g[...]
        out[i, R_W : R_W + FR, :F_HID] = ws[...]
        out[i, R_W : R_W + FR, F_HID:] = wn[...]


def node_kernel(me, got, y, gp, wg, lhs, rhs, act_all):
    for i in range(NF):
        lhs[i * FR : (i + 1) * FR, :] = got[i, R_W : R_W + FR, :F_HID]
        lhs[F_IN + i * FR : F_IN + (i + 1) * FR, :] = got[i, R_W : R_W + FR, F_HID:]
        rhs[i * FR : (i + 1) * FR, :] = got[i, R_X : R_X + FR, :]
        rhs[F_IN + i * FR : F_IN + (i + 1) * FR, :] = got[i, R_AGG : R_AGG + FR, :]
    tn = (((0,), (0,)), ((), ()))
    pre = lax.dot_general(lhs[...], rhs[...], tn, preferred_element_type=f32)
    gate = 1.0 / (1.0 + jnp.exp(-pre))
    act = pre * gate
    act_all[...] = act
    g = jnp.concatenate([got[i, R_G : R_G + HR, :] for i in range(NF)], axis=0).astype(f32)
    sq = jnp.sum(act * act, axis=0, keepdims=True)
    al = jnp.sum(g * act, axis=0, keepdims=True)
    rs = lax.rsqrt(sq / F_HID + EPS)
    coef = rs * rs * rs * (al / F_HID)
    grad_act = rs * g - act * coef
    grad = (grad_act * gate * (1.0 + pre * (1.0 - gate))).astype(bf16)
    gp[...] = grad
    f = me[0]
    y[...] = (act_all[pl.ds(pl.multiple_of(f * HR, HR), HR), :] * rs).astype(bf16)
    w = lax.dot_general(
        got[f, R_AGG : R_AGG + 2 * FR, :], grad, (((1,), (1,)), ((), ())), preferred_element_type=f32
    ) * (1.0 / math.sqrt(NODES))
    for j in range(8):
        wg[j] = w[j * 8 : (j + 1) * 8, :]


def back_kernel(rows, cols, brows, gp, ws, wn, adj, badj, base, b0, b1, b2, acc, ga):
    own = jnp.dot(ws[...], gp[...], preferred_element_type=f32)
    grad_agg = jnp.dot(wn[...], gp[...], preferred_element_type=f32).astype(bf16)
    for t in range(TILES):
        acc[t] = own[:, t * TILE : (t + 1) * TILE]
        ga[t] = grad_agg[:, t * TILE : (t + 1) * TILE]
    outs = (b0, b1, b2)
    for s in range(ROUNDS * BT):
        b = s % BT
        outs[s // BT][:, b * TILE : (b + 1) * TILE] = jnp.dot(
            ga[brows[s]], badj[s], preferred_element_type=f32
        ).astype(bf16)
    for k in range(KIN):
        acc[cols[k]] += jnp.dot(ga[rows[k]], adj[k], preferred_element_type=f32)
    for t in range(TILES):
        base[:, t * TILE : (t + 1) * TILE] = acc[t]


def join_kernel(send, base, c0, c1, c2, out):
    out[...] = base[...]
    got = (c0, c1, c2)
    for s in range(ROUNDS * BT):
        b = s % BT
        out[:, lanes(send[s])] += got[s // BT][:, b * TILE : (b + 1) * TILE].astype(f32)


def call(kernel, ins, outs, scratch=(), flops=0, nbytes=1 << 20):
    many = isinstance(outs, tuple)
    return pl.pallas_call(
        kernel,
        out_shape=outs,
        in_specs=[SMEM if i else VMEM for i in ins],
        out_specs=tuple(VMEM for _ in outs) if many else VMEM,
        scratch_shapes=list(scratch),
        cost_estimate=pl.CostEstimate(flops=flops, bytes_accessed=nbytes, transcendentals=0),
    )


def swap(x, axis):
    return lax.ppermute(x, axis, [(0, 1), (1, 0)])


def shards(x, ws, wn, in_adj, in_rows, in_cols, bnd_adj, bnd_send, bnd_rows, g):
    S = jax.ShapeDtypeStruct
    part = S((FR, LOCAL), bf16)
    picked = call(pick_kernel, (1, 0), (part,) * 3)(bnd_send, x)
    got = [swap(picked[r], PAIRS[r]) for r in range(ROUNDS)]
    give = call(
        agg_kernel,
        (1, 1, 1) + (0,) * 9,
        S((NF, ROWS, LOCAL), bf16),
        (pltpu.VMEM((TILES, FR, TILE), f32),),
    )(in_rows, in_cols, bnd_rows, x, *got, in_adj, bnd_adj, g, ws, wn)
    block = lax.all_to_all(give, "f", 0, 0, tiled=True)
    me = lax.axis_index("f").astype(jnp.int32).reshape(1)
    y, gp, wg = call(
        node_kernel,
        (1, 0),
        (S((HR, LOCAL), bf16), S((F_HID, LOCAL), bf16), S((8, 8, F_HID), f32)),
        (
            pltpu.VMEM((2 * F_IN, F_HID), bf16),
            pltpu.VMEM((2 * F_IN, LOCAL), bf16),
            pltpu.VMEM((F_HID, LOCAL), f32),
        ),
    )(me, block)
    wg = lax.all_to_all(wg, Y, 0, 0, tiled=True)
    base, *back = call(
        back_kernel,
        (1, 1, 1) + (0,) * 5,
        (S((FR, LOCAL), f32),) + (part,) * 3,
        (pltpu.VMEM((TILES, FR, TILE), f32), pltpu.VMEM((TILES, FR, TILE), bf16)),
    )(in_rows, in_cols, bnd_rows, gp, ws, wn, in_adj, bnd_adj)
    wg = jnp.broadcast_to(jnp.sum(wg, axis=0), (16, 8, F_HID))
    wg = lax.all_to_all(wg, ZC, 0, 0, tiled=True)
    home = [swap(back[r], PAIRS[r]) for r in range(ROUNDS)]
    wg = jnp.broadcast_to(jnp.sum(wg, axis=0), (8, 8, F_HID))
    wg = lax.all_to_all(wg, Y, 0, 0, tiled=True).reshape(2 * FR, F_HID)
    grad_x = call(join_kernel, (1,) + (0,) * 4, S((FR, LOCAL), f32))(bnd_send, base, *home)
    return y, grad_x, wg[FR:], wg[:FR]


def solution(mesh):
    fine = Mesh(mesh.devices.reshape(SIZES), AXES)
    in_specs = (
        P("f", DOM),
        P("f", None),
        P("f", None),
        P(DOM, None, None),
        P(DOM),
        P(DOM),
        P(DOM, None, None),
        P(DOM),
        P(DOM),
        P("f", DOM),
    )
    out_specs = (P("f", DOM), P("f", DOM), P("f", None), P("f", None))
    return jax.shard_map(shards, mesh=fine, in_specs=in_specs, out_specs=out_specs, check_vma=False)
```

time: 290 us -> 102 us (0.35)
  the two profiles are of different devices: /device:TPU:1 before, /device:TPU:32 now
where the time goes in v1:
time: 102 us; the launch traced here: 101 us
  starting transfers between devices  38.3 us (38%)
  waiting for transfers between devices  25.6 us (25%)
  blocking collectives  22.4 us (22%)
  Pallas kernels  10.5 us (10%)
  local copies, waits for them, and re-layouts  3.34 us (3%)
    ppermute x6, starting transfers between devices, swap(): return lax.ppermute(x, axis, [(0, 1), (1, 0)])  25.2 us
    ppermute x6, waiting for transfers between devices, swap(): return lax.ppermute(x, axis, [(0, 1), (1, 0)])  16.4 us
    all_to_all x1, blocking collectives, shards(): wg = lax.all_to_all(wg, ZC, 0, 0, tiled=True)  12.3 us
    all_to_all x1, blocking collectives, shards(): wg = lax.all_to_all(wg, Y, 0, 0, tiled=True)  10.1 us
    all_to_all x1, waiting for transfers between devices, shards(): block = lax.all_to_all(give, 'f', 0, 0, tiled=True)  9.26 us
    all_to_all x1, starting transfers between devices, shards(): wg = lax.all_to_all(wg, Y, 0, 0, tiled=True).reshape(2 * FR, F_HID)  8.73 us
    all_to_all x1, starting transfers between devices, shards(): block = lax.all_to_all(give, 'f', 0, 0, tiled=True)  4.29 us
    pallas_call x1, Pallas kernels, shards(): call(agg_kernel, (1, 1, 1) + (0,) * 9, S((NF, ROWS, LOCAL), bf16), (pltpu...  2.62 us
  transfers between devices with their start and end apart: 8, of which 5 were waited for; matrix products, arithmetic and copies ran while one was open for 0% of the time, Pallas kernels for 4%

profile of v1, /device:TPU:32, one launch (start us, length us, event | category | flops | bytes accessed | tf_op | source)
XLA Modules:
  0.0 100.9 jit_solution(7257450999541362774)
XLA Ops:
  0.6 1.4 %shard_map.129 = (bf16[32,512]{1,0:T(8,128)(2,1)}, bf16[32,512]{1,0:T(8,128)(2,1)}, bf16[32,512]{1,0:T(8,128)(2,1)}) custom-call(s32[12]{0:T(128)} %send.3, bf16[32,512]{1,0:T(8,128)(2,1)} %x.3), custom_call_target="tpu_custom_call" | custom-call | bytes 1048576 | tf_op jit(solution)/shard_map/pallas_call | solution.py:145
  2.1 4.3 %collective-permute-start = (bf16[32,512]{1,0:T(8,128)(2,1)}, bf16[32,512]{1,0:T(8,128)(2,1)S(1)}, u32[]{:S(2)}, u32[]{:S(2)}) collective-permute-start(bf16[32,512]{1,0:T(8,128)(2,1)} %get-tuple-element.14), channel_id=1, source_target_pairs={{0,8},{8,0},{1,9},{9,1},{2,10},{10,2},{3,11},{11,3},{4,12},{12,4},... | collective-permute-start | bytes 98312 | tf_op jit(solution)/shard_map/ppermute | solution.py:139
  6.3 10.0 %collective-permute-start.1 = (bf16[32,512]{1,0:T(8,128)(2,1)}, bf16[32,512]{1,0:T(8,128)(2,1)S(1)}, u32[]{:S(2)}, u32[]{:S(2)}) collective-permute-start(bf16[32,512]{1,0:T(8,128)(2,1)} %get-tuple-element.15), channel_id=1, source_target_pairs={{0,32},{32,0},{1,33},{33,1},{2,34},{34,2},{3,35},{35,3},{4,36},{36... | collective-permute-start | bytes 98312 | tf_op jit(solution)/shard_map/ppermute | solution.py:139
  16.4 2.0 %collective-permute-start.2 = (bf16[32,512]{1,0:T(8,128)(2,1)}, bf16[32,512]{1,0:T(8,128)(2,1)S(1)}, u32[]{:S(2)}, u32[]{:S(2)}) collective-permute-start(bf16[32,512]{1,0:T(8,128)(2,1)} %get-tuple-element.16), channel_id=1, source_target_pairs={{0,256},{256,0},{1,257},{257,1},{2,258},{258,2},{3,259},{259,3},{4... | collective-permute-start | bytes 98312 | tf_op jit(solution)/shard_map/ppermute | solution.py:139
  18.4 0.0 collective-permute-done.r0
  18.4 0.0 copy-start.2
  18.4 0.1 collective-permute-done.1.r1
  18.5 0.0 copy-start.4
  18.5 8.0 %collective-permute-done.2.r2 = bf16[32,512]{1,0:T(8,128)(2,1)S(1)} collective-permute-done((bf16[32,512]{1,0:T(8,128)(2,1)}, bf16[32,512]{1,0:T(8,128)(2,1)S(1)}, u32[]{:S(2)}, u32[]{:S(2)}) %collective-permute-start.2) | collective-permute-done | bytes 32800 | tf_op jit(solution)/shard_map/ppermute | solution.py:139
  26.5 0.0 copy-done.2
  26.5 0.0 copy-done.4
  26.5 0.0 copy-start.6
  26.5 0.6 copy-done.6
  27.2 2.6 %shard_map.130 = bf16[4,160,512]{2,1,0:T(8,128)(2,1)} custom-call(s32[12]{0:T(128)} %rows.3, s32[12]{0:T(128)} %cols.3, s32[12]{0:T(128)} %brows.3, bf16[32,512]{1,0:T(8,128)(2,1)} %x.3, bf16[32,512]{1,0:T(8,128)(2,1)} %copy-done.2, bf16[32,512]{1,0:T(8,128)(2,1)} %copy-done.4, bf16[32,512]{1,0:T(8,128)(2,1)} %copy-done.6, bf16[12,128,128]{2,1,0:T(8,128)(2,1)} %adj.3, ...), custom_call_target="tpu_custom_call" | custom-call | bytes 1048576 | tf_op jit(solution)/shard_map/pallas_call | solution.py:147
  29.8 4.3 %all-to-all-start = ((bf16[4,160,512]{2,1,0:T(8,128)(2,1)}), bf16[4,160,512]{2,1,0:T(8,128)(2,1)S(1)}, u32[]{:S(2)}, u32[]{:S(2)}) async-start(bf16[4,160,512]{2,1,0:T(8,128)(2,1)} %shard_map.130), calls=%async_computation | async-start | bytes 1310720 | tf_op jit(solution)/shard_map/all_to_all | solution.py:153
  34.1 9.3 %all-to-all-done.got = bf16[4,160,512]{2,1,0:T(8,128)(2,1)S(1)} async-done(((bf16[4,160,512]{2,1,0:T(8,128)(2,1)}), bf16[4,160,512]{2,1,0:T(8,128)(2,1)S(1)}, u32[]{:S(2)}, u32[]{:S(2)}) %all-to-all-start) | async-done | bytes 655392 | tf_op jit(solution)/shard_map/all_to_all | solution.py:153
  43.3 0.0 copy-start
  43.3 0.8 copy-done
  44.2 2.5 %shard_map.131 = (bf16[64,512]{1,0:T(8,128)(2,1)}, bf16[256,512]{1,0:T(8,128)(2,1)}, f32[8,8,256]{2,1,0:T(8,128)}) custom-call(s32[1]{0:T(128)} %bitcast.me, bf16[4,160,512]{2,1,0:T(8,128)(2,1)} %copy-done), custom_call_target="tpu_custom_call" | custom-call | bytes 1048576 | tf_op jit(solution)/shard_map/pallas_call | solution.py:155
  46.7 10.1 %all_to_all.20 = f32[8,8,256]{2,1,0:T(8,128)S(1)} all-to-all(f32[8,8,256]{2,1,0:T(8,128)} %get-tuple-element.23), channel_id=1, replica_groups=mesh['y2'=2,'yl'=4,'z2'=2,'z1'=2,'z0'=2,'c'=2,'f'=4] {'y2','yl'}, dimensions={0} | all-to-all | bytes 131072 | tf_op jit(solution)/shard_map/all_to_all | solution.py:165
  56.9 12.3 %all_to_all.21 = f32[16,8,256]{2,1,0:T(8,128)S(1)} all-to-all(f32[16,8,256]{2,1,0:T(8,128)S(1)} %broadcast_in_dim.6), channel_id=1, replica_groups=mesh['y2'=2,'yl'=4,'z2'=2,'z1'=2,'z0'=2,'c'=2,'f'=4] {'z2','z1','z0','c'}, dimensions={0} | all-to-all | bytes 262144 | tf_op jit(solution)/shard_map/all_to_all | solution.py:173
  69.2 0.6 broadcast_in_dim.7
  69.8 8.7 %all-to-all-start.3 = ((f32[8,8,256]{2,1,0:T(8,128)}), f32[8,8,256]{2,1,0:T(8,128)S(1)}, u32[]{:S(2)}, u32[]{:S(2)}) async-start(f32[8,8,256]{2,1,0:T(8,128)} %broadcast_in_dim.7), calls=%async_computation.3 | async-start | bytes 131072 | tf_op jit(solution)/shard_map/all_to_all | solution.py:176
  78.5 2.4 %shard_map.132 = (f32[32,512]{1,0:T(8,128)}, bf16[32,512]{1,0:T(8,128)(2,1)}, bf16[32,512]{1,0:T(8,128)(2,1)}, bf16[32,512]{1,0:T(8,128)(2,1)}) custom-call(s32[12]{0:T(128)} %rows.3, s32[12]{0:T(128)} %cols.3, s32[12]{0:T(128)} %brows.3, bf16[256,512]{1,0:T(8,128)(2,1)} %get-tuple-element.18.gp, bf16[32,256]{1,0:T(8,128)(2,1)} %ws.3, bf16[32,256]{1,0:T(8,128)(2,1)} %wn.3, ...), custom_call_target="tpu_custom_call" | custom-call | bytes 1048576 | tf_op jit(solution)/shard_map/pallas_call | solution.py:166
  80.9 2.5 %collective-permute-start.3 = (bf16[32,512]{1,0:T(8,128)(2,1)}, bf16[32,512]{1,0:T(8,128)(2,1)S(1)}, u32[]{:S(2)}, u32[]{:S(2)}) collective-permute-start(bf16[32,512]{1,0:T(8,128)(2,1)} %get-tuple-element.20), channel_id=1, source_target_pairs={{0,8},{8,0},{1,9},{9,1},{2,10},{10,2},{3,11},{11,3},{4,12},{12,4},... | collective-permute-start | bytes 98312 | tf_op jit(solution)/shard_map/ppermute | solution.py:139
  83.4 4.5 %collective-permute-start.4 = (bf16[32,512]{1,0:T(8,128)(2,1)}, bf16[32,512]{1,0:T(8,128)(2,1)S(1)}, u32[]{:S(2)}, u32[]{:S(2)}) collective-permute-start(bf16[32,512]{1,0:T(8,128)(2,1)} %get-tuple-element.21), channel_id=1, source_target_pairs={{0,32},{32,0},{1,33},{33,1},{2,34},{34,2},{3,35},{35,3},{4,36},{36... | collective-permute-start | bytes 98312 | tf_op jit(solution)/shard_map/ppermute | solution.py:139
  87.9 2.0 %collective-permute-start.5 = (bf16[32,512]{1,0:T(8,128)(2,1)}, bf16[32,512]{1,0:T(8,128)(2,1)S(1)}, u32[]{:S(2)}, u32[]{:S(2)}) collective-permute-start(bf16[32,512]{1,0:T(8,128)(2,1)} %get-tuple-element.22), channel_id=1, source_target_pairs={{0,256},{256,0},{1,257},{257,1},{2,258},{258,2},{3,259},{259,3},{4... | collective-permute-start | bytes 98312 | tf_op jit(solution)/shard_map/ppermute | solution.py:139
  89.9 0.0 collective-permute-done.3.c0
  89.9 0.0 copy-start.1
  89.9 3.5 %collective-permute-done.4.c1 = bf16[32,512]{1,0:T(8,128)(2,1)S(1)} collective-permute-done((bf16[32,512]{1,0:T(8,128)(2,1)}, bf16[32,512]{1,0:T(8,128)(2,1)S(1)}, u32[]{:S(2)}, u32[]{:S(2)}) %collective-permute-start.4) | collective-permute-done | bytes 32800 | tf_op jit(solution)/shard_map/ppermute | solution.py:139
  93.4 0.0 copy-start.3
  93.4 4.7 %collective-permute-done.5.c2 = bf16[32,512]{1,0:T(8,128)(2,1)S(1)} collective-permute-done((bf16[32,512]{1,0:T(8,128)(2,1)}, bf16[32,512]{1,0:T(8,128)(2,1)S(1)}, u32[]{:S(2)}, u32[]{:S(2)}) %collective-permute-start.5) | collective-permute-done | bytes 32800 | tf_op jit(solution)/shard_map/ppermute | solution.py:139
  98.1 0.0 copy-start.5
  98.1 0.0 copy-done.1
  98.1 0.0 copy-done.3
  98.1 0.6 copy-done.5
  98.7 1.6 %shard_map.133 = f32[32,512]{1,0:T(8,128)} custom-call(s32[12]{0:T(128)} %send.3, f32[32,512]{1,0:T(8,128)} %get-tuple-element.19.base, bf16[32,512]{1,0:T(8,128)(2,1)} %copy-done.1, bf16[32,512]{1,0:T(8,128)(2,1)} %copy-done.3, bf16[32,512]{1,0:T(8,128)(2,1)} %copy-done.5), custom_call_target="tpu_custom_call" | custom-call | bytes 1048576 | tf_op jit(solution)/shard_map/pallas_call | solution.py:177
  100.3 0.0 all-to-all-done.3
  100.3 0.6 slice_bitcast_fusion
  (3 shorter events, 0.0 us)
Async XLA Ops:
  2.1 16.3 %collective-permute-start = (bf16[32,512]{1,0:T(8,128)(2,1)}, bf16[32,512]{1,0:T(8,128)(2,1)S(1)}, u32[]{:S(2)}, u32[]{:S(2)}) collective-permute-start(bf16[32,512]{1,0:T(8,128)(2,1)} %get-tuple-element.14), channel_id=1, source_target_pairs={{0,8},{8,0},{1,9},{9,1},{2,10},{10,2},{3,11},{11,3},{4,12},{12,4},... | collective-permute-start | bytes 98312 | tf_op jit(solution)/shard_map/ppermute | solution.py:139
  6.3 12.1 %collective-permute-start.1 = (bf16[32,512]{1,0:T(8,128)(2,1)}, bf16[32,512]{1,0:T(8,128)(2,1)S(1)}, u32[]{:S(2)}, u32[]{:S(2)}) collective-permute-start(bf16[32,512]{1,0:T(8,128)(2,1)} %get-tuple-element.15), channel_id=1, source_target_pairs={{0,32},{32,0},{1,33},{33,1},{2,34},{34,2},{3,35},{35,3},{4,36},{36... | collective-permute-start | bytes 98312 | tf_op jit(solution)/shard_map/ppermute | solution.py:139
  16.4 10.2 %collective-permute-start.2 = (bf16[32,512]{1,0:T(8,128)(2,1)}, bf16[32,512]{1,0:T(8,128)(2,1)S(1)}, u32[]{:S(2)}, u32[]{:S(2)}) collective-permute-start(bf16[32,512]{1,0:T(8,128)(2,1)} %get-tuple-element.16), channel_id=1, source_target_pairs={{0,256},{256,0},{1,257},{257,1},{2,258},{258,2},{3,259},{259,3},{4... | collective-permute-start | bytes 98312 | tf_op jit(solution)/shard_map/ppermute | solution.py:139
  18.4 8.1 %copy-start.2 = (bf16[32,512]{1,0:T(8,128)(2,1)}, bf16[32,512]{1,0:T(8,128)(2,1)S(1)}, u32[]{:S(2)}) copy-start(bf16[32,512]{1,0:T(8,128)(2,1)S(1)} %collective-permute-done.r0) | copy-start | bytes 98308
  18.5 8.1 %copy-start.4 = (bf16[32,512]{1,0:T(8,128)(2,1)}, bf16[32,512]{1,0:T(8,128)(2,1)S(1)}, u32[]{:S(2)}) copy-start(bf16[32,512]{1,0:T(8,128)(2,1)S(1)} %collective-permute-done.1.r1) | copy-start | bytes 98308
  26.5 0.6 copy-start.6
  29.8 13.6 %all-to-all-start = ((bf16[4,160,512]{2,1,0:T(8,128)(2,1)}), bf16[4,160,512]{2,1,0:T(8,128)(2,1)S(1)}, u32[]{:S(2)}, u32[]{:S(2)}) async-start(bf16[4,160,512]{2,1,0:T(8,128)(2,1)} %shard_map.130), calls=%async_computation | async-start | bytes 1310720 | tf_op jit(solution)/shard_map/all_to_all | solution.py:153
  43.3 0.8 copy-start
  69.8 30.5 %all-to-all-start.3 = ((f32[8,8,256]{2,1,0:T(8,128)}), f32[8,8,256]{2,1,0:T(8,128)S(1)}, u32[]{:S(2)}, u32[]{:S(2)}) async-start(f32[8,8,256]{2,1,0:T(8,128)} %broadcast_in_dim.7), calls=%async_computation.3 | async-start | bytes 131072 | tf_op jit(solution)/shard_map/all_to_all | solution.py:176
  80.9 9.0 %collective-permute-start.3 = (bf16[32,512]{1,0:T(8,128)(2,1)}, bf16[32,512]{1,0:T(8,128)(2,1)S(1)}, u32[]{:S(2)}, u32[]{:S(2)}) collective-permute-start(bf16[32,512]{1,0:T(8,128)(2,1)} %get-tuple-element.20), channel_id=1, source_target_pairs={{0,8},{8,0},{1,9},{9,1},{2,10},{10,2},{3,11},{11,3},{4,12},{12,4},... | collective-permute-start | bytes 98312 | tf_op jit(solution)/shard_map/ppermute | solution.py:139
  83.4 10.0 %collective-permute-start.4 = (bf16[32,512]{1,0:T(8,128)(2,1)}, bf16[32,512]{1,0:T(8,128)(2,1)S(1)}, u32[]{:S(2)}, u32[]{:S(2)}) collective-permute-start(bf16[32,512]{1,0:T(8,128)(2,1)} %get-tuple-element.21), channel_id=1, source_target_pairs={{0,32},{32,0},{1,33},{33,1},{2,34},{34,2},{3,35},{35,3},{4,36},{36... | collective-permute-start | bytes 98312 | tf_op jit(solution)/shard_map/ppermute | solution.py:139
  87.9 10.3 %collective-permute-start.5 = (bf16[32,512]{1,0:T(8,128)(2,1)}, bf16[32,512]{1,0:T(8,128)(2,1)S(1)}, u32[]{:S(2)}, u32[]{:S(2)}) collective-permute-start(bf16[32,512]{1,0:T(8,128)(2,1)} %get-tuple-element.22), channel_id=1, source_target_pairs={{0,256},{256,0},{1,257},{257,1},{2,258},{258,2},{3,259},{259,3},{4... | collective-permute-start | bytes 98312 | tf_op jit(solution)/shard_map/ppermute | solution.py:139
  89.9 8.3 %copy-start.1 = (bf16[32,512]{1,0:T(8,128)(2,1)}, bf16[32,512]{1,0:T(8,128)(2,1)S(1)}, u32[]{:S(2)}) copy-start(bf16[32,512]{1,0:T(8,128)(2,1)S(1)} %collective-permute-done.3.c0) | copy-start | bytes 98308
  93.4 4.7 %copy-start.3 = (bf16[32,512]{1,0:T(8,128)(2,1)}, bf16[32,512]{1,0:T(8,128)(2,1)S(1)}, u32[]{:S(2)}) copy-start(bf16[32,512]{1,0:T(8,128)(2,1)S(1)} %collective-permute-done.4.c1) | copy-start | bytes 98308
  98.1 0.6 copy-start.5

commit v2 on v1

--- a/solution.py
+++ b/solution.py
@@ -125,7 +125,7 @@
 
 def call(kernel, ins, outs, scratch=(), flops=0, nbytes=1 << 20):
     many = isinstance(outs, tuple)
-    return pl.pallas_call(
+    run = pl.pallas_call(
         kernel,
         out_shape=outs,
         in_specs=[SMEM if i else VMEM for i in ins],
@@ -134,6 +134,15 @@
         cost_estimate=pl.CostEstimate(flops=flops, bytes_accessed=nbytes, transcendentals=0),
     )
 
+    def apply(*args):
+        near = [
+            a if i else pltpu.with_memory_space_constraint(a, pltpu.VMEM)
+            for i, a in zip(ins, args, strict=True)
+        ]
+        return run(*near)
+
+    return apply
+
 
 def swap(x, axis):
     return lax.ppermute(x, axis, [(0, 1), (1, 0)])
@@ -141,9 +150,9 @@
 
 def shards(x, ws, wn, in_adj, in_rows, in_cols, bnd_adj, bnd_send, bnd_rows, g):
     S = jax.ShapeDtypeStruct
-    part = S((FR, LOCAL), bf16)
+    part = pltpu.VMEM((FR, LOCAL), bf16)
     picked = call(pick_kernel, (1, 0), (part,) * 3)(bnd_send, x)
-    got = [swap(picked[r], PAIRS[r]) for r in range(ROUNDS)]
+    got = [swap(picked[r], PAIRS[r]) for r in (2, 1, 0)][::-1]
     give = call(
         agg_kernel,
         (1, 1, 1) + (0,) * 9,
@@ -155,7 +164,7 @@
     y, gp, wg = call(
         node_kernel,
         (1, 0),
-        (S((HR, LOCAL), bf16), S((F_HID, LOCAL), bf16), S((8, 8, F_HID), f32)),
+        (S((HR, LOCAL), bf16), pltpu.VMEM((F_HID, LOCAL), bf16), S((8, 8, F_HID), f32)),
         (
             pltpu.VMEM((2 * F_IN, F_HID), bf16),
             pltpu.VMEM((2 * F_IN, LOCAL), bf16),
@@ -166,14 +175,20 @@
     base, *back = call(
         back_kernel,
         (1, 1, 1) + (0,) * 5,
-        (S((FR, LOCAL), f32),) + (part,) * 3,
+        (pltpu.VMEM((FR, LOCAL), f32),) + (part,) * 3,
         (pltpu.VMEM((TILES, FR, TILE), f32), pltpu.VMEM((TILES, FR, TILE), bf16)),
     )(in_rows, in_cols, bnd_rows, gp, ws, wn, in_adj, bnd_adj)
+    wg, base, *back = lax.optimization_barrier((wg, base, *back))
+    home = [None] * ROUNDS
+    home[2] = swap(back[2], PAIRS[2])
     wg = jnp.broadcast_to(jnp.sum(wg, axis=0), (16, 8, F_HID))
     wg = lax.all_to_all(wg, ZC, 0, 0, tiled=True)
-    home = [swap(back[r], PAIRS[r]) for r in range(ROUNDS)]
+    home[1] = swap(back[1], PAIRS[1])
+    wg, home[2] = lax.optimization_barrier((wg, home[2]))
     wg = jnp.broadcast_to(jnp.sum(wg, axis=0), (8, 8, F_HID))
+    wg, back[0] = lax.optimization_barrier((wg, back[0]))
     wg = lax.all_to_all(wg, Y, 0, 0, tiled=True).reshape(2 * FR, F_HID)
+    home[0] = swap(back[0], PAIRS[0])
     grad_x = call(join_kernel, (1,) + (0,) * 4, S((FR, LOCAL), f32))(bnd_send, base, *home)
     return y, grad_x, wg[FR:], wg[:FR]
 

time: 102 us -> 97 us (0.951)
  the two profiles are of different devices: /device:TPU:32 before, /device:TPU:8 now
where the time goes in v2:
time: 97 us; the launch traced here: 96.2 us
  starting transfers between devices  55.1 us (57%)
  waiting for transfers between devices  27.9 us (29%)
  Pallas kernels  6.9 us (7%)
  local copies, waits for them, and re-layouts  5.5 us (6%)
    ppermute x6, starting transfers between devices, swap(): return lax.ppermute(x, axis, [(0, 1), (1, 0)])  34.5 us
    ppermute x6, waiting for transfers between devices, swap(): return lax.ppermute(x, axis, [(0, 1), (1, 0)])  13.1 us
    all_to_all x1, waiting for transfers between devices, shards(): block = lax.all_to_all(give, 'f', 0, 0, tiled=True)  9.17 us
    all_to_all x1, starting transfers between devices, shards(): wg = lax.all_to_all(wg, Y, 0, 0, tiled=True)  7.78 us
    pallas_call x5, Pallas kernels, apply(): return run(*near)  6.9 us
    all_to_all x1, waiting for transfers between devices, shards(): wg = lax.all_to_all(wg, Y, 0, 0, tiled=True)  5.7 us
    all_to_all x1, starting transfers between devices, shards(): wg = lax.all_to_all(wg, Y, 0, 0, tiled=True).reshape(2 * FR, F_HID)  4.79 us
    all_to_all x1, starting transfers between devices, shards(): block = lax.all_to_all(give, 'f', 0, 0, tiled=True)  4.29 us
  transfers between devices with their start and end apart: 10, of which 5 were waited for; matrix products, arithmetic and copies ran while one was open for 0% of the time, Pallas kernels for 3%

profile of v2, /device:TPU:8, one launch (start us, length us, event | category | flops | bytes accessed | tf_op | source)
XLA Modules:
  0.0 96.2 jit_solution(8502103785115081693)
XLA Ops:
  0.6 0.0 copy-start.4
  0.6 0.7 copy-done.4
  1.4 0.0 copy-start.5
  1.4 0.0 copy-start.6
  1.4 0.8 shard_map.129
  2.2 4.3 %collective-permute-start = (bf16[32,512]{1,0:T(8,128)(2,1)S(1)}, bf16[32,512]{1,0:T(8,128)(2,1)S(1)}, u32[]{:S(2)}, u32[]{:S(2)}) collective-permute-start(bf16[32,512]{1,0:T(8,128)(2,1)S(1)} %get-tuple-element.23), channel_id=1, source_target_pairs={{0,8},{8,0},{1,9},{9,1},{2,10},{10,2},{3,11},{11,3},{4,12},{12,4},... | collective-permute-start | bytes 98312 | tf_op jit(solution)/shard_map/ppermute | solution.py:148
  6.5 10.0 %collective-permute-start.1 = (bf16[32,512]{1,0:T(8,128)(2,1)S(1)}, bf16[32,512]{1,0:T(8,128)(2,1)S(1)}, u32[]{:S(2)}, u32[]{:S(2)}) collective-permute-start(bf16[32,512]{1,0:T(8,128)(2,1)S(1)} %get-tuple-element.24), channel_id=1, source_target_pairs={{0,32},{32,0},{1,33},{33,1},{2,34},{34,2},{3,35},{35,3},{4,36},{36... | collective-permute-start | bytes 98312 | tf_op jit(solution)/shard_map/ppermute | solution.py:148
  16.5 6.8 %collective-permute-start.2 = (bf16[32,512]{1,0:T(8,128)(2,1)S(1)}, bf16[32,512]{1,0:T(8,128)(2,1)S(1)}, u32[]{:S(2)}, u32[]{:S(2)}) collective-permute-start(bf16[32,512]{1,0:T(8,128)(2,1)S(1)} %get-tuple-element.25), channel_id=1, source_target_pairs={{0,256},{256,0},{1,257},{257,1},{2,258},{258,2},{3,259},{259,3},{4... | collective-permute-start | bytes 98312 | tf_op jit(solution)/shard_map/ppermute | solution.py:148
  23.4 0.0 collective-permute-done.r0
  23.4 0.0 collective-permute-done.1.r1
  23.4 3.0 %collective-permute-done.2.r2 = bf16[32,512]{1,0:T(8,128)(2,1)S(1)} collective-permute-done((bf16[32,512]{1,0:T(8,128)(2,1)S(1)}, bf16[32,512]{1,0:T(8,128)(2,1)S(1)}, u32[]{:S(2)}, u32[]{:S(2)}) %collective-permute-start.2) | collective-permute-done | bytes 32800 | tf_op jit(solution)/shard_map/ppermute | solution.py:148
  26.4 0.0 copy-done.5
  26.4 0.0 copy-done.6
  26.4 0.0 copy-start
  26.4 1.0 %copy-done = bf16[12,128,128]{2,1,0:T(8,128)(2,1)S(1)} copy-done((bf16[12,128,128]{2,1,0:T(8,128)(2,1)S(1)}, bf16[12,128,128]{2,1,0:T(8,128)(2,1)}, u32[]{:S(2)}) %copy-start) | copy-done | bytes 393240
  27.4 0.0 copy-start.2
  27.4 1.0 %copy-done.2 = bf16[12,128,128]{2,1,0:T(8,128)(2,1)S(1)} copy-done((bf16[12,128,128]{2,1,0:T(8,128)(2,1)S(1)}, bf16[12,128,128]{2,1,0:T(8,128)(2,1)}, u32[]{:S(2)}) %copy-start.2) | copy-done | bytes 393240
  28.4 0.0 copy-start.7
  28.4 0.8 copy-done.7
  29.2 2.1 %shard_map.130 = bf16[4,160,512]{2,1,0:T(8,128)(2,1)} custom-call(s32[12]{0:T(128)} %rows.3, s32[12]{0:T(128)} %cols.3, s32[12]{0:T(128)} %brows.3, bf16[32,512]{1,0:T(8,128)(2,1)S(1)} %copy-done.4, bf16[32,512]{1,0:T(8,128)(2,1)S(1)} %collective-permute-done.r0, bf16[32,512]{1,0:T(8,128)(2,1)S(1)} %collective-permute-done.1.r1, ...), custom_call_target="tpu_custom_call" | custom-call | bytes 1048576 | tf_op jit(solution)/shard_map/pallas_call | solution.py:142
  31.3 4.3 %all-to-all-start = ((bf16[4,160,512]{2,1,0:T(8,128)(2,1)}), bf16[4,160,512]{2,1,0:T(8,128)(2,1)S(1)}, u32[]{:S(2)}, u32[]{:S(2)}) async-start(bf16[4,160,512]{2,1,0:T(8,128)(2,1)} %shard_map.130), calls=%async_computation | async-start | bytes 1310720 | tf_op jit(solution)/shard_map/all_to_all | solution.py:162
  35.6 9.2 %all-to-all-done.got = bf16[4,160,512]{2,1,0:T(8,128)(2,1)S(1)} async-done(((bf16[4,160,512]{2,1,0:T(8,128)(2,1)}), bf16[4,160,512]{2,1,0:T(8,128)(2,1)S(1)}, u32[]{:S(2)}, u32[]{:S(2)}) %all-to-all-start) | async-done | bytes 655392 | tf_op jit(solution)/shard_map/all_to_all | solution.py:162
  44.7 0.0 copy-start.1
  44.7 0.0 copy-start.3
  44.7 1.4 %shard_map.131 = (bf16[64,512]{1,0:T(8,128)(2,1)}, bf16[256,512]{1,0:T(8,128)(2,1)S(1)}, f32[8,8,256]{2,1,0:T(8,128)}) custom-call(s32[1]{0:T(128)} %bitcast.me, bf16[4,160,512]{2,1,0:T(8,128)(2,1)S(1)} %all-to-all-done.got), custom_call_target="tpu_custom_call" | custom-call | bytes 1048576 | tf_op jit(solution)/shard_map/pallas_call | solution.py:142
  46.2 7.8 %all-to-all-start.1 = ((f32[8,8,256]{2,1,0:T(8,128)}), f32[8,8,256]{2,1,0:T(8,128)S(1)}, u32[]{:S(2)}, u32[]{:S(2)}) async-start(f32[8,8,256]{2,1,0:T(8,128)} %get-tuple-element.27), calls=%async_computation.1 | async-start | bytes 131072 | tf_op jit(solution)/shard_map/all_to_all | solution.py:174
  54.0 0.0 copy-done.1
  54.0 0.0 copy-done.3
  54.0 1.2 %shard_map.132 = (f32[32,512]{1,0:T(8,128)S(1)}, bf16[32,512]{1,0:T(8,128)(2,1)S(1)}, bf16[32,512]{1,0:T(8,128)(2,1)S(1)}, bf16[32,512]{1,0:T(8,128)(2,1)S(1)}) custom-call(s32[12]{0:T(128)} %rows.3, s32[12]{0:T(128)} %cols.3, s32[12]{0:T(128)} %brows.3, bf16[256,512]{1,0:T(8,128)(2,1)S(1)} %get-tuple-element.28.gp, bf16[32,256]{1,0:T(8,128)(2,1)S(1)} %copy-done.5, ...), custom_call_target="tpu_custom_call" | custom-call | bytes 1048576 | tf_op jit(solution)/shard_map/pallas_call | solution.py:142
  55.2 5.7 %all-to-all-done.1 = f32[8,8,256]{2,1,0:T(8,128)S(1)} async-done(((f32[8,8,256]{2,1,0:T(8,128)}), f32[8,8,256]{2,1,0:T(8,128)S(1)}, u32[]{:S(2)}, u32[]{:S(2)}) %all-to-all-start.1) | async-done | bytes 65568 | tf_op jit(solution)/shard_map/all_to_all | solution.py:174
  60.9 0.7 broadcast_in_dim.6
  61.6 3.8 %all-to-all-start.2 = ((f32[16,8,256]{2,1,0:T(8,128)}), f32[16,8,256]{2,1,0:T(8,128)S(1)}, u32[]{:S(2)}, u32[]{:S(2)}) async-start(f32[16,8,256]{2,1,0:T(8,128)} %broadcast_in_dim.6), calls=%async_computation.2 | async-start | bytes 262144 | tf_op jit(solution)/shard_map/all_to_all | solution.py:185
  65.3 3.3 %collective-permute-start.3 = (bf16[32,512]{1,0:T(8,128)(2,1)S(1)}, bf16[32,512]{1,0:T(8,128)(2,1)S(1)}, u32[]{:S(2)}, u32[]{:S(2)}) collective-permute-start(bf16[32,512]{1,0:T(8,128)(2,1)S(1)} %get-tuple-element.35), channel_id=1, source_target_pairs={{0,256},{256,0},{1,257},{257,1},{2,258},{258,2},{3,259},{259,3},{4... | collective-permute-start | bytes 98312 | tf_op jit(solution)/shard_map/ppermute | solution.py:148
  68.6 6.8 %collective-permute-done.3.c2 = bf16[32,512]{1,0:T(8,128)(2,1)S(1)} collective-permute-done((bf16[32,512]{1,0:T(8,128)(2,1)S(1)}, bf16[32,512]{1,0:T(8,128)(2,1)S(1)}, u32[]{:S(2)}, u32[]{:S(2)}) %collective-permute-start.3) | collective-permute-done | bytes 32800 | tf_op jit(solution)/shard_map/ppermute | solution.py:148
  75.4 0.0 all-to-all-done.2
  75.4 0.6 broadcast_in_dim.7
  76.0 4.8 %all-to-all-start.3 = ((f32[8,8,256]{2,1,0:T(8,128)}), f32[8,8,256]{2,1,0:T(8,128)S(1)}, u32[]{:S(2)}, u32[]{:S(2)}) async-start(f32[8,8,256]{2,1,0:T(8,128)} %broadcast_in_dim.7), calls=%async_computation.3 | async-start | bytes 131072 | tf_op jit(solution)/shard_map/all_to_all | solution.py:190
  80.8 7.6 %collective-permute-start.5 = (bf16[32,512]{1,0:T(8,128)(2,1)S(1)}, bf16[32,512]{1,0:T(8,128)(2,1)S(1)}, u32[]{:S(2)}, u32[]{:S(2)}) collective-permute-start(bf16[32,512]{1,0:T(8,128)(2,1)S(1)} %get-tuple-element.39), channel_id=1, source_target_pairs={{0,32},{32,0},{1,33},{33,1},{2,34},{34,2},{3,35},{35,3},{4,36},{36... | collective-permute-start | bytes 98312 | tf_op jit(solution)/shard_map/ppermute | solution.py:148
  88.4 2.5 %collective-permute-start.4 = (bf16[32,512]{1,0:T(8,128)(2,1)S(1)}, bf16[32,512]{1,0:T(8,128)(2,1)S(1)}, u32[]{:S(2)}, u32[]{:S(2)}) collective-permute-start(bf16[32,512]{1,0:T(8,128)(2,1)S(1)} %get-tuple-element.38), channel_id=1, source_target_pairs={{0,8},{8,0},{1,9},{9,1},{2,10},{10,2},{3,11},{11,3},{4,12},{12,4},... | collective-permute-start | bytes 98312 | tf_op jit(solution)/shard_map/ppermute | solution.py:148
  90.9 0.0 collective-permute-done.5.c1
  90.9 3.3 %collective-permute-done.4.c0 = bf16[32,512]{1,0:T(8,128)(2,1)S(1)} collective-permute-done((bf16[32,512]{1,0:T(8,128)(2,1)S(1)}, bf16[32,512]{1,0:T(8,128)(2,1)S(1)}, u32[]{:S(2)}, u32[]{:S(2)}) %collective-permute-start.4) | collective-permute-done | bytes 32800 | tf_op jit(solution)/shard_map/ppermute | solution.py:148
  94.2 1.4 %shard_map.133 = f32[32,512]{1,0:T(8,128)} custom-call(s32[12]{0:T(128)} %send.3, f32[32,512]{1,0:T(8,128)S(1)} %get-tuple-element.33.base, bf16[32,512]{1,0:T(8,128)(2,1)S(1)} %collective-permute-done.4.c0, bf16[32,512]{1,0:T(8,128)(2,1)S(1)} %collective-permute-done.5.c1, bf16[32,512]{1,0:T(8,128)(2,1)S(1)} %collective-permute-done.3.c2), custom_call_target="tpu_custom_call" | custom-call | bytes 1048576 | tf_op jit(solution)/shard_map/pallas_call | solution.py:142
  95.6 0.0 all-to-all-done.3
  95.6 0.6 slice_bitcast_fusion
  (2 shorter events, 0.0 us)
Async XLA Ops:
  0.6 0.8 copy-start.4
  1.4 25.0 %copy-start.5 = (bf16[32,256]{1,0:T(8,128)(2,1)S(1)}, bf16[32,256]{1,0:T(8,128)(2,1)}, u32[]{:S(2)}) copy-start(bf16[32,256]{1,0:T(8,128)(2,1)} %ws.3) | copy-start | bytes 49156
  1.4 25.0 %copy-start.6 = (bf16[32,256]{1,0:T(8,128)(2,1)S(1)}, bf16[32,256]{1,0:T(8,128)(2,1)}, u32[]{:S(2)}) copy-start(bf16[32,256]{1,0:T(8,128)(2,1)} %wn.3) | copy-start | bytes 49156
  2.2 21.2 %collective-permute-start = (bf16[32,512]{1,0:T(8,128)(2,1)S(1)}, bf16[32,512]{1,0:T(8,128)(2,1)S(1)}, u32[]{:S(2)}, u32[]{:S(2)}) collective-permute-start(bf16[32,512]{1,0:T(8,128)(2,1)S(1)} %get-tuple-element.23), channel_id=1, source_target_pairs={{0,8},{8,0},{1,9},{9,1},{2,10},{10,2},{3,11},{11,3},{4,12},{12,4},... | collective-permute-start | bytes 98312 | tf_op jit(solution)/shard_map/ppermute | solution.py:148
  6.5 16.9 %collective-permute-start.1 = (bf16[32,512]{1,0:T(8,128)(2,1)S(1)}, bf16[32,512]{1,0:T(8,128)(2,1)S(1)}, u32[]{:S(2)}, u32[]{:S(2)}) collective-permute-start(bf16[32,512]{1,0:T(8,128)(2,1)S(1)} %get-tuple-element.24), channel_id=1, source_target_pairs={{0,32},{32,0},{1,33},{33,1},{2,34},{34,2},{3,35},{35,3},{4,36},{36... | collective-permute-start | bytes 98312 | tf_op jit(solution)/shard_map/ppermute | solution.py:148
  16.5 9.8 %collective-permute-start.2 = (bf16[32,512]{1,0:T(8,128)(2,1)S(1)}, bf16[32,512]{1,0:T(8,128)(2,1)S(1)}, u32[]{:S(2)}, u32[]{:S(2)}) collective-permute-start(bf16[32,512]{1,0:T(8,128)(2,1)S(1)} %get-tuple-element.25), channel_id=1, source_target_pairs={{0,256},{256,0},{1,257},{257,1},{2,258},{258,2},{3,259},{259,3},{4... | collective-permute-start | bytes 98312 | tf_op jit(solution)/shard_map/ppermute | solution.py:148
  26.4 1.0 %copy-start = (bf16[12,128,128]{2,1,0:T(8,128)(2,1)S(1)}, bf16[12,128,128]{2,1,0:T(8,128)(2,1)}, u32[]{:S(2)}) copy-start(bf16[12,128,128]{2,1,0:T(8,128)(2,1)} %adj.3) | copy-start | bytes 1179652
  27.4 1.0 %copy-start.2 = (bf16[12,128,128]{2,1,0:T(8,128)(2,1)S(1)}, bf16[12,128,128]{2,1,0:T(8,128)(2,1)}, u32[]{:S(2)}) copy-start(bf16[12,128,128]{2,1,0:T(8,128)(2,1)} %badj.3) | copy-start | bytes 1179652
  28.4 0.8 copy-start.7
  31.3 13.5 %all-to-all-start = ((bf16[4,160,512]{2,1,0:T(8,128)(2,1)}), bf16[4,160,512]{2,1,0:T(8,128)(2,1)S(1)}, u32[]{:S(2)}, u32[]{:S(2)}) async-start(bf16[4,160,512]{2,1,0:T(8,128)(2,1)} %shard_map.130), calls=%async_computation | async-start | bytes 1310720 | tf_op jit(solution)/shard_map/all_to_all | solution.py:162
  44.7 9.2 %copy-start.1 = (bf16[12,128,128]{2,1,0:T(8,128)(2,1)S(1)}, bf16[12,128,128]{2,1,0:T(8,128)(2,1)}, u32[]{:S(2)}) copy-start(bf16[12,128,128]{2,1,0:T(8,128)(2,1)} %adj.3) | copy-start | bytes 1179652
  44.7 9.2 %copy-start.3 = (bf16[12,128,128]{2,1,0:T(8,128)(2,1)S(1)}, bf16[12,128,128]{2,1,0:T(8,128)(2,1)}, u32[]{:S(2)}) copy-start(bf16[12,128,128]{2,1,0:T(8,128)(2,1)} %badj.3) | copy-start | bytes 1179652
  46.2 14.7 %all-to-all-start.1 = ((f32[8,8,256]{2,1,0:T(8,128)}), f32[8,8,256]{2,1,0:T(8,128)S(1)}, u32[]{:S(2)}, u32[]{:S(2)}) async-start(f32[8,8,256]{2,1,0:T(8,128)} %get-tuple-element.27), calls=%async_computation.1 | async-start | bytes 131072 | tf_op jit(solution)/shard_map/all_to_all | solution.py:174
  61.6 13.9 %all-to-all-start.2 = ((f32[16,8,256]{2,1,0:T(8,128)}), f32[16,8,256]{2,1,0:T(8,128)S(1)}, u32[]{:S(2)}, u32[]{:S(2)}) async-start(f32[16,8,256]{2,1,0:T(8,128)} %broadcast_in_dim.6), calls=%async_computation.2 | async-start | bytes 262144 | tf_op jit(solution)/shard_map/all_to_all | solution.py:185
  65.3 10.1 %collective-permute-start.3 = (bf16[32,512]{1,0:T(8,128)(2,1)S(1)}, bf16[32,512]{1,0:T(8,128)(2,1)S(1)}, u32[]{:S(2)}, u32[]{:S(2)}) collective-permute-start(bf16[32,512]{1,0:T(8,128)(2,1)S(1)} %get-tuple-element.35), channel_id=1, source_target_pairs={{0,256},{256,0},{1,257},{257,1},{2,258},{258,2},{3,259},{259,3},{4... | collective-permute-start | bytes 98312 | tf_op jit(solution)/shard_map/ppermute | solution.py:148
  76.0 19.5 %all-to-all-start.3 = ((f32[8,8,256]{2,1,0:T(8,128)}), f32[8,8,256]{2,1,0:T(8,128)S(1)}, u32[]{:S(2)}, u32[]{:S(2)}) async-start(f32[8,8,256]{2,1,0:T(8,128)} %broadcast_in_dim.7), calls=%async_computation.3 | async-start | bytes 131072 | tf_op jit(solution)/shard_map/all_to_all | solution.py:190
  80.8 10.1 %collective-permute-start.5 = (bf16[32,512]{1,0:T(8,128)(2,1)S(1)}, bf16[32,512]{1,0:T(8,128)(2,1)S(1)}, u32[]{:S(2)}, u32[]{:S(2)}) collective-permute-start(bf16[32,512]{1,0:T(8,128)(2,1)S(1)} %get-tuple-element.39), channel_id=1, source_target_pairs={{0,32},{32,0},{1,33},{33,1},{2,34},{34,2},{3,35},{35,3},{4,36},{36... | collective-permute-start | bytes 98312 | tf_op jit(solution)/shard_map/ppermute | solution.py:148
  88.4 5.8 %collective-permute-start.4 = (bf16[32,512]{1,0:T(8,128)(2,1)S(1)}, bf16[32,512]{1,0:T(8,128)(2,1)S(1)}, u32[]{:S(2)}, u32[]{:S(2)}) collective-permute-start(bf16[32,512]{1,0:T(8,128)(2,1)S(1)} %get-tuple-element.38), channel_id=1, source_target_pairs={{0,8},{8,0},{1,9},{9,1},{2,10},{10,2},{3,11},{11,3},{4,12},{12,4},... | collective-permute-start | bytes 98312 | tf_op jit(solution)/shard_map/ppermute | solution.py:148

commit v3 on v2

v3 whole, which is shorter than its diff:
```python
import math

import jax
import jax.numpy as jnp
from jax import lax
from jax.experimental import pallas as pl
from jax.experimental.pallas import tpu as pltpu
from jax.sharding import Mesh
from jax.sharding import PartitionSpec as P

F_IN = 128
F_HID = 256
TILE = 128
TILES = 4
ROUNDS = 3
BT = 4
KIN = 12
NODES = 65536
NF = 4
FR = F_IN // NF
HR = F_HID // NF
LOCAL = TILES * TILE
EPS = 1e-05

AXES = ("y2", "yl", "z2", "z1", "z0", "c", "f")
SIZES = (2, 4, 2, 2, 2, 2, 4)
DOM = AXES[:6]
Y = ("y2", "yl")
NY = 8
ZC = ("z2", "z1", "z0", "c")
NZC = 16
PAIRS = ("z0", "z2", "y2")
FLIP = (2, 8)

R_AGG, R_X, R_G, R_W = 0, FR, 2 * FR, 2 * FR + HR
ROWS = R_W + FR

SMEM = pl.BlockSpec(memory_space=pltpu.SMEM)
VMEM = pl.BlockSpec(memory_space=pltpu.VMEM)
f32, bf16 = jnp.float32, jnp.bfloat16


def lanes(tile):
    return pl.ds(pl.multiple_of(tile * TILE, TILE), TILE)


def tile_of(b):
    return slice(b * TILE, (b + 1) * TILE)


def pick_kernel(send, x, o2, o1, o0):
    for r, out in enumerate((o0, o1, o2)):
        for b in range(BT):
            out[:, tile_of(b)] = x[:, lanes(send[r * BT + b])]


def agg_kernel(rows, cols, brows, x, r2, r1, r0, adj, badj, g, ws, wn, out, acc):
    nt = (((1,), (1,)), ((), ()))
    acc[...] = jnp.zeros_like(acc)
    for k in range(KIN):
        acc[rows[k]] += lax.dot_general(
            x[:, lanes(cols[k])], adj[k], nt, preferred_element_type=f32
        )
    got = (r0, r1, r2)
    for s in range(ROUNDS * BT):
        acc[brows[s]] += lax.dot_general(
            got[s // BT][:, tile_of(s % BT)], badj[s], nt, preferred_element_type=f32
        )
    for i in range(NF):
        for t in range(TILES):
            out[i, R_AGG : R_AGG + FR, tile_of(t)] = acc[t].astype(bf16)
        out[i, R_X : R_X + FR, :] = x[...]
        out[i, R_G : R_G + HR, :] = g[...]
        out[i, R_W : R_W + FR, :F_HID] = ws[...]
        out[i, R_W : R_W + FR, F_HID:] = wn[...]


def split(w):
    high = w.astype(bf16).astype(f32)
    return jnp.concatenate([high, w - high], axis=0).astype(bf16)


def whole(two):
    both = two.astype(f32)
    return both[:8] + both[8:]


def node_kernel(
    me, rows, cols, brows, got, ws, wn, adj, badj, y, base, b2, slots, lhs, rhs, act_all, acc, ga
):
    for i in range(NF):
        lhs[i * FR : (i + 1) * FR, :] = got[i, R_W : R_W + FR, :F_HID]
        lhs[F_IN + i * FR : F_IN + (i + 1) * FR, :] = got[i, R_W : R_W + FR, F_HID:]
        rhs[i * FR : (i + 1) * FR, :] = got[i, R_X : R_X + FR, :]
        rhs[F_IN + i * FR : F_IN + (i + 1) * FR, :] = got[i, R_AGG : R_AGG + FR, :]
    tn = (((0,), (0,)), ((), ()))
    pre = lax.dot_general(lhs[...], rhs[...], tn, preferred_element_type=f32)
    gate = 1.0 / (1.0 + jnp.exp(-pre))
    act = pre * gate
    act_all[...] = act
    g = jnp.concatenate([got[i, R_G : R_G + HR, :] for i in range(NF)], axis=0).astype(f32)
    sq = jnp.sum(act * act, axis=0, keepdims=True)
    al = jnp.sum(g * act, axis=0, keepdims=True)
    rs = lax.rsqrt(sq / F_HID + EPS)
    coef = rs * rs * rs * (al / F_HID)
    grad_act = rs * g - act * coef
    grad = (grad_act * gate * (1.0 + pre * (1.0 - gate))).astype(bf16)
    f = me[0]
    y[...] = (act_all[pl.ds(pl.multiple_of(f * HR, HR), HR), :] * rs).astype(bf16)
    w = lax.dot_general(
        got[f, R_AGG : R_AGG + 2 * FR, :], grad, (((1,), (1,)), ((), ())), preferred_element_type=f32
    ) * (1.0 / math.sqrt(NODES))
    for j in range(NZC):
        slots[j, :16, :] = split(w[j // 2 * 8 : j // 2 * 8 + 8, tile_of(j % 2)])
    own = jnp.dot(ws[...], grad, preferred_element_type=f32)
    grad_agg = jnp.dot(wn[...], grad, preferred_element_type=f32).astype(bf16)
    for t in range(TILES):
        acc[t] = own[:, tile_of(t)]
        ga[t] = grad_agg[:, tile_of(t)]
    for s in range(ROUNDS * BT):
        r, b = divmod(s, BT)
        back = jnp.dot(ga[brows[s]], badj[s], preferred_element_type=f32).astype(bf16)
        if r == 2:
            b2[:, tile_of(b)] = back
        else:
            slots[r * 8 + b, 16:, :] = back[:16]
            slots[r * 8 + 4 + b, 16:, :] = back[16:]
    for k in range(KIN):
        acc[cols[k]] += jnp.dot(ga[rows[k]], adj[k], preferred_element_type=f32)
    for t in range(TILES):
        base[:, tile_of(t)] = acc[t]


def first_sum_kernel(slots, out):
    total = whole(slots[0, :16, :])
    for j in range(1, NZC):
        total += whole(slots[j, :16, :])
    for j in range(NY):
        out[j] = total


def second_sum_kernel(me, terms, slots, out):
    total = terms[0]
    for j in range(1, NY):
        total += terms[j]
    done = split(total)
    flip = jnp.where(me[1] < 8, FLIP[0], FLIP[1])
    for j in range(NZC):
        out[j, :16, :] = done
        out[j, 16:, :] = slots[j ^ flip, 16:, :]


def join_kernel(send, slots, base, c2, gx, gws, gwn):
    for j in range(NZC):
        out, row = (gwn, j // 2 * 8) if j < 8 else (gws, j // 2 * 8 - FR)
        out[row : row + 8, tile_of(j % 2)] = whole(slots[j, :16, :])
    gx[...] = base[...]
    for s in range(ROUNDS * BT):
        r, b = divmod(s, BT)
        if r == 2:
            gx[:, lanes(send[s])] += c2[:, tile_of(b)].astype(f32)
        else:
            gx[:16, lanes(send[s])] += slots[r * 8 + b, 16:, :].astype(f32)
            gx[16:, lanes(send[s])] += slots[r * 8 + 4 + b, 16:, :].astype(f32)


def call(kernel, ins, outs, scratch=(), flops=0, nbytes=1 << 20):
    many = isinstance(outs, tuple)
    run = pl.pallas_call(
        kernel,
        out_shape=outs,
        in_specs=[SMEM if i else VMEM for i in ins],
        out_specs=tuple(VMEM for _ in outs) if many else VMEM,
        scratch_shapes=list(scratch),
        cost_estimate=pl.CostEstimate(flops=flops, bytes_accessed=nbytes, transcendentals=0),
    )

    def apply(*args):
        near = [
            a if i else pltpu.with_memory_space_constraint(a, pltpu.VMEM)
            for i, a in zip(ins, args, strict=True)
        ]
        return run(*near)

    return apply


def swap(x, axis):
    return lax.ppermute(x, axis, [(0, 1), (1, 0)])


def shards(x, ws, wn, in_adj, in_rows, in_cols, bnd_adj, bnd_send, bnd_rows, g):
    S, V = jax.ShapeDtypeStruct, pltpu.VMEM
    part = V((FR, LOCAL), bf16)
    me = jnp.stack([lax.axis_index("f"), lax.axis_index(ZC)]).astype(jnp.int32)
    p2, p1, p0 = call(pick_kernel, (1, 0), (part,) * 3, nbytes=1 << 25)(bnd_send, x)
    got = [swap(p, axis) for p, axis in zip((p2, p1, p0), PAIRS[::-1])]
    give = call(
        agg_kernel,
        (1, 1, 1) + (0,) * 9,
        S((NF, ROWS, LOCAL), bf16),
        (V((TILES, FR, TILE), f32),),
    )(in_rows, in_cols, bnd_rows, x, *got, in_adj, bnd_adj, g, ws, wn)
    block = lax.all_to_all(give, "f", 0, 0, tiled=True)
    y, base, back, slots = call(
        node_kernel,
        (1, 1, 1, 1) + (0,) * 5,
        (S((HR, LOCAL), bf16), V((FR, LOCAL), f32), part, S((NZC, 32, TILE), bf16)),
        (
            V((2 * F_IN, F_HID), bf16),
            V((2 * F_IN, LOCAL), bf16),
            V((F_HID, LOCAL), f32),
            V((TILES, FR, TILE), f32),
            V((TILES, FR, TILE), bf16),
        ),
    )(me, in_rows, in_cols, bnd_rows, block, ws, wn, in_adj, bnd_adj)
    slots = lax.all_to_all(slots, ZC, 0, 0, tiled=True)
    home = swap(back, PAIRS[2])
    terms = call(first_sum_kernel, (0,), S((NY, 8, TILE), f32))(slots)
    terms = lax.all_to_all(terms, Y, 0, 0, tiled=True)
    slots = call(second_sum_kernel, (1, 0, 0), S((NZC, 32, TILE), bf16))(me, terms, slots)
    slots = lax.all_to_all(slots, ZC, 0, 0, tiled=True)
    gx, gws, gwn = call(
        join_kernel,
        (1, 0, 0, 0),
        (S((FR, LOCAL), f32), S((FR, F_HID), f32), S((FR, F_HID), f32)),
    )(bnd_send, slots, base, home)
    return y, gx, gws, gwn


def solution(mesh):
    fine = Mesh(mesh.devices.reshape(SIZES), AXES)
    in_specs = (
        P("f", DOM),
        P("f", None),
        P("f", None),
        P(DOM, None, None),
        P(DOM),
        P(DOM),
        P(DOM, None, None),
        P(DOM),
        P(DOM),
        P("f", DOM),
    )
    out_specs = (P("f", DOM), P("f", DOM), P("f", None), P("f", None))
    return jax.shard_map(shards, mesh=fine, in_specs=in_specs, out_specs=out_specs, check_vma=False)
```

time: 97 us -> 91 us (0.938)
  the two profiles are of different devices: /device:TPU:8 before, /device:TPU:1 now
where the time goes in v3:
time: 91 us; the launch traced here: 90.2 us
  starting transfers between devices  32.4 us (36%)
  blocking collectives  28 us (31%)
  waiting for transfers between devices  16.3 us (18%)
  Pallas kernels  8.69 us (10%)
  local copies, waits for them, and re-layouts  3.6 us (4%)
    ppermute x4, starting transfers between devices, swap(): return lax.ppermute(x, axis, [(0, 1), (1, 0)])  24.1 us
    all_to_all x1, blocking collectives, shards(): slots = lax.all_to_all(slots, ZC, 0, 0, tiled=True)  17.6 us
    all_to_all x1, blocking collectives, shards(): terms = lax.all_to_all(terms, Y, 0, 0, tiled=True)  10.3 us
    pallas_call x6, Pallas kernels, apply(): return run(*near)  8.69 us
    ppermute x4, waiting for transfers between devices, swap(): return lax.ppermute(x, axis, [(0, 1), (1, 0)])  8.04 us
    all_to_all x1, waiting for transfers between devices, shards(): block = lax.all_to_all(give, 'f', 0, 0, tiled=True)  7.37 us
    all_to_all x1, starting transfers between devices, shards(): block = lax.all_to_all(give, 'f', 0, 0, tiled=True)  4.14 us
    all_to_all x1, starting transfers between devices, shards(): slots = lax.all_to_all(slots, ZC, 0, 0, tiled=True)  4.11 us
  transfers between devices with their start and end apart: 6, of which 4 were waited for; matrix products, arithmetic and copies ran while one was open for 1% of the time, Pallas kernels for 0%

profile of v3, /device:TPU:1, one launch (start us, length us, event | category | flops | bytes accessed | tf_op | source)
XLA Modules:
  0.0 90.2 jit_solution(12564211984460661010)
XLA Ops:
  0.6 0.0 copy-start.4
  0.6 0.7 copy-done.4
  1.4 0.0 copy-start.5
  1.4 0.0 copy-start.6
  1.4 0.8 shard_map.129
  2.2 8.3 %collective-permute-start = (bf16[32,512]{1,0:T(8,128)(2,1)S(1)}, bf16[32,512]{1,0:T(8,128)(2,1)S(1)}, u32[]{:S(2)}, u32[]{:S(2)}) collective-permute-start(bf16[32,512]{1,0:T(8,128)(2,1)S(1)} %get-tuple-element.14), channel_id=1, source_target_pairs={{0,256},{256,0},{1,257},{257,1},{2,258},{258,2},{3,259},{259,3},{4... | collective-permute-start | bytes 98312 | tf_op jit(solution)/shard_map/ppermute | solution.py:189
  10.5 10.6 %collective-permute-start.1 = (bf16[32,512]{1,0:T(8,128)(2,1)S(1)}, bf16[32,512]{1,0:T(8,128)(2,1)S(1)}, u32[]{:S(2)}, u32[]{:S(2)}) collective-permute-start(bf16[32,512]{1,0:T(8,128)(2,1)S(1)} %get-tuple-element.15), channel_id=1, source_target_pairs={{0,32},{32,0},{1,33},{33,1},{2,34},{34,2},{3,35},{35,3},{4,36},{36... | collective-permute-start | bytes 98312 | tf_op jit(solution)/shard_map/ppermute | solution.py:189
  21.2 3.1 %collective-permute-start.2 = (bf16[32,512]{1,0:T(8,128)(2,1)S(1)}, bf16[32,512]{1,0:T(8,128)(2,1)S(1)}, u32[]{:S(2)}, u32[]{:S(2)}) collective-permute-start(bf16[32,512]{1,0:T(8,128)(2,1)S(1)} %get-tuple-element.16), channel_id=1, source_target_pairs={{0,8},{8,0},{1,9},{9,1},{2,10},{10,2},{3,11},{11,3},{4,12},{12,4},... | collective-permute-start | bytes 98312 | tf_op jit(solution)/shard_map/ppermute | solution.py:189
  24.3 0.0 collective-permute-done.r2
  24.3 0.0 collective-permute-done.1.r1
  24.3 1.5 %collective-permute-done.2.r0 = bf16[32,512]{1,0:T(8,128)(2,1)S(1)} collective-permute-done((bf16[32,512]{1,0:T(8,128)(2,1)S(1)}, bf16[32,512]{1,0:T(8,128)(2,1)S(1)}, u32[]{:S(2)}, u32[]{:S(2)}) %collective-permute-start.2) | collective-permute-done | bytes 32800 | tf_op jit(solution)/shard_map/ppermute | solution.py:189
  25.8 0.0 copy-done.5
  25.8 0.0 copy-done.6
  25.8 0.0 copy-start
  25.8 1.0 %copy-done = bf16[12,128,128]{2,1,0:T(8,128)(2,1)S(1)} copy-done((bf16[12,128,128]{2,1,0:T(8,128)(2,1)S(1)}, bf16[12,128,128]{2,1,0:T(8,128)(2,1)}, u32[]{:S(2)}) %copy-start) | copy-done | bytes 393240
  26.8 0.0 copy-start.2
  26.8 1.0 %copy-done.2 = bf16[12,128,128]{2,1,0:T(8,128)(2,1)S(1)} copy-done((bf16[12,128,128]{2,1,0:T(8,128)(2,1)S(1)}, bf16[12,128,128]{2,1,0:T(8,128)(2,1)}, u32[]{:S(2)}) %copy-start.2) | copy-done | bytes 393240
  27.8 0.0 copy-start.7
  27.8 0.8 copy-done.7
  28.7 2.1 %shard_map.130 = bf16[4,160,512]{2,1,0:T(8,128)(2,1)} custom-call(s32[12]{0:T(128)} %rows.3, s32[12]{0:T(128)} %cols.3, s32[12]{0:T(128)} %brows.3, bf16[32,512]{1,0:T(8,128)(2,1)S(1)} %copy-done.4, bf16[32,512]{1,0:T(8,128)(2,1)S(1)} %collective-permute-done.r2, bf16[32,512]{1,0:T(8,128)(2,1)S(1)} %collective-permute-done.1.r1, ...), custom_call_target="tpu_custom_call" | custom-call | bytes 1048576 | tf_op jit(solution)/shard_map/pallas_call | solution.py:183
  30.7 0.0 copy-start.1
  30.7 0.0 copy-start.3
  30.7 4.1 %all-to-all-start = ((bf16[4,160,512]{2,1,0:T(8,128)(2,1)}), bf16[4,160,512]{2,1,0:T(8,128)(2,1)S(1)}, u32[]{:S(2)}, u32[]{:S(2)}) async-start(bf16[4,160,512]{2,1,0:T(8,128)(2,1)} %shard_map.130), calls=%async_computation | async-start | bytes 1310720 | tf_op jit(solution)/shard_map/all_to_all | solution.py:204
  34.9 0.6 pad_add_fusion.me
  35.5 7.4 %all-to-all-done.got = bf16[4,160,512]{2,1,0:T(8,128)(2,1)S(1)} async-done(((bf16[4,160,512]{2,1,0:T(8,128)(2,1)}), bf16[4,160,512]{2,1,0:T(8,128)(2,1)S(1)}, u32[]{:S(2)}, u32[]{:S(2)}) %all-to-all-start) | async-done | bytes 655392 | tf_op jit(solution)/shard_map/all_to_all | solution.py:204
  42.8 0.0 copy-done.1
  42.8 0.0 copy-done.3
  42.8 2.5 %shard_map.131 = (bf16[64,512]{1,0:T(8,128)(2,1)}, f32[32,512]{1,0:T(8,128)S(1)}, bf16[32,512]{1,0:T(8,128)(2,1)S(1)}, bf16[16,32,128]{2,1,0:T(8,128)(2,1)}) custom-call(s32[2]{0:T(128)} %pad_add_fusion.me, s32[12]{0:T(128)} %rows.3, s32[12]{0:T(128)} %cols.3, s32[12]{0:T(128)} %brows.3, bf16[4,160,512]{2,1,0:T(8,128)(2,1)S(1)} %all-to-all-done.got, ...), custom_call_target="tpu_custom_call" | custom-call | bytes 1048576 | tf_op jit(solution)/shard_map/pallas_call | solution.py:183
  45.3 17.6 %all_to_all.20.slots = bf16[16,32,128]{2,1,0:T(8,128)(2,1)S(1)} all-to-all(bf16[16,32,128]{2,1,0:T(8,128)(2,1)} %get-tuple-element.18), channel_id=1, replica_groups=mesh['y2'=2,'yl'=4,'z2'=2,'z1'=2,'z0'=2,'c'=2,'f'=4] {'z2','z1','z0','c'}, dimensions={0} | all-to-all | bytes 262144 | tf_op jit(solution)/shard_map/all_to_all | solution.py:217
  62.9 0.6 shard_map.132
  63.6 10.3 %all_to_all.21.terms = f32[8,8,128]{2,1,0:T(8,128)S(1)} all-to-all(f32[8,8,128]{2,1,0:T(8,128)} %shard_map.132), channel_id=1, replica_groups=mesh['y2'=2,'yl'=4,'z2'=2,'z1'=2,'z0'=2,'c'=2,'f'=4] {'y2','yl'}, dimensions={0} | all-to-all | bytes 65536 | tf_op jit(solution)/shard_map/all_to_all | solution.py:220
  73.9 1.4 %shard_map.133 = bf16[16,32,128]{2,1,0:T(8,128)(2,1)} custom-call(s32[2]{0:T(128)} %pad_add_fusion.me, f32[8,8,128]{2,1,0:T(8,128)S(1)} %all_to_all.21.terms, bf16[16,32,128]{2,1,0:T(8,128)(2,1)S(1)} %all_to_all.20.slots), custom_call_target="tpu_custom_call" | custom-call | bytes 1048576 | tf_op jit(solution)/shard_map/pallas_call | solution.py:183
  75.2 4.1 %all-to-all-start.3 = ((bf16[16,32,128]{2,1,0:T(8,128)(2,1)}), bf16[16,32,128]{2,1,0:T(8,128)(2,1)S(1)}, u32[]{:S(2)}, u32[]{:S(2)}) async-start(bf16[16,32,128]{2,1,0:T(8,128)(2,1)} %shard_map.133), calls=%async_computation.3 | async-start | bytes 262144 | tf_op jit(solution)/shard_map/all_to_all | solution.py:222
  79.4 2.1 %collective-permute-start.3 = (bf16[32,512]{1,0:T(8,128)(2,1)S(1)}, bf16[32,512]{1,0:T(8,128)(2,1)S(1)}, u32[]{:S(2)}, u32[]{:S(2)}) collective-permute-start(bf16[32,512]{1,0:T(8,128)(2,1)S(1)} %get-tuple-element.20), channel_id=1, source_target_pairs={{0,256},{256,0},{1,257},{257,1},{2,258},{258,2},{3,259},{259,3},{4... | collective-permute-start | bytes 98312 | tf_op jit(solution)/shard_map/ppermute | solution.py:189
  81.5 6.5 %collective-permute-done.3.c2 = bf16[32,512]{1,0:T(8,128)(2,1)S(1)} collective-permute-done((bf16[32,512]{1,0:T(8,128)(2,1)S(1)}, bf16[32,512]{1,0:T(8,128)(2,1)S(1)}, u32[]{:S(2)}, u32[]{:S(2)}) %collective-permute-start.3) | collective-permute-done | bytes 32800 | tf_op jit(solution)/shard_map/ppermute | solution.py:189
  88.0 0.9 %all-to-all-done.3.slots = bf16[16,32,128]{2,1,0:T(8,128)(2,1)S(1)} async-done(((bf16[16,32,128]{2,1,0:T(8,128)(2,1)}), bf16[16,32,128]{2,1,0:T(8,128)(2,1)S(1)}, u32[]{:S(2)}, u32[]{:S(2)}) %all-to-all-start.3) | async-done | bytes 131104 | tf_op jit(solution)/shard_map/all_to_all | solution.py:222
  88.9 1.4 %shard_map.134 = (f32[32,512]{1,0:T(8,128)}, f32[32,256]{1,0:T(8,128)}, f32[32,256]{1,0:T(8,128)}) custom-call(s32[12]{0:T(128)} %send.3, bf16[16,32,128]{2,1,0:T(8,128)(2,1)S(1)} %all-to-all-done.3.slots, f32[32,512]{1,0:T(8,128)S(1)} %get-tuple-element.19.base, bf16[32,512]{1,0:T(8,128)(2,1)S(1)} %collective-permute-done.3.c2), custom_call_target="tpu_custom_call" | custom-call | bytes 1048576 | tf_op jit(solution)/shard_map/pallas_call | solution.py:183
Async XLA Ops:
  0.6 0.8 copy-start.4
  1.4 24.4 %copy-start.5 = (bf16[32,256]{1,0:T(8,128)(2,1)S(1)}, bf16[32,256]{1,0:T(8,128)(2,1)}, u32[]{:S(2)}) copy-start(bf16[32,256]{1,0:T(8,128)(2,1)} %ws.3) | copy-start | bytes 49156
  1.4 24.4 %copy-start.6 = (bf16[32,256]{1,0:T(8,128)(2,1)S(1)}, bf16[32,256]{1,0:T(8,128)(2,1)}, u32[]{:S(2)}) copy-start(bf16[32,256]{1,0:T(8,128)(2,1)} %wn.3) | copy-start | bytes 49156
  2.2 22.0 %collective-permute-start = (bf16[32,512]{1,0:T(8,128)(2,1)S(1)}, bf16[32,512]{1,0:T(8,128)(2,1)S(1)}, u32[]{:S(2)}, u32[]{:S(2)}) collective-permute-start(bf16[32,512]{1,0:T(8,128)(2,1)S(1)} %get-tuple-element.14), channel_id=1, source_target_pairs={{0,256},{256,0},{1,257},{257,1},{2,258},{258,2},{3,259},{259,3},{4... | collective-permute-start | bytes 98312 | tf_op jit(solution)/shard_map/ppermute | solution.py:189
  10.5 13.8 %collective-permute-start.1 = (bf16[32,512]{1,0:T(8,128)(2,1)S(1)}, bf16[32,512]{1,0:T(8,128)(2,1)S(1)}, u32[]{:S(2)}, u32[]{:S(2)}) collective-permute-start(bf16[32,512]{1,0:T(8,128)(2,1)S(1)} %get-tuple-element.15), channel_id=1, source_target_pairs={{0,32},{32,0},{1,33},{33,1},{2,34},{34,2},{3,35},{35,3},{4,36},{36... | collective-permute-start | bytes 98312 | tf_op jit(solution)/shard_map/ppermute | solution.py:189
  21.2 4.7 %collective-permute-start.2 = (bf16[32,512]{1,0:T(8,128)(2,1)S(1)}, bf16[32,512]{1,0:T(8,128)(2,1)S(1)}, u32[]{:S(2)}, u32[]{:S(2)}) collective-permute-start(bf16[32,512]{1,0:T(8,128)(2,1)S(1)} %get-tuple-element.16), channel_id=1, source_target_pairs={{0,8},{8,0},{1,9},{9,1},{2,10},{10,2},{3,11},{11,3},{4,12},{12,4},... | collective-permute-start | bytes 98312 | tf_op jit(solution)/shard_map/ppermute | solution.py:189
  25.8 1.0 %copy-start = (bf16[12,128,128]{2,1,0:T(8,128)(2,1)S(1)}, bf16[12,128,128]{2,1,0:T(8,128)(2,1)}, u32[]{:S(2)}) copy-start(bf16[12,128,128]{2,1,0:T(8,128)(2,1)} %adj.3) | copy-start | bytes 1179652
  26.8 1.0 %copy-start.2 = (bf16[12,128,128]{2,1,0:T(8,128)(2,1)S(1)}, bf16[12,128,128]{2,1,0:T(8,128)(2,1)}, u32[]{:S(2)}) copy-start(bf16[12,128,128]{2,1,0:T(8,128)(2,1)} %badj.3) | copy-start | bytes 1179652
  27.8 0.8 copy-start.7
  30.7 12.1 %copy-start.1 = (bf16[12,128,128]{2,1,0:T(8,128)(2,1)S(1)}, bf16[12,128,128]{2,1,0:T(8,128)(2,1)}, u32[]{:S(2)}) copy-start(bf16[12,128,128]{2,1,0:T(8,128)(2,1)} %adj.3) | copy-start | bytes 1179652
  30.7 12.1 %copy-start.3 = (bf16[12,128,128]{2,1,0:T(8,128)(2,1)S(1)}, bf16[12,128,128]{2,1,0:T(8,128)(2,1)}, u32[]{:S(2)}) copy-start(bf16[12,128,128]{2,1,0:T(8,128)(2,1)} %badj.3) | copy-start | bytes 1179652
  30.7 12.1 %all-to-all-start = ((bf16[4,160,512]{2,1,0:T(8,128)(2,1)}), bf16[4,160,512]{2,1,0:T(8,128)(2,1)S(1)}, u32[]{:S(2)}, u32[]{:S(2)}) async-start(bf16[4,160,512]{2,1,0:T(8,128)(2,1)} %shard_map.130), calls=%async_computation | async-start | bytes 1310720 | tf_op jit(solution)/shard_map/all_to_all | solution.py:204
  75.2 13.6 %all-to-all-start.3 = ((bf16[16,32,128]{2,1,0:T(8,128)(2,1)}), bf16[16,32,128]{2,1,0:T(8,128)(2,1)S(1)}, u32[]{:S(2)}, u32[]{:S(2)}) async-start(bf16[16,32,128]{2,1,0:T(8,128)(2,1)} %shard_map.133), calls=%async_computation.3 | async-start | bytes 262144 | tf_op jit(solution)/shard_map/all_to_all | solution.py:222
  79.4 8.6 %collective-permute-start.3 = (bf16[32,512]{1,0:T(8,128)(2,1)S(1)}, bf16[32,512]{1,0:T(8,128)(2,1)S(1)}, u32[]{:S(2)}, u32[]{:S(2)}) collective-permute-start(bf16[32,512]{1,0:T(8,128)(2,1)S(1)} %get-tuple-element.20), channel_id=1, source_target_pairs={{0,256},{256,0},{1,257},{257,1},{2,258},{258,2},{3,259},{259,3},{4... | collective-permute-start | bytes 98312 | tf_op jit(solution)/shard_map/ppermute | solution.py:189

commit v4 on v3

--- a/solution.py
+++ b/solution.py
@@ -48,10 +48,20 @@
     return slice(b * TILE, (b + 1) * TILE)
 
 
-def pick_kernel(send, x, o2, o1, o0):
+def stage_kernel(send, x, *refs):
+    n = (len(refs) - 5) // 2
+    far, near, (o2, o1, o0), sem = (x, *refs[:n]), refs[n : 2 * n + 1], refs[2 * n + 1 : -1], refs[-1]
+    copies = [
+        pltpu.make_async_copy(a, b, sem.at[i]) for i, (a, b) in enumerate(zip(far, near, strict=True))
+    ]
+    for copy in copies:
+        copy.start()
+    copies[0].wait()
     for r, out in enumerate((o0, o1, o2)):
         for b in range(BT):
-            out[:, tile_of(b)] = x[:, lanes(send[r * BT + b])]
+            out[:, tile_of(b)] = near[0][:, lanes(send[r * BT + b])]
+    for copy in copies[1:]:
+        copy.wait()
 
 
 def agg_kernel(rows, cols, brows, x, r2, r1, r0, adj, badj, g, ws, wn, out, acc):
@@ -166,10 +176,11 @@
 
 def call(kernel, ins, outs, scratch=(), flops=0, nbytes=1 << 20):
     many = isinstance(outs, tuple)
+    kinds = (VMEM, SMEM, pl.BlockSpec(memory_space=pl.ANY))
     run = pl.pallas_call(
         kernel,
         out_shape=outs,
-        in_specs=[SMEM if i else VMEM for i in ins],
+        in_specs=[kinds[i] for i in ins],
         out_specs=tuple(VMEM for _ in outs) if many else VMEM,
         scratch_shapes=list(scratch),
         cost_estimate=pl.CostEstimate(flops=flops, bytes_accessed=nbytes, transcendentals=0),
@@ -193,19 +204,25 @@
     S, V = jax.ShapeDtypeStruct, pltpu.VMEM
     part = V((FR, LOCAL), bf16)
     me = jnp.stack([lax.axis_index("f"), lax.axis_index(ZC)]).astype(jnp.int32)
-    p2, p1, p0 = call(pick_kernel, (1, 0), (part,) * 3, nbytes=1 << 25)(bnd_send, x)
+    far = (x, in_adj, bnd_adj, g, ws, wn)
+    x, in_adj, bnd_adj, g, ws, wn, p2, p1, p0 = call(
+        stage_kernel,
+        (1,) + (2,) * len(far),
+        tuple(V(a.shape, a.dtype) for a in far) + (part,) * 3,
+        (pltpu.SemaphoreType.DMA((len(far),)),),
+    )(bnd_send, *far)
     got = [swap(p, axis) for p, axis in zip((p2, p1, p0), PAIRS[::-1])]
     give = call(
         agg_kernel,
         (1, 1, 1) + (0,) * 9,
-        S((NF, ROWS, LOCAL), bf16),
+        V((NF, ROWS, LOCAL), bf16),
         (V((TILES, FR, TILE), f32),),
     )(in_rows, in_cols, bnd_rows, x, *got, in_adj, bnd_adj, g, ws, wn)
     block = lax.all_to_all(give, "f", 0, 0, tiled=True)
     y, base, back, slots = call(
         node_kernel,
         (1, 1, 1, 1) + (0,) * 5,
-        (S((HR, LOCAL), bf16), V((FR, LOCAL), f32), part, S((NZC, 32, TILE), bf16)),
+        (S((HR, LOCAL), bf16), V((FR, LOCAL), f32), part, V((NZC, 32, TILE), bf16)),
         (
             V((2 * F_IN, F_HID), bf16),
             V((2 * F_IN, LOCAL), bf16),
@@ -216,9 +233,10 @@
     )(me, in_rows, in_cols, bnd_rows, block, ws, wn, in_adj, bnd_adj)
     slots = lax.all_to_all(slots, ZC, 0, 0, tiled=True)
     home = swap(back, PAIRS[2])
-    terms = call(first_sum_kernel, (0,), S((NY, 8, TILE), f32))(slots)
+    slots, home = lax.optimization_barrier((slots, home))
+    terms = call(first_sum_kernel, (0,), V((NY, 8, TILE), f32))(slots)
     terms = lax.all_to_all(terms, Y, 0, 0, tiled=True)
-    slots = call(second_sum_kernel, (1, 0, 0), S((NZC, 32, TILE), bf16))(me, terms, slots)
+    slots = call(second_sum_kernel, (1, 0, 0), V((NZC, 32, TILE), bf16))(me, terms, slots)
     slots = lax.all_to_all(slots, ZC, 0, 0, tiled=True)
     gx, gws, gwn = call(
         join_kernel,

time: 91 us -> 90.2 us (level)
  starting transfers between devices: 32.4 us -> 36.4 us
  local copies, waits for them, and re-layouts: 3.6 us -> 0 us
    all_to_all x1, starting transfers between devices: 4.11 us -> 8.47 us  [shards(): slots = lax.all_to_all(slots, ZC, 0, 0, tiled=True)]
    unnamed x16 -> x0, local copies, waits for them, and re-layouts: 3.6 us -> none
    all_to_all x1, blocking collectives: 10.3 us -> 9.24 us  [shards(): terms = lax.all_to_all(terms, Y, 0, 0, tiled=True)]
where the time goes in v4:
time: 90.2 us; the launch traced here: 89.7 us
  starting transfers between devices  36.4 us (40%)
  blocking collectives  27.2 us (30%)
  waiting for transfers between devices  16.4 us (18%)
  Pallas kernels  8.43 us (9%)
    ppermute x4, starting transfers between devices, swap(): return lax.ppermute(x, axis, [(0, 1), (1, 0)])  24 us
    all_to_all x1, blocking collectives, shards(): slots = lax.all_to_all(slots, ZC, 0, 0, tiled=True)  17.9 us
    all_to_all x1, blocking collectives, shards(): terms = lax.all_to_all(terms, Y, 0, 0, tiled=True)  9.24 us
    all_to_all x1, starting transfers between devices, shards(): slots = lax.all_to_all(slots, ZC, 0, 0, tiled=True)  8.47 us
    pallas_call x6, Pallas kernels, apply(): return run(*near)  8.43 us
    ppermute x4, waiting for transfers between devices, swap(): return lax.ppermute(x, axis, [(0, 1), (1, 0)])  8.35 us
    all_to_all x1, waiting for transfers between devices, shards(): block = lax.all_to_all(give, 'f', 0, 0, tiled=True)  7.37 us
    all_to_all x1, starting transfers between devices, shards(): block = lax.all_to_all(give, 'f', 0, 0, tiled=True)  4.01 us
  transfers between devices with their start and end apart: 6, of which 4 were waited for; matrix products, arithmetic and copies ran while one was open for 1% of the time, Pallas kernels for 0%

profile of v4, /device:TPU:1, one launch (start us, length us, event | category | flops | bytes accessed | tf_op | source)
XLA Modules:
  0.0 89.7 jit_solution(9144592856633868883)
XLA Ops:
  0.6 1.9 %shard_map.129 = (bf16[32,512]{1,0:T(8,128)(2,1)S(1)}, bf16[12,128,128]{2,1,0:T(8,128)(2,1)S(1)}, bf16[12,128,128]{2,1,0:T(8,128)(2,1)S(1)}, bf16[64,512]{1,0:T(...) custom-call(s32[12]{0:T(128)} %send.3, ...), custom_call_target="tpu_custom_call" | custom-call | bytes 1048576 | tf_op jit(solution)/shard_map/pallas_call | solution.py:194
  2.5 8.3 %collective-permute-start = (bf16[32,512]{1,0:T(8,128)(2,1)S(1)}, bf16[32,512]{1,0:T(8,128)(2,1)S(1)}, u32[]{:S(2)}, u32[]{:S(2)}) collective-permute-start(bf16[32,512]{1,0:T(8,128)(2,1)S(1)} %get-tuple-element.23), channel_id=1, source_target_pairs={{0,256},{256,0},{1,257},{257,1},{2,258},{258,2},{3,259},{259,3},{4... | collective-permute-start | bytes 98312 | tf_op jit(solution)/shard_map/ppermute | solution.py:200
  10.8 10.6 %collective-permute-start.1 = (bf16[32,512]{1,0:T(8,128)(2,1)S(1)}, bf16[32,512]{1,0:T(8,128)(2,1)S(1)}, u32[]{:S(2)}, u32[]{:S(2)}) collective-permute-start(bf16[32,512]{1,0:T(8,128)(2,1)S(1)} %get-tuple-element.24), channel_id=1, source_target_pairs={{0,32},{32,0},{1,33},{33,1},{2,34},{34,2},{3,35},{35,3},{4,36},{36... | collective-permute-start | bytes 98312 | tf_op jit(solution)/shard_map/ppermute | solution.py:200
  21.4 3.1 %collective-permute-start.2 = (bf16[32,512]{1,0:T(8,128)(2,1)S(1)}, bf16[32,512]{1,0:T(8,128)(2,1)S(1)}, u32[]{:S(2)}, u32[]{:S(2)}) collective-permute-start(bf16[32,512]{1,0:T(8,128)(2,1)S(1)} %get-tuple-element.25), channel_id=1, source_target_pairs={{0,8},{8,0},{1,9},{9,1},{2,10},{10,2},{3,11},{11,3},{4,12},{12,4},... | collective-permute-start | bytes 98312 | tf_op jit(solution)/shard_map/ppermute | solution.py:200
  24.5 0.0 collective-permute-done.r2
  24.6 0.0 collective-permute-done.1.r1
  24.6 1.5 %collective-permute-done.2.r0 = bf16[32,512]{1,0:T(8,128)(2,1)S(1)} collective-permute-done((bf16[32,512]{1,0:T(8,128)(2,1)S(1)}, bf16[32,512]{1,0:T(8,128)(2,1)S(1)}, u32[]{:S(2)}, u32[]{:S(2)}) %collective-permute-start.2) | collective-permute-done | bytes 32800 | tf_op jit(solution)/shard_map/ppermute | solution.py:200
  26.1 2.1 %shard_map.130 = bf16[4,160,512]{2,1,0:T(8,128)(2,1)} custom-call(s32[12]{0:T(128)} %rows.3, s32[12]{0:T(128)} %cols.3, s32[12]{0:T(128)} %brows.3, bf16[32,512]{1,0:T(8,128)(2,1)S(1)} %get-tuple-element.22.x, bf16[32,512]{1,0:T(8,128)(2,1)S(1)} %collective-permute-done.r2, bf16[32,512]{1,0:T(8,128)(2,1)S(1)} %collective-permute-done.1.r1, ...), custom_call_target="tpu_custom_call" | custom-call | bytes 1048576 | tf_op jit(solution)/shard_map/pallas_call | solution.py:194
  28.2 4.0 %all-to-all-start = ((bf16[4,160,512]{2,1,0:T(8,128)(2,1)}), bf16[4,160,512]{2,1,0:T(8,128)(2,1)S(1)}, u32[]{:S(2)}, u32[]{:S(2)}) async-start(bf16[4,160,512]{2,1,0:T(8,128)(2,1)} %shard_map.130), calls=%async_computation | async-start | bytes 1310720 | tf_op jit(solution)/shard_map/all_to_all | solution.py:221
  32.2 0.6 pad_add_fusion.me
  32.8 7.4 %all-to-all-done.got = bf16[4,160,512]{2,1,0:T(8,128)(2,1)S(1)} async-done(((bf16[4,160,512]{2,1,0:T(8,128)(2,1)}), bf16[4,160,512]{2,1,0:T(8,128)(2,1)S(1)}, u32[]{:S(2)}, u32[]{:S(2)}) %all-to-all-start) | async-done | bytes 655392 | tf_op jit(solution)/shard_map/all_to_all | solution.py:221
  40.1 2.4 %shard_map.131 = (bf16[64,512]{1,0:T(8,128)(2,1)}, f32[32,512]{1,0:T(8,128)S(1)}, bf16[32,512]{1,0:T(8,128)(2,1)S(1)}, bf16[16,32,128]{2,1,0:T(8,128)(2,1)}) custom-call(s32[2]{0:T(128)} %pad_add_fusion.me, s32[12]{0:T(128)} %rows.3, s32[12]{0:T(128)} %cols.3, s32[12]{0:T(128)} %brows.3, bf16[4,160,512]{2,1,0:T(8,128)(2,1)S(1)} %all-to-all-done.got, ...), custom_call_target="tpu_custom_call" | custom-call | bytes 1048576 | tf_op jit(solution)/shard_map/pallas_call | solution.py:194
  42.6 8.5 %all-to-all-start.1 = ((bf16[16,32,128]{2,1,0:T(8,128)(2,1)}), bf16[16,32,128]{2,1,0:T(8,128)(2,1)S(1)}, u32[]{:S(2)}, u32[]{:S(2)}) async-start(bf16[16,32,128]{2,1,0:T(8,128)(2,1)} %get-tuple-element.32), calls=%async_computation.1 | async-start | bytes 262144 | tf_op jit(solution)/shard_map/all_to_all | solution.py:234
  51.0 1.9 %collective-permute-start.3 = (bf16[32,512]{1,0:T(8,128)(2,1)S(1)}, bf16[32,512]{1,0:T(8,128)(2,1)S(1)}, u32[]{:S(2)}, u32[]{:S(2)}) collective-permute-start(bf16[32,512]{1,0:T(8,128)(2,1)S(1)} %get-tuple-element.33), channel_id=1, source_target_pairs={{0,256},{256,0},{1,257},{257,1},{2,258},{258,2},{3,259},{259,3},{4... | collective-permute-start | bytes 98312 | tf_op jit(solution)/shard_map/ppermute | solution.py:200
  53.0 6.8 %collective-permute-done.3.c2 = bf16[32,512]{1,0:T(8,128)(2,1)S(1)} collective-permute-done((bf16[32,512]{1,0:T(8,128)(2,1)S(1)}, bf16[32,512]{1,0:T(8,128)(2,1)S(1)}, u32[]{:S(2)}, u32[]{:S(2)}) %collective-permute-start.3) | collective-permute-done | bytes 32800 | tf_op jit(solution)/shard_map/ppermute | solution.py:200
  59.8 0.7 all-to-all-done.1.slots
  60.5 9.2 %all_to_all.20.terms = f32[8,8,128]{2,1,0:T(8,128)S(1)} all-to-all(f32[8,8,128]{2,1,0:T(8,128)S(1)} %shard_map.132), channel_id=1, replica_groups=mesh['y2'=2,'yl'=4,'z2'=2,'z1'=2,'z0'=2,'c'=2,'f'=4] {'y2','yl'}, dimensions={0} | all-to-all | bytes 65536 | tf_op jit(solution)/shard_map/all_to_all | solution.py:238
  69.8 0.7 shard_map.133
  70.5 17.9 %all_to_all.21.slots = bf16[16,32,128]{2,1,0:T(8,128)(2,1)S(1)} all-to-all(bf16[16,32,128]{2,1,0:T(8,128)(2,1)S(1)} %shard_map.133), channel_id=1, replica_groups=mesh['y2'=2,'yl'=4,'z2'=2,'z1'=2,'z0'=2,'c'=2,'f'=4] {'z2','z1','z0','c'}, dimensions={0} | all-to-all | bytes 262144 | tf_op jit(solution)/shard_map/all_to_all | solution.py:240
  88.4 1.4 %shard_map.134 = (f32[32,512]{1,0:T(8,128)}, f32[32,256]{1,0:T(8,128)}, f32[32,256]{1,0:T(8,128)}) custom-call(s32[12]{0:T(128)} %send.3, bf16[16,32,128]{2,1,0:T(8,128)(2,1)S(1)} %all_to_all.21.slots, f32[32,512]{1,0:T(8,128)S(1)} %get-tuple-element.35.base, bf16[32,512]{1,0:T(8,128)(2,1)S(1)} %collective-permute-done.3.c2), custom_call_target="tpu_custom_call" | custom-call | bytes 1048576 | tf_op jit(solution)/shard_map/pallas_call | solution.py:194
  (1 shorter events, 0.0 us)
Async XLA Ops:
  2.5 22.0 %collective-permute-start = (bf16[32,512]{1,0:T(8,128)(2,1)S(1)}, bf16[32,512]{1,0:T(8,128)(2,1)S(1)}, u32[]{:S(2)}, u32[]{:S(2)}) collective-permute-start(bf16[32,512]{1,0:T(8,128)(2,1)S(1)} %get-tuple-element.23), channel_id=1, source_target_pairs={{0,256},{256,0},{1,257},{257,1},{2,258},{258,2},{3,259},{259,3},{4... | collective-permute-start | bytes 98312 | tf_op jit(solution)/shard_map/ppermute | solution.py:200
  10.8 13.8 %collective-permute-start.1 = (bf16[32,512]{1,0:T(8,128)(2,1)S(1)}, bf16[32,512]{1,0:T(8,128)(2,1)S(1)}, u32[]{:S(2)}, u32[]{:S(2)}) collective-permute-start(bf16[32,512]{1,0:T(8,128)(2,1)S(1)} %get-tuple-element.24), channel_id=1, source_target_pairs={{0,32},{32,0},{1,33},{33,1},{2,34},{34,2},{3,35},{35,3},{4,36},{36... | collective-permute-start | bytes 98312 | tf_op jit(solution)/shard_map/ppermute | solution.py:200
  21.4 4.7 %collective-permute-start.2 = (bf16[32,512]{1,0:T(8,128)(2,1)S(1)}, bf16[32,512]{1,0:T(8,128)(2,1)S(1)}, u32[]{:S(2)}, u32[]{:S(2)}) collective-permute-start(bf16[32,512]{1,0:T(8,128)(2,1)S(1)} %get-tuple-element.25), channel_id=1, source_target_pairs={{0,8},{8,0},{1,9},{9,1},{2,10},{10,2},{3,11},{11,3},{4,12},{12,4},... | collective-permute-start | bytes 98312 | tf_op jit(solution)/shard_map/ppermute | solution.py:200
  28.2 12.0 %all-to-all-start = ((bf16[4,160,512]{2,1,0:T(8,128)(2,1)}), bf16[4,160,512]{2,1,0:T(8,128)(2,1)S(1)}, u32[]{:S(2)}, u32[]{:S(2)}) async-start(bf16[4,160,512]{2,1,0:T(8,128)(2,1)} %shard_map.130), calls=%async_computation | async-start | bytes 1310720 | tf_op jit(solution)/shard_map/all_to_all | solution.py:221
  42.6 17.9 %all-to-all-start.1 = ((bf16[16,32,128]{2,1,0:T(8,128)(2,1)}), bf16[16,32,128]{2,1,0:T(8,128)(2,1)S(1)}, u32[]{:S(2)}, u32[]{:S(2)}) async-start(bf16[16,32,128]{2,1,0:T(8,128)(2,1)} %get-tuple-element.32), calls=%async_computation.1 | async-start | bytes 262144 | tf_op jit(solution)/shard_map/all_to_all | solution.py:234
  51.0 8.8 %collective-permute-start.3 = (bf16[32,512]{1,0:T(8,128)(2,1)S(1)}, bf16[32,512]{1,0:T(8,128)(2,1)S(1)}, u32[]{:S(2)}, u32[]{:S(2)}) collective-permute-start(bf16[32,512]{1,0:T(8,128)(2,1)S(1)} %get-tuple-element.33), channel_id=1, source_target_pairs={{0,256},{256,0},{1,257},{257,1},{2,258},{258,2},{3,259},{259,3},{4... | collective-permute-start | bytes 98312 | tf_op jit(solution)/shard_map/ppermute | solution.py:200

commit v5 on v3

--- a/solution.py
+++ b/solution.py
@@ -48,31 +48,55 @@
     return slice(b * TILE, (b + 1) * TILE)
 
 
-def pick_kernel(send, x, o2, o1, o0):
+def pick_kernel(send, far, x, o2, o1, o0, sem):
+    copy = pltpu.make_async_copy(far, x, sem)
+    copy.start()
+    copy.wait()
     for r, out in enumerate((o0, o1, o2)):
         for b in range(BT):
             out[:, tile_of(b)] = x[:, lanes(send[r * BT + b])]
 
 
-def agg_kernel(rows, cols, brows, x, r2, r1, r0, adj, badj, g, ws, wn, out, acc):
-    nt = (((1,), (1,)), ((), ()))
+NT = (((1,), (1,)), ((), ()))
+
+
+def inner_kernel(rows, cols, x, *refs):
+    far, near, (give, acc, g, sem) = refs[:5], refs[5:9], refs[9:]
+    adj, badj, ws, wn = near
+    copies = [
+        pltpu.make_async_copy(a, b, sem.at[i])
+        for i, (a, b) in enumerate(zip(far, (*near, g), strict=True))
+    ]
+    for copy in copies:
+        copy.start()
     acc[...] = jnp.zeros_like(acc)
+    for i in range(NF):
+        give[i, R_X : R_X + FR, :] = x[...]
+    copies[0].wait()
     for k in range(KIN):
         acc[rows[k]] += lax.dot_general(
-            x[:, lanes(cols[k])], adj[k], nt, preferred_element_type=f32
+            x[:, lanes(cols[k])], adj[k], NT, preferred_element_type=f32
         )
+    for copy in copies[1:]:
+        copy.wait()
+    for i in range(NF):
+        give[i, R_G : R_G + HR, :] = g[...]
+        give[i, R_W : R_W + FR, :F_HID] = ws[...]
+        give[i, R_W : R_W + FR, F_HID:] = wn[...]
+
+
+def outer_kernel(brows, r2, r1, r0, badj, inner, half, give, acc):
+    del half
+    acc[...] = inner[...]
     got = (r0, r1, r2)
     for s in range(ROUNDS * BT):
         acc[brows[s]] += lax.dot_general(
-            got[s // BT][:, tile_of(s % BT)], badj[s], nt, preferred_element_type=f32
+            got[s // BT][:, tile_of(s % BT)], badj[s], NT, preferred_element_type=f32
         )
-    for i in range(NF):
-        for t in range(TILES):
-            out[i, R_AGG : R_AGG + FR, tile_of(t)] = acc[t].astype(bf16)
-        out[i, R_X : R_X + FR, :] = x[...]
-        out[i, R_G : R_G + HR, :] = g[...]
-        out[i, R_W : R_W + FR, :F_HID] = ws[...]
-        out[i, R_W : R_W + FR, F_HID:] = wn[...]
+    for t in range(TILES):
+        part = acc[t].astype(bf16)
+        for i in range(NF):
+            give[i, R_AGG : R_AGG + FR, tile_of(t)] = part
 
 
 def split(w):
@@ -86,7 +110,7 @@
 
 
 def node_kernel(
-    me, rows, cols, brows, got, ws, wn, adj, badj, y, base, b2, slots, lhs, rhs, act_all, acc, ga
+    rows, cols, brows, got, ws, wn, adj, badj, y, base, b2, slots, lhs, rhs, act_all, acc, ga
 ):
     for i in range(NF):
         lhs[i * FR : (i + 1) * FR, :] = got[i, R_W : R_W + FR, :F_HID]
@@ -105,7 +129,7 @@
     coef = rs * rs * rs * (al / F_HID)
     grad_act = rs * g - act * coef
     grad = (grad_act * gate * (1.0 + pre * (1.0 - gate))).astype(bf16)
-    f = me[0]
+    f = lax.axis_index("f")
     y[...] = (act_all[pl.ds(pl.multiple_of(f * HR, HR), HR), :] * rs).astype(bf16)
     w = lax.dot_general(
         got[f, R_AGG : R_AGG + 2 * FR, :], grad, (((1,), (1,)), ((), ())), preferred_element_type=f32
@@ -139,12 +163,12 @@
         out[j] = total
 
 
-def second_sum_kernel(me, terms, slots, out):
+def second_sum_kernel(terms, slots, out):
     total = terms[0]
     for j in range(1, NY):
         total += terms[j]
     done = split(total)
-    flip = jnp.where(me[1] < 8, FLIP[0], FLIP[1])
+    flip = jnp.where(lax.axis_index("z2") == 0, FLIP[0], FLIP[1])
     for j in range(NZC):
         out[j, :16, :] = done
         out[j, 16:, :] = slots[j ^ flip, 16:, :]
@@ -164,14 +188,16 @@
             gx[16:, lanes(send[s])] += slots[r * 8 + 4 + b, 16:, :].astype(f32)
 
 
-def call(kernel, ins, outs, scratch=(), flops=0, nbytes=1 << 20):
+def call(kernel, ins, outs, scratch=(), flops=0, nbytes=1 << 20, aliases=()):
     many = isinstance(outs, tuple)
+    kinds = (VMEM, SMEM, pl.BlockSpec(memory_space=pl.ANY))
     run = pl.pallas_call(
         kernel,
         out_shape=outs,
-        in_specs=[SMEM if i else VMEM for i in ins],
+        in_specs=[kinds[i] for i in ins],
         out_specs=tuple(VMEM for _ in outs) if many else VMEM,
         scratch_shapes=list(scratch),
+        input_output_aliases=dict(aliases),
         cost_estimate=pl.CostEstimate(flops=flops, bytes_accessed=nbytes, transcendentals=0),
     )
 
@@ -192,20 +218,29 @@
 def shards(x, ws, wn, in_adj, in_rows, in_cols, bnd_adj, bnd_send, bnd_rows, g):
     S, V = jax.ShapeDtypeStruct, pltpu.VMEM
     part = V((FR, LOCAL), bf16)
-    me = jnp.stack([lax.axis_index("f"), lax.axis_index(ZC)]).astype(jnp.int32)
-    p2, p1, p0 = call(pick_kernel, (1, 0), (part,) * 3, nbytes=1 << 25)(bnd_send, x)
+    sems = pltpu.SemaphoreType.DMA
+    here, p2, p1, p0 = call(pick_kernel, (1, 2), (part,) * 4, (sems(()),))(bnd_send, x)
     got = [swap(p, axis) for p, axis in zip((p2, p1, p0), PAIRS[::-1])]
+    far = (in_adj, bnd_adj, ws, wn)
+    in_adj, bnd_adj, ws, wn, give, acc = call(
+        inner_kernel,
+        (1, 1, 0) + (2,) * 5,
+        tuple(V(a.shape, a.dtype) for a in far)
+        + (V((NF, ROWS, LOCAL), bf16), V((TILES, FR, TILE), f32)),
+        (V((HR, LOCAL), bf16), sems((5,))),
+    )(in_rows, in_cols, here, *far, g)
     give = call(
-        agg_kernel,
-        (1, 1, 1) + (0,) * 9,
-        S((NF, ROWS, LOCAL), bf16),
+        outer_kernel,
+        (1,) + (0,) * 6,
+        V((NF, ROWS, LOCAL), bf16),
         (V((TILES, FR, TILE), f32),),
-    )(in_rows, in_cols, bnd_rows, x, *got, in_adj, bnd_adj, g, ws, wn)
+        aliases=((6, 0),),
+    )(bnd_rows, *got, bnd_adj, acc, give)
     block = lax.all_to_all(give, "f", 0, 0, tiled=True)
     y, base, back, slots = call(
         node_kernel,
-        (1, 1, 1, 1) + (0,) * 5,
-        (S((HR, LOCAL), bf16), V((FR, LOCAL), f32), part, S((NZC, 32, TILE), bf16)),
+        (1, 1, 1) + (0,) * 5,
+        (V((HR, LOCAL), bf16), V((FR, LOCAL), f32), part, V((NZC, 32, TILE), bf16)),
         (
             V((2 * F_IN, F_HID), bf16),
             V((2 * F_IN, LOCAL), bf16),
@@ -213,12 +248,13 @@
             V((TILES, FR, TILE), f32),
             V((TILES, FR, TILE), bf16),
         ),
-    )(me, in_rows, in_cols, bnd_rows, block, ws, wn, in_adj, bnd_adj)
+    )(in_rows, in_cols, bnd_rows, block, ws, wn, in_adj, bnd_adj)
     slots = lax.all_to_all(slots, ZC, 0, 0, tiled=True)
     home = swap(back, PAIRS[2])
-    terms = call(first_sum_kernel, (0,), S((NY, 8, TILE), f32))(slots)
+    slots, home = lax.optimization_barrier((slots, home))
+    terms = call(first_sum_kernel, (0,), V((NY, 8, TILE), f32))(slots)
     terms = lax.all_to_all(terms, Y, 0, 0, tiled=True)
-    slots = call(second_sum_kernel, (1, 0, 0), S((NZC, 32, TILE), bf16))(me, terms, slots)
+    slots = call(second_sum_kernel, (0, 0), V((NZC, 32, TILE), bf16))(terms, slots)
     slots = lax.all_to_all(slots, ZC, 0, 0, tiled=True)
     gx, gws, gwn = call(
         join_kernel,

time: 91 us -> 88.8 us (0.976)
  starting transfers between devices: 32.4 us -> 40.3 us
  blocking collectives: 28 us -> 21.6 us
  local copies, waits for them, and re-layouts: 3.6 us -> 0.63 us
    all_to_all x1 -> x2, starting transfers between devices: 4.11 us -> 16.3 us  [shards(): slots = lax.all_to_all(slots, ZC, 0, 0, tiled=True)]
    all_to_all x1 -> x2, waiting for transfers between devices: 0.91 us -> 9.24 us  [shards(): slots = lax.all_to_all(slots, ZC, 0, 0, tiled=True)]
    all_to_all x1 -> x0, waiting for transfers between devices: 7.37 us -> none  [shards(): block = lax.all_to_all(give, 'f', 0, 0, tiled=True)]
    all_to_all x1, blocking collectives: 17.6 us -> 12.3 us  [shards(): block = lax.all_to_all(give, 'f', 0, 0, tiled=True)]
    all_to_all x1 -> x0, starting transfers between devices: 4.14 us -> none  [shards(): block = lax.all_to_all(give, 'f', 0, 0, tiled=True)]
    unnamed x16 -> x1, local copies, waits for them, and re-layouts: 3.6 us -> 0.63 us
    ppermute x4, waiting for transfers between devices: 8.04 us -> 6.81 us  [swap(): return lax.ppermute(x, axis, [(0, 1), (1, 0)])]
    all_to_all x1, blocking collectives: 10.3 us -> 9.24 us  [shards(): terms = lax.all_to_all(terms, Y, 0, 0, tiled=True)]
  transfers between devices with their start and end apart: 6 -> 6, of which waited for: 4 -> 3; matrix products, arithmetic and copies ran while one was open for 1% -> 1% of each run, Pallas kernels for 0% -> 2%
where the time goes in v5:
time: 88.8 us; the launch traced here: 88.2 us
  starting transfers between devices  40.3 us (45%)
  blocking collectives  21.6 us (24%)
  waiting for transfers between devices  16.1 us (18%)
  Pallas kernels  9 us (10%)
    ppermute x4, starting transfers between devices, swap(): return lax.ppermute(x, axis, [(0, 1), (1, 0)])  24 us
    all_to_all x2, starting transfers between devices, shards(): slots = lax.all_to_all(slots, ZC, 0, 0, tiled=True)  16.3 us
    all_to_all x1, blocking collectives, shards(): block = lax.all_to_all(give, 'f', 0, 0, tiled=True)  12.3 us
    all_to_all x2, waiting for transfers between devices, shards(): slots = lax.all_to_all(slots, ZC, 0, 0, tiled=True)  9.24 us
    all_to_all x1, blocking collectives, shards(): terms = lax.all_to_all(terms, Y, 0, 0, tiled=True)  9.24 us
    pallas_call x7, Pallas kernels, apply(): return run(*near)  9 us
    ppermute x4, waiting for transfers between devices, swap(): return lax.ppermute(x, axis, [(0, 1), (1, 0)])  6.81 us
  transfers between devices with their start and end apart: 6, of which 3 were waited for; matrix products, arithmetic and copies ran while one was open for 1% of the time, Pallas kernels for 2%

profile of v5, /device:TPU:1, one launch (start us, length us, event | category | flops | bytes accessed | tf_op | source)
XLA Modules:
  0.0 88.2 jit_solution(14561179420811969928)
XLA Ops:
  0.6 1.5 %shard_map.129 = (bf16[32,512]{1,0:T(8,128)(2,1)S(1)}, bf16[32,512]{1,0:T(8,128)(2,1)S(1)}, bf16[32,512]{1,0:T(8,128)(2,1)S(1)}, bf16[32,512]{1,0:T(8,128)(2,1)S(1)}) custom-call(s32[12]{0:T(128)} %send.3, bf16[32,512]{1,0:T(8,128)(2,1)} %far.1), custom_call_target="tpu_custom_call" | custom-call | bytes 1048576 | tf_op jit(solution)/shard_map/pallas_call | solution.py:209
  2.1 8.3 %collective-permute-start = (bf16[32,512]{1,0:T(8,128)(2,1)S(1)}, bf16[32,512]{1,0:T(8,128)(2,1)S(1)}, u32[]{:S(2)}, u32[]{:S(2)}) collective-permute-start(bf16[32,512]{1,0:T(8,128)(2,1)S(1)} %get-tuple-element.23), channel_id=1, source_target_pairs={{0,256},{256,0},{1,257},{257,1},{2,258},{258,2},{3,259},{259,3},{4... | collective-permute-start | bytes 98312 | tf_op jit(solution)/shard_map/ppermute | solution.py:215
  10.4 10.6 %collective-permute-start.1 = (bf16[32,512]{1,0:T(8,128)(2,1)S(1)}, bf16[32,512]{1,0:T(8,128)(2,1)S(1)}, u32[]{:S(2)}, u32[]{:S(2)}) collective-permute-start(bf16[32,512]{1,0:T(8,128)(2,1)S(1)} %get-tuple-element.24), channel_id=1, source_target_pairs={{0,32},{32,0},{1,33},{33,1},{2,34},{34,2},{3,35},{35,3},{4,36},{36... | collective-permute-start | bytes 98312 | tf_op jit(solution)/shard_map/ppermute | solution.py:215
  21.0 3.1 %collective-permute-start.2 = (bf16[32,512]{1,0:T(8,128)(2,1)S(1)}, bf16[32,512]{1,0:T(8,128)(2,1)S(1)}, u32[]{:S(2)}, u32[]{:S(2)}) collective-permute-start(bf16[32,512]{1,0:T(8,128)(2,1)S(1)} %get-tuple-element.25), channel_id=1, source_target_pairs={{0,8},{8,0},{1,9},{9,1},{2,10},{10,2},{3,11},{11,3},{4,12},{12,4},... | collective-permute-start | bytes 98312 | tf_op jit(solution)/shard_map/ppermute | solution.py:215
  24.1 2.1 %shard_map.130 = (bf16[12,128,128]{2,1,0:T(8,128)(2,1)S(1)}, bf16[12,128,128]{2,1,0:T(8,128)(2,1)S(1)}, bf16[32,256]{1,0:T(8,128)(2,1)S(1)}, bf16[32,256]{1,0:T(...) custom-call(s32[12]{0:T(128)} %rows.3, s32[12]{0:T(128)} %cols.3, ...), custom_call_target="tpu_custom_call" | custom-call | bytes 1048576 | tf_op jit(solution)/shard_map/pallas_call | solution.py:209
  26.2 0.0 collective-permute-done.r2
  26.2 0.0 collective-permute-done.1.r1
  26.2 0.0 collective-permute-done.2.r0
  26.2 1.0 %shard_map.131 = bf16[4,160,512]{2,1,0:T(8,128)(2,1)S(1)} custom-call(s32[12]{0:T(128)} %brows.3, bf16[32,512]{1,0:T(8,128)(2,1)S(1)} %collective-permute-done.r2, bf16[32,512]{1,0:T(8,128)(2,1)S(1)} %collective-permute-done.1.r1, bf16[32,512]{1,0:T(8,128)(2,1)S(1)} %collective-permute-done.2.r0, ...), custom_call_target="tpu_custom_call", output_to_operand_aliasing={{}: (6, {})} | custom-call | bytes 1048576 | tf_op jit(solution)/shard_map/pallas_call | solution.py:209
  27.3 12.3 %all_to_all.20.got = bf16[4,160,512]{2,1,0:T(8,128)(2,1)S(1)} all-to-all(bf16[4,160,512]{2,1,0:T(8,128)(2,1)S(1)} %shard_map.131), channel_id=1, replica_groups=mesh['y2'=2,'yl'=4,'z2'=2,'z1'=2,'z0'=2,'c'=2,'f'=4] {'f'}, dimensions={0} | all-to-all | bytes 1310720 | tf_op jit(solution)/shard_map/all_to_all | solution.py:239
  39.6 2.4 %shard_map.132 = (bf16[64,512]{1,0:T(8,128)(2,1)S(1)}, f32[32,512]{1,0:T(8,128)S(1)}, bf16[32,512]{1,0:T(8,128)(2,1)S(1)}, bf16[16,32,128]{2,1,0:T(8,128)(2,1)}) custom-call(s32[12]{0:T(128)} %rows.3, s32[12]{0:T(128)} %cols.3, s32[12]{0:T(128)} %brows.3, bf16[4,160,512]{2,1,0:T(8,128)(2,1)S(1)} %all_to_all.20.got, ...), custom_call_target="tpu_custom_call" | custom-call | bytes 1048576 | tf_op jit(solution)/shard_map/pallas_call | solution.py:209
  42.0 7.3 %all-to-all-start.1 = ((bf16[16,32,128]{2,1,0:T(8,128)(2,1)}), bf16[16,32,128]{2,1,0:T(8,128)(2,1)S(1)}, u32[]{:S(2)}, u32[]{:S(2)}) async-start(bf16[16,32,128]{2,1,0:T(8,128)(2,1)} %get-tuple-element.34), calls=%async_computation.1 | async-start | bytes 262144 | tf_op jit(solution)/shard_map/all_to_all | solution.py:252
  49.3 1.9 %collective-permute-start.3 = (bf16[32,512]{1,0:T(8,128)(2,1)S(1)}, bf16[32,512]{1,0:T(8,128)(2,1)S(1)}, u32[]{:S(2)}, u32[]{:S(2)}) collective-permute-start(bf16[32,512]{1,0:T(8,128)(2,1)S(1)} %get-tuple-element.35), channel_id=1, source_target_pairs={{0,256},{256,0},{1,257},{257,1},{2,258},{258,2},{3,259},{259,3},{4... | collective-permute-start | bytes 98312 | tf_op jit(solution)/shard_map/ppermute | solution.py:215
  51.3 6.8 %collective-permute-done.3.c2 = bf16[32,512]{1,0:T(8,128)(2,1)S(1)} collective-permute-done((bf16[32,512]{1,0:T(8,128)(2,1)S(1)}, bf16[32,512]{1,0:T(8,128)(2,1)S(1)}, u32[]{:S(2)}, u32[]{:S(2)}) %collective-permute-start.3) | collective-permute-done | bytes 32800 | tf_op jit(solution)/shard_map/ppermute | solution.py:215
  58.1 0.7 all-to-all-done.1.slots
  58.8 9.2 %all_to_all.21.terms = f32[8,8,128]{2,1,0:T(8,128)S(1)} all-to-all(f32[8,8,128]{2,1,0:T(8,128)S(1)} %shard_map.133), channel_id=1, replica_groups=mesh['y2'=2,'yl'=4,'z2'=2,'z1'=2,'z0'=2,'c'=2,'f'=4] {'y2','yl'}, dimensions={0} | all-to-all | bytes 65536 | tf_op jit(solution)/shard_map/all_to_all | solution.py:256
  68.1 0.7 shard_map.134
  68.7 9.0 %all-to-all-start.3 = ((bf16[16,32,128]{2,1,0:T(8,128)(2,1)}), bf16[16,32,128]{2,1,0:T(8,128)(2,1)S(1)}, u32[]{:S(2)}, u32[]{:S(2)}) async-start(bf16[16,32,128]{2,1,0:T(8,128)(2,1)} %shard_map.134), calls=%async_computation.3 | async-start | bytes 262144 | tf_op jit(solution)/shard_map/all_to_all | solution.py:258
  77.7 0.6 copy.16
  78.3 8.5 %all-to-all-done.3.slots = bf16[16,32,128]{2,1,0:T(8,128)(2,1)S(1)} async-done(((bf16[16,32,128]{2,1,0:T(8,128)(2,1)}), bf16[16,32,128]{2,1,0:T(8,128)(2,1)S(1)}, u32[]{:S(2)}, u32[]{:S(2)}) %all-to-all-start.3) | async-done | bytes 131104 | tf_op jit(solution)/shard_map/all_to_all | solution.py:258
  86.9 1.4 %shard_map.135 = (f32[32,512]{1,0:T(8,128)}, f32[32,256]{1,0:T(8,128)}, f32[32,256]{1,0:T(8,128)}) custom-call(s32[12]{0:T(128)} %send.3, bf16[16,32,128]{2,1,0:T(8,128)(2,1)S(1)} %all-to-all-done.3.slots, f32[32,512]{1,0:T(8,128)S(1)} %get-tuple-element.37.base, bf16[32,512]{1,0:T(8,128)(2,1)S(1)} %collective-permute-done.3.c2), custom_call_target="tpu_custom_call" | custom-call | bytes 1048576 | tf_op jit(solution)/shard_map/pallas_call | solution.py:209
  (1 shorter events, 0.0 us)
Async XLA Ops:
  2.1 24.1 %collective-permute-start = (bf16[32,512]{1,0:T(8,128)(2,1)S(1)}, bf16[32,512]{1,0:T(8,128)(2,1)S(1)}, u32[]{:S(2)}, u32[]{:S(2)}) collective-permute-start(bf16[32,512]{1,0:T(8,128)(2,1)S(1)} %get-tuple-element.23), channel_id=1, source_target_pairs={{0,256},{256,0},{1,257},{257,1},{2,258},{258,2},{3,259},{259,3},{4... | collective-permute-start | bytes 98312 | tf_op jit(solution)/shard_map/ppermute | solution.py:215
  10.4 15.8 %collective-permute-start.1 = (bf16[32,512]{1,0:T(8,128)(2,1)S(1)}, bf16[32,512]{1,0:T(8,128)(2,1)S(1)}, u32[]{:S(2)}, u32[]{:S(2)}) collective-permute-start(bf16[32,512]{1,0:T(8,128)(2,1)S(1)} %get-tuple-element.24), channel_id=1, source_target_pairs={{0,32},{32,0},{1,33},{33,1},{2,34},{34,2},{3,35},{35,3},{4,36},{36... | collective-permute-start | bytes 98312 | tf_op jit(solution)/shard_map/ppermute | solution.py:215
  21.0 5.2 %collective-permute-start.2 = (bf16[32,512]{1,0:T(8,128)(2,1)S(1)}, bf16[32,512]{1,0:T(8,128)(2,1)S(1)}, u32[]{:S(2)}, u32[]{:S(2)}) collective-permute-start(bf16[32,512]{1,0:T(8,128)(2,1)S(1)} %get-tuple-element.25), channel_id=1, source_target_pairs={{0,8},{8,0},{1,9},{9,1},{2,10},{10,2},{3,11},{11,3},{4,12},{12,4},... | collective-permute-start | bytes 98312 | tf_op jit(solution)/shard_map/ppermute | solution.py:215
  42.0 16.8 %all-to-all-start.1 = ((bf16[16,32,128]{2,1,0:T(8,128)(2,1)}), bf16[16,32,128]{2,1,0:T(8,128)(2,1)S(1)}, u32[]{:S(2)}, u32[]{:S(2)}) async-start(bf16[16,32,128]{2,1,0:T(8,128)(2,1)} %get-tuple-element.34), calls=%async_computation.1 | async-start | bytes 262144 | tf_op jit(solution)/shard_map/all_to_all | solution.py:252
  49.3 8.8 %collective-permute-start.3 = (bf16[32,512]{1,0:T(8,128)(2,1)S(1)}, bf16[32,512]{1,0:T(8,128)(2,1)S(1)}, u32[]{:S(2)}, u32[]{:S(2)}) collective-permute-start(bf16[32,512]{1,0:T(8,128)(2,1)S(1)} %get-tuple-element.35), channel_id=1, source_target_pairs={{0,256},{256,0},{1,257},{257,1},{2,258},{258,2},{3,259},{259,3},{4... | collective-permute-start | bytes 98312 | tf_op jit(solution)/shard_map/ppermute | solution.py:215
  68.7 18.1 %all-to-all-start.3 = ((bf16[16,32,128]{2,1,0:T(8,128)(2,1)}), bf16[16,32,128]{2,1,0:T(8,128)(2,1)S(1)}, u32[]{:S(2)}, u32[]{:S(2)}) async-start(bf16[16,32,128]{2,1,0:T(8,128)(2,1)} %shard_map.134), calls=%async_computation.3 | async-start | bytes 262144 | tf_op jit(solution)/shard_map/all_to_all | solution.py:258

commit v6 on v5

--- a/solution.py
+++ b/solution.py
@@ -48,10 +48,8 @@
     return slice(b * TILE, (b + 1) * TILE)
 
 
-def pick_kernel(send, far, x, o2, o1, o0, sem):
-    copy = pltpu.make_async_copy(far, x, sem)
-    copy.start()
-    copy.wait()
+def pick_kernel(send, x, here, o2, o1, o0):
+    here[...] = x[...]
     for r, out in enumerate((o0, o1, o2)):
         for b in range(BT):
             out[:, tile_of(b)] = x[:, lanes(send[r * BT + b])]
@@ -109,9 +107,7 @@
     return both[:8] + both[8:]
 
 
-def node_kernel(
-    rows, cols, brows, got, ws, wn, adj, badj, y, base, b2, slots, lhs, rhs, act_all, acc, ga
-):
+def node_kernel(brows, got, ws, wn, badj, y, acc, ga, b2, slots, lhs, rhs, act_all):
     for i in range(NF):
         lhs[i * FR : (i + 1) * FR, :] = got[i, R_W : R_W + FR, :F_HID]
         lhs[F_IN + i * FR : F_IN + (i + 1) * FR, :] = got[i, R_W : R_W + FR, F_HID:]
@@ -136,11 +132,12 @@
     ) * (1.0 / math.sqrt(NODES))
     for j in range(NZC):
         slots[j, :16, :] = split(w[j // 2 * 8 : j // 2 * 8 + 8, tile_of(j % 2)])
-    own = jnp.dot(ws[...], grad, preferred_element_type=f32)
-    grad_agg = jnp.dot(wn[...], grad, preferred_element_type=f32).astype(bf16)
+    both = jnp.dot(
+        jnp.concatenate([ws[...], wn[...]], axis=0), grad, preferred_element_type=f32
+    )
     for t in range(TILES):
-        acc[t] = own[:, tile_of(t)]
-        ga[t] = grad_agg[:, tile_of(t)]
+        acc[t] = both[:FR, tile_of(t)]
+        ga[t] = both[FR:, tile_of(t)].astype(bf16)
     for s in range(ROUNDS * BT):
         r, b = divmod(s, BT)
         back = jnp.dot(ga[brows[s]], badj[s], preferred_element_type=f32).astype(bf16)
@@ -149,6 +146,11 @@
         else:
             slots[r * 8 + b, 16:, :] = back[:16]
             slots[r * 8 + 4 + b, 16:, :] = back[16:]
+
+
+def back_kernel(rows, cols, own, ga, adj, y, base, out, acc):
+    out[...] = y[...]
+    acc[...] = own[...]
     for k in range(KIN):
         acc[cols[k]] += jnp.dot(ga[rows[k]], adj[k], preferred_element_type=f32)
     for t in range(TILES):
@@ -190,7 +192,7 @@
 
 def call(kernel, ins, outs, scratch=(), flops=0, nbytes=1 << 20, aliases=()):
     many = isinstance(outs, tuple)
-    kinds = (VMEM, SMEM, pl.BlockSpec(memory_space=pl.ANY))
+    kinds = (VMEM, SMEM, pl.BlockSpec(memory_space=pl.ANY), VMEM)
     run = pl.pallas_call(
         kernel,
         out_shape=outs,
@@ -219,7 +221,7 @@
     S, V = jax.ShapeDtypeStruct, pltpu.VMEM
     part = V((FR, LOCAL), bf16)
     sems = pltpu.SemaphoreType.DMA
-    here, p2, p1, p0 = call(pick_kernel, (1, 2), (part,) * 4, (sems(()),))(bnd_send, x)
+    here, p2, p1, p0 = call(pick_kernel, (1, 3), (part,) * 4)(bnd_send, x)
     got = [swap(p, axis) for p, axis in zip((p2, p1, p0), PAIRS[::-1])]
     far = (in_adj, bnd_adj, ws, wn)
     in_adj, bnd_adj, ws, wn, give, acc = call(
@@ -237,21 +239,27 @@
         aliases=((6, 0),),
     )(bnd_rows, *got, bnd_adj, acc, give)
     block = lax.all_to_all(give, "f", 0, 0, tiled=True)
-    y, base, back, slots = call(
+    y, own, ga, back, slots = call(
         node_kernel,
-        (1, 1, 1) + (0,) * 5,
-        (V((HR, LOCAL), bf16), V((FR, LOCAL), f32), part, V((NZC, 32, TILE), bf16)),
+        (1,) + (0,) * 4,
         (
-            V((2 * F_IN, F_HID), bf16),
-            V((2 * F_IN, LOCAL), bf16),
-            V((F_HID, LOCAL), f32),
+            V((HR, LOCAL), bf16),
             V((TILES, FR, TILE), f32),
             V((TILES, FR, TILE), bf16),
+            part,
+            S((NZC, 32, TILE), bf16),
         ),
-    )(in_rows, in_cols, bnd_rows, block, ws, wn, in_adj, bnd_adj)
+        (V((2 * F_IN, F_HID), bf16), V((2 * F_IN, LOCAL), bf16), V((F_HID, LOCAL), f32)),
+    )(bnd_rows, block, ws, wn, bnd_adj)
     slots = lax.all_to_all(slots, ZC, 0, 0, tiled=True)
     home = swap(back, PAIRS[2])
-    slots, home = lax.optimization_barrier((slots, home))
+    base, y = call(
+        back_kernel,
+        (1, 1) + (0,) * 4,
+        (V((FR, LOCAL), f32), S((HR, LOCAL), bf16)),
+        (V((TILES, FR, TILE), f32),),
+    )(in_rows, in_cols, own, ga, in_adj, y)
+    slots, home, base = lax.optimization_barrier((slots, home, base))
     terms = call(first_sum_kernel, (0,), V((NY, 8, TILE), f32))(slots)
     terms = lax.all_to_all(terms, Y, 0, 0, tiled=True)
     slots = call(second_sum_kernel, (0, 0), V((NZC, 32, TILE), bf16))(terms, slots)

time: 88.8 us -> 87.2 us (0.982)
  blocking collectives: 21.6 us -> 39.5 us
  waiting for transfers between devices: 16.1 us -> 6.08 us
  starting transfers between devices: 40.3 us -> 31.3 us
    all_to_all x0 -> x1, blocking collectives: none -> 17.9 us  [shards(): slots = lax.all_to_all(slots, ZC, 0, 0, tiled=True)]
    all_to_all x2 -> x1, starting transfers between devices: 16.3 us -> 7.32 us  [shards(): slots = lax.all_to_all(slots, ZC, 0, 0, tiled=True)]
    all_to_all x2 -> x1, waiting for transfers between devices: 9.24 us -> 0.71 us  [shards(): slots = lax.all_to_all(slots, ZC, 0, 0, tiled=True)]
    ppermute x4, waiting for transfers between devices: 6.81 us -> 5.37 us  [swap(): return lax.ppermute(x, axis, [(0, 1), (1, 0)])]
    pallas_call x7 -> x8, Pallas kernels: 9 us -> 9.04 us  [apply(): return run(*near)]
  transfers between devices with their start and end apart: 6 -> 5, of which waited for: 3 -> 2; matrix products, arithmetic and copies ran while one was open for 1% -> 0% of each run, Pallas kernels for 2% -> 4%
where the time goes in v6:
time: 87.2 us; the launch traced here: 86.6 us
  blocking collectives  39.5 us (45%)
  starting transfers between devices  31.3 us (36%)
  Pallas kernels  9.04 us (10%)
  waiting for transfers between devices  6.08 us (7%)
    ppermute x4, starting transfers between devices, swap(): return lax.ppermute(x, axis, [(0, 1), (1, 0)])  24 us
    all_to_all x1, blocking collectives, shards(): slots = lax.all_to_all(slots, ZC, 0, 0, tiled=True)  17.9 us
    all_to_all x1, blocking collectives, shards(): block = lax.all_to_all(give, 'f', 0, 0, tiled=True)  12.3 us
    all_to_all x1, blocking collectives, shards(): terms = lax.all_to_all(terms, Y, 0, 0, tiled=True)  9.24 us
    pallas_call x8, Pallas kernels, apply(): return run(*near)  9.04 us
    all_to_all x1, starting transfers between devices, shards(): slots = lax.all_to_all(slots, ZC, 0, 0, tiled=True)  7.32 us
    ppermute x4, waiting for transfers between devices, swap(): return lax.ppermute(x, axis, [(0, 1), (1, 0)])  5.37 us
  transfers between devices with their start and end apart: 5, of which 2 were waited for; matrix products, arithmetic and copies ran while one was open for 0% of the time, Pallas kernels for 4%

profile of v6, /device:TPU:1, one launch (start us, length us, event | category | flops | bytes accessed | tf_op | source)
XLA Modules:
  0.0 86.6 jit_solution(334933126418725494)
XLA Ops:
  0.6 0.8 shard_map.129
  1.4 8.3 %collective-permute-start = (bf16[32,512]{1,0:T(8,128)(2,1)S(1)}, bf16[32,512]{1,0:T(8,128)(2,1)S(1)}, u32[]{:S(2)}, u32[]{:S(2)}) collective-permute-start(bf16[32,512]{1,0:T(8,128)(2,1)S(1)} %get-tuple-element.27), channel_id=1, source_target_pairs={{0,256},{256,0},{1,257},{257,1},{2,258},{258,2},{3,259},{259,3},{4... | collective-permute-start | bytes 98312 | tf_op jit(solution)/shard_map/ppermute | solution.py:217
  9.7 10.6 %collective-permute-start.1 = (bf16[32,512]{1,0:T(8,128)(2,1)S(1)}, bf16[32,512]{1,0:T(8,128)(2,1)S(1)}, u32[]{:S(2)}, u32[]{:S(2)}) collective-permute-start(bf16[32,512]{1,0:T(8,128)(2,1)S(1)} %get-tuple-element.28), channel_id=1, source_target_pairs={{0,32},{32,0},{1,33},{33,1},{2,34},{34,2},{3,35},{35,3},{4,36},{36... | collective-permute-start | bytes 98312 | tf_op jit(solution)/shard_map/ppermute | solution.py:217
  20.4 3.1 %collective-permute-start.2 = (bf16[32,512]{1,0:T(8,128)(2,1)S(1)}, bf16[32,512]{1,0:T(8,128)(2,1)S(1)}, u32[]{:S(2)}, u32[]{:S(2)}) collective-permute-start(bf16[32,512]{1,0:T(8,128)(2,1)S(1)} %get-tuple-element.29), channel_id=1, source_target_pairs={{0,8},{8,0},{1,9},{9,1},{2,10},{10,2},{3,11},{11,3},{4,12},{12,4},... | collective-permute-start | bytes 98312 | tf_op jit(solution)/shard_map/ppermute | solution.py:217
  23.5 2.1 %shard_map.130 = (bf16[12,128,128]{2,1,0:T(8,128)(2,1)S(1)}, bf16[12,128,128]{2,1,0:T(8,128)(2,1)S(1)}, bf16[32,256]{1,0:T(8,128)(2,1)S(1)}, bf16[32,256]{1,0:T(...) custom-call(s32[12]{0:T(128)} %rows.3, s32[12]{0:T(128)} %cols.3, ...), custom_call_target="tpu_custom_call" | custom-call | bytes 1048576 | tf_op jit(solution)/shard_map/pallas_call | solution.py:211
  25.6 0.0 collective-permute-done.r2
  25.6 0.0 collective-permute-done.1.r1
  25.6 0.0 collective-permute-done.2.r0
  25.6 1.0 %shard_map.131 = bf16[4,160,512]{2,1,0:T(8,128)(2,1)S(1)} custom-call(s32[12]{0:T(128)} %brows.3, bf16[32,512]{1,0:T(8,128)(2,1)S(1)} %collective-permute-done.r2, bf16[32,512]{1,0:T(8,128)(2,1)S(1)} %collective-permute-done.1.r1, bf16[32,512]{1,0:T(8,128)(2,1)S(1)} %collective-permute-done.2.r0, ...), custom_call_target="tpu_custom_call", output_to_operand_aliasing={{}: (6, {})} | custom-call | bytes 1048576 | tf_op jit(solution)/shard_map/pallas_call | solution.py:211
  26.6 12.3 %all_to_all.20.got = bf16[4,160,512]{2,1,0:T(8,128)(2,1)S(1)} all-to-all(bf16[4,160,512]{2,1,0:T(8,128)(2,1)S(1)} %shard_map.131), channel_id=1, replica_groups=mesh['y2'=2,'yl'=4,'z2'=2,'z1'=2,'z0'=2,'c'=2,'f'=4] {'f'}, dimensions={0} | all-to-all | bytes 1310720 | tf_op jit(solution)/shard_map/all_to_all | solution.py:241
  39.0 2.3 %shard_map.132 = (bf16[64,512]{1,0:T(8,128)(2,1)S(1)}, f32[4,32,128]{2,1,0:T(8,128)S(1)}, bf16[4,32,128]{2,1,0:T(8,128)(2,1)S(1)}, bf16[32,512]{1,0:T(8,128)(2,1)S(1)}, bf16[16,32,128]{2,1,0:T(8,128)(2,1)}) custom-call(s32[12]{0:T(128)} %brows.3, bf16[4,160,512]{2,1,0:T(8,128)(2,1)S(1)} %all_to_all.20.got, bf16[32,256]{1,0:T(8,128)(2,1)S(1)} %get-tuple-element.34.ws, ...), custom_call_target="tpu_custom_call" | custom-call | bytes 1048576 | tf_op jit(solution)/shard_map/pallas_call | solution.py:211
  41.3 7.3 %all-to-all-start.1 = ((bf16[16,32,128]{2,1,0:T(8,128)(2,1)}), bf16[16,32,128]{2,1,0:T(8,128)(2,1)S(1)}, u32[]{:S(2)}, u32[]{:S(2)}) async-start(bf16[16,32,128]{2,1,0:T(8,128)(2,1)} %get-tuple-element.41), calls=%async_computation.1 | async-start | bytes 262144 | tf_op jit(solution)/shard_map/all_to_all | solution.py:254
  48.6 1.9 %collective-permute-start.3 = (bf16[32,512]{1,0:T(8,128)(2,1)S(1)}, bf16[32,512]{1,0:T(8,128)(2,1)S(1)}, u32[]{:S(2)}, u32[]{:S(2)}) collective-permute-start(bf16[32,512]{1,0:T(8,128)(2,1)S(1)} %get-tuple-element.42), channel_id=1, source_target_pairs={{0,256},{256,0},{1,257},{257,1},{2,258},{258,2},{3,259},{259,3},{4... | collective-permute-start | bytes 98312 | tf_op jit(solution)/shard_map/ppermute | solution.py:217
  50.5 1.4 %shard_map.133 = (f32[32,512]{1,0:T(8,128)S(1)}, bf16[64,512]{1,0:T(8,128)(2,1)}) custom-call(s32[12]{0:T(128)} %rows.3, s32[12]{0:T(128)} %cols.3, f32[4,32,128]{2,1,0:T(8,128)S(1)} %get-tuple-element.36.own, bf16[4,32,128]{2,1,0:T(8,128)(2,1)S(1)} %get-tuple-element.37.ga, bf16[12,128,128]{2,1,0:T(8,128)(2,1)S(1)} %get-tuple-element.38.adj, ...), custom_call_target="tpu_custom_call" | custom-call | bytes 1048576 | tf_op jit(solution)/shard_map/pallas_call | solution.py:211
  52.0 5.4 %collective-permute-done.3.c2 = bf16[32,512]{1,0:T(8,128)(2,1)S(1)} collective-permute-done((bf16[32,512]{1,0:T(8,128)(2,1)S(1)}, bf16[32,512]{1,0:T(8,128)(2,1)S(1)}, u32[]{:S(2)}, u32[]{:S(2)}) %collective-permute-start.3) | collective-permute-done | bytes 32800 | tf_op jit(solution)/shard_map/ppermute | solution.py:217
  57.3 0.7 all-to-all-done.1.slots
  58.1 9.2 %all_to_all.21.terms = f32[8,8,128]{2,1,0:T(8,128)S(1)} all-to-all(f32[8,8,128]{2,1,0:T(8,128)S(1)} %shard_map.134), channel_id=1, replica_groups=mesh['y2'=2,'yl'=4,'z2'=2,'z1'=2,'z0'=2,'c'=2,'f'=4] {'y2','yl'}, dimensions={0} | all-to-all | bytes 65536 | tf_op jit(solution)/shard_map/all_to_all | solution.py:264
  67.3 17.9 %all_to_all.22.slots = bf16[16,32,128]{2,1,0:T(8,128)(2,1)S(1)} all-to-all(bf16[16,32,128]{2,1,0:T(8,128)(2,1)S(1)} %shard_map.135), channel_id=1, replica_groups=mesh['y2'=2,'yl'=4,'z2'=2,'z1'=2,'z0'=2,'c'=2,'f'=4] {'z2','z1','z0','c'}, dimensions={0} | all-to-all | bytes 262144 | tf_op jit(solution)/shard_map/all_to_all | solution.py:266
  85.3 1.4 %shard_map.136 = (f32[32,512]{1,0:T(8,128)}, f32[32,256]{1,0:T(8,128)}, f32[32,256]{1,0:T(8,128)}) custom-call(s32[12]{0:T(128)} %send.3, bf16[16,32,128]{2,1,0:T(8,128)(2,1)S(1)} %all_to_all.22.slots, f32[32,512]{1,0:T(8,128)S(1)} %get-tuple-element.45.base, bf16[32,512]{1,0:T(8,128)(2,1)S(1)} %collective-permute-done.3.c2), custom_call_target="tpu_custom_call" | custom-call | bytes 1048576 | tf_op jit(solution)/shard_map/pallas_call | solution.py:211
  (2 shorter events, 0.0 us)
Async XLA Ops:
  1.4 24.1 %collective-permute-start = (bf16[32,512]{1,0:T(8,128)(2,1)S(1)}, bf16[32,512]{1,0:T(8,128)(2,1)S(1)}, u32[]{:S(2)}, u32[]{:S(2)}) collective-permute-start(bf16[32,512]{1,0:T(8,128)(2,1)S(1)} %get-tuple-element.27), channel_id=1, source_target_pairs={{0,256},{256,0},{1,257},{257,1},{2,258},{258,2},{3,259},{259,3},{4... | collective-permute-start | bytes 98312 | tf_op jit(solution)/shard_map/ppermute | solution.py:217
  9.7 15.9 %collective-permute-start.1 = (bf16[32,512]{1,0:T(8,128)(2,1)S(1)}, bf16[32,512]{1,0:T(8,128)(2,1)S(1)}, u32[]{:S(2)}, u32[]{:S(2)}) collective-permute-start(bf16[32,512]{1,0:T(8,128)(2,1)S(1)} %get-tuple-element.28), channel_id=1, source_target_pairs={{0,32},{32,0},{1,33},{33,1},{2,34},{34,2},{3,35},{35,3},{4,36},{36... | collective-permute-start | bytes 98312 | tf_op jit(solution)/shard_map/ppermute | solution.py:217
  20.4 5.2 %collective-permute-start.2 = (bf16[32,512]{1,0:T(8,128)(2,1)S(1)}, bf16[32,512]{1,0:T(8,128)(2,1)S(1)}, u32[]{:S(2)}, u32[]{:S(2)}) collective-permute-start(bf16[32,512]{1,0:T(8,128)(2,1)S(1)} %get-tuple-element.29), channel_id=1, source_target_pairs={{0,8},{8,0},{1,9},{9,1},{2,10},{10,2},{3,11},{11,3},{4,12},{12,4},... | collective-permute-start | bytes 98312 | tf_op jit(solution)/shard_map/ppermute | solution.py:217
  41.3 16.8 %all-to-all-start.1 = ((bf16[16,32,128]{2,1,0:T(8,128)(2,1)}), bf16[16,32,128]{2,1,0:T(8,128)(2,1)S(1)}, u32[]{:S(2)}, u32[]{:S(2)}) async-start(bf16[16,32,128]{2,1,0:T(8,128)(2,1)} %get-tuple-element.41), calls=%async_computation.1 | async-start | bytes 262144 | tf_op jit(solution)/shard_map/all_to_all | solution.py:254
  48.6 8.8 %collective-permute-start.3 = (bf16[32,512]{1,0:T(8,128)(2,1)S(1)}, bf16[32,512]{1,0:T(8,128)(2,1)S(1)}, u32[]{:S(2)}, u32[]{:S(2)}) collective-permute-start(bf16[32,512]{1,0:T(8,128)(2,1)S(1)} %get-tuple-element.42), channel_id=1, source_target_pairs={{0,256},{256,0},{1,257},{257,1},{2,258},{258,2},{3,259},{259,3},{4... | collective-permute-start | bytes 98312 | tf_op jit(solution)/shard_map/ppermute | solution.py:217

commit v7 on v6

--- a/solution.py
+++ b/solution.py
@@ -140,10 +140,11 @@
         ga[t] = both[FR:, tile_of(t)].astype(bf16)
     for s in range(ROUNDS * BT):
         r, b = divmod(s, BT)
-        back = jnp.dot(ga[brows[s]], badj[s], preferred_element_type=f32).astype(bf16)
+        back = jnp.dot(ga[brows[s]], badj[s], preferred_element_type=f32)
         if r == 2:
             b2[:, tile_of(b)] = back
         else:
+            back = back.astype(bf16)
             slots[r * 8 + b, 16:, :] = back[:16]
             slots[r * 8 + 4 + b, 16:, :] = back[16:]
 
@@ -184,7 +185,7 @@
     for s in range(ROUNDS * BT):
         r, b = divmod(s, BT)
         if r == 2:
-            gx[:, lanes(send[s])] += c2[:, tile_of(b)].astype(f32)
+            gx[:, lanes(send[s])] += c2[:, tile_of(b)]
         else:
             gx[:16, lanes(send[s])] += slots[r * 8 + b, 16:, :].astype(f32)
             gx[16:, lanes(send[s])] += slots[r * 8 + 4 + b, 16:, :].astype(f32)
@@ -246,7 +247,7 @@
             V((HR, LOCAL), bf16),
             V((TILES, FR, TILE), f32),
             V((TILES, FR, TILE), bf16),
-            part,
+            V((FR, LOCAL), f32),
             S((NZC, 32, TILE), bf16),
         ),
         (V((2 * F_IN, F_HID), bf16), V((2 * F_IN, LOCAL), bf16), V((F_HID, LOCAL), f32)),
@@ -259,9 +260,10 @@
         (V((FR, LOCAL), f32), S((HR, LOCAL), bf16)),
         (V((TILES, FR, TILE), f32),),
     )(in_rows, in_cols, own, ga, in_adj, y)
-    slots, home, base = lax.optimization_barrier((slots, home, base))
+    slots, base = lax.optimization_barrier((slots, base))
     terms = call(first_sum_kernel, (0,), V((NY, 8, TILE), f32))(slots)
     terms = lax.all_to_all(terms, Y, 0, 0, tiled=True)
+    terms, home = lax.optimization_barrier((terms, home))
     slots = call(second_sum_kernel, (0, 0), V((NZC, 32, TILE), bf16))(terms, slots)
     slots = lax.all_to_all(slots, ZC, 0, 0, tiled=True)
     gx, gws, gwn = call(

time: 87.2 us -> 86 us (0.986)
  blocking collectives: 39.5 us -> 27.2 us
  waiting for transfers between devices: 6.08 us -> 13.2 us
  starting transfers between devices: 31.3 us -> 34.6 us
    all_to_all x1 -> x0, blocking collectives: 9.24 us -> none  [shards(): terms = lax.all_to_all(terms, Y, 0, 0, tiled=True)]
    all_to_all x0 -> x1, waiting for transfers between devices: none -> 7.13 us  [shards(): terms = lax.all_to_all(terms, Y, 0, 0, tiled=True)]
    all_to_all x1, waiting for transfers between devices: 0.71 us -> 6.08 us  [shards(): slots = lax.all_to_all(slots, ZC, 0, 0, tiled=True)]
    ppermute x4, waiting for transfers between devices: 5.37 us -> 0.01 us  [swap(): return lax.ppermute(x, axis, [(0, 1), (1, 0)])]
    all_to_all x0 -> x1, starting transfers between devices: none -> 3.34 us  [shards(): terms = lax.all_to_all(terms, Y, 0, 0, tiled=True)]
    all_to_all x1, blocking collectives: 17.9 us -> 14.8 us  [shards(): slots = lax.all_to_all(slots, ZC, 0, 0, tiled=True)]
  transfers between devices with their start and end apart: 5 -> 6, of which waited for: 2 -> 2; matrix products, arithmetic and copies ran while one was open for 0% -> 0% of each run, Pallas kernels for 4% -> 5%
where the time goes in v7:
time: 86 us; the launch traced here: 85.4 us
  starting transfers between devices  34.6 us (40%)
  blocking collectives  27.2 us (32%)
  waiting for transfers between devices  13.2 us (15%)
  Pallas kernels  9.67 us (11%)
    ppermute x4, starting transfers between devices, swap(): return lax.ppermute(x, axis, [(0, 1), (1, 0)])  24 us
    all_to_all x1, blocking collectives, shards(): slots = lax.all_to_all(slots, ZC, 0, 0, tiled=True)  14.8 us
    all_to_all x1, blocking collectives, shards(): block = lax.all_to_all(give, 'f', 0, 0, tiled=True)  12.3 us
    pallas_call x8, Pallas kernels, apply(): return run(*near)  9.67 us
    all_to_all x1, starting transfers between devices, shards(): slots = lax.all_to_all(slots, ZC, 0, 0, tiled=True)  7.32 us
    all_to_all x1, waiting for transfers between devices, shards(): terms = lax.all_to_all(terms, Y, 0, 0, tiled=True)  7.13 us
    all_to_all x1, waiting for transfers between devices, shards(): slots = lax.all_to_all(slots, ZC, 0, 0, tiled=True)  6.08 us
    all_to_all x1, starting transfers between devices, shards(): terms = lax.all_to_all(terms, Y, 0, 0, tiled=True)  3.34 us
  transfers between devices with their start and end apart: 6, of which 2 were waited for; matrix products, arithmetic and copies ran while one was open for 0% of the time, Pallas kernels for 5%

profile of v7, /device:TPU:1, one launch (start us, length us, event | category | flops | bytes accessed | tf_op | source)
XLA Modules:
  0.0 85.4 jit_solution(7347169255038205654)
XLA Ops:
  0.6 0.8 shard_map.129
  1.4 8.3 %collective-permute-start = (bf16[32,512]{1,0:T(8,128)(2,1)S(1)}, bf16[32,512]{1,0:T(8,128)(2,1)S(1)}, u32[]{:S(2)}, u32[]{:S(2)}) collective-permute-start(bf16[32,512]{1,0:T(8,128)(2,1)S(1)} %get-tuple-element.28), channel_id=1, source_target_pairs={{0,256},{256,0},{1,257},{257,1},{2,258},{258,2},{3,259},{259,3},{4... | collective-permute-start | bytes 98312 | tf_op jit(solution)/shard_map/ppermute | solution.py:218
  9.7 10.6 %collective-permute-start.1 = (bf16[32,512]{1,0:T(8,128)(2,1)S(1)}, bf16[32,512]{1,0:T(8,128)(2,1)S(1)}, u32[]{:S(2)}, u32[]{:S(2)}) collective-permute-start(bf16[32,512]{1,0:T(8,128)(2,1)S(1)} %get-tuple-element.29), channel_id=1, source_target_pairs={{0,32},{32,0},{1,33},{33,1},{2,34},{34,2},{3,35},{35,3},{4,36},{36... | collective-permute-start | bytes 98312 | tf_op jit(solution)/shard_map/ppermute | solution.py:218
  20.4 3.1 %collective-permute-start.2 = (bf16[32,512]{1,0:T(8,128)(2,1)S(1)}, bf16[32,512]{1,0:T(8,128)(2,1)S(1)}, u32[]{:S(2)}, u32[]{:S(2)}) collective-permute-start(bf16[32,512]{1,0:T(8,128)(2,1)S(1)} %get-tuple-element.30), channel_id=1, source_target_pairs={{0,8},{8,0},{1,9},{9,1},{2,10},{10,2},{3,11},{11,3},{4,12},{12,4},... | collective-permute-start | bytes 98312 | tf_op jit(solution)/shard_map/ppermute | solution.py:218
  23.5 2.1 %shard_map.130 = (bf16[12,128,128]{2,1,0:T(8,128)(2,1)S(1)}, bf16[12,128,128]{2,1,0:T(8,128)(2,1)S(1)}, bf16[32,256]{1,0:T(8,128)(2,1)S(1)}, bf16[32,256]{1,0:T(...) custom-call(s32[12]{0:T(128)} %rows.3, s32[12]{0:T(128)} %cols.3, ...), custom_call_target="tpu_custom_call" | custom-call | bytes 1048576 | tf_op jit(solution)/shard_map/pallas_call | solution.py:212
  25.6 0.0 collective-permute-done.r2
  25.6 0.0 collective-permute-done.1.r1
  25.6 0.0 collective-permute-done.2.r0
  25.6 1.0 %shard_map.131 = bf16[4,160,512]{2,1,0:T(8,128)(2,1)S(1)} custom-call(s32[12]{0:T(128)} %brows.3, bf16[32,512]{1,0:T(8,128)(2,1)S(1)} %collective-permute-done.r2, bf16[32,512]{1,0:T(8,128)(2,1)S(1)} %collective-permute-done.1.r1, bf16[32,512]{1,0:T(8,128)(2,1)S(1)} %collective-permute-done.2.r0, ...), custom_call_target="tpu_custom_call", output_to_operand_aliasing={{}: (6, {})} | custom-call | bytes 1048576 | tf_op jit(solution)/shard_map/pallas_call | solution.py:212
  26.6 12.3 %all_to_all.20.got = bf16[4,160,512]{2,1,0:T(8,128)(2,1)S(1)} all-to-all(bf16[4,160,512]{2,1,0:T(8,128)(2,1)S(1)} %shard_map.131), channel_id=1, replica_groups=mesh['y2'=2,'yl'=4,'z2'=2,'z1'=2,'z0'=2,'c'=2,'f'=4] {'f'}, dimensions={0} | all-to-all | bytes 1310720 | tf_op jit(solution)/shard_map/all_to_all | solution.py:242
  39.0 2.3 %shard_map.132 = (bf16[64,512]{1,0:T(8,128)(2,1)S(1)}, f32[4,32,128]{2,1,0:T(8,128)S(1)}, bf16[4,32,128]{2,1,0:T(8,128)(2,1)S(1)}, f32[32,512]{1,0:T(8,128)S(1)}, bf16[16,32,128]{2,1,0:T(8,128)(2,1)}) custom-call(s32[12]{0:T(128)} %brows.3, bf16[4,160,512]{2,1,0:T(8,128)(2,1)S(1)} %all_to_all.20.got, bf16[32,256]{1,0:T(8,128)(2,1)S(1)} %get-tuple-element.35.ws, ...), custom_call_target="tpu_custom_call" | custom-call | bytes 1048576 | tf_op jit(solution)/shard_map/pallas_call | solution.py:212
  41.3 7.3 %all-to-all-start.1 = ((bf16[16,32,128]{2,1,0:T(8,128)(2,1)}), bf16[16,32,128]{2,1,0:T(8,128)(2,1)S(1)}, u32[]{:S(2)}, u32[]{:S(2)}) async-start(bf16[16,32,128]{2,1,0:T(8,128)(2,1)} %get-tuple-element.42), calls=%async_computation.1 | async-start | bytes 262144 | tf_op jit(solution)/shard_map/all_to_all | solution.py:255
  48.6 1.9 %collective-permute-start.3 = (f32[32,512]{1,0:T(8,128)S(1)}, f32[32,512]{1,0:T(8,128)S(1)}, u32[]{:S(2)}, u32[]{:S(2)}) collective-permute-start(f32[32,512]{1,0:T(8,128)S(1)} %get-tuple-element.45), channel_id=1, source_target_pairs={{0,256},{256,0},{1,257},{257,1},{2,258},{258,2},{3,259},{259,3},{4... | collective-permute-start | bytes 196616 | tf_op jit(solution)/shard_map/ppermute | solution.py:218
  50.5 1.4 %shard_map.133 = (f32[32,512]{1,0:T(8,128)S(1)}, bf16[64,512]{1,0:T(8,128)(2,1)}) custom-call(s32[12]{0:T(128)} %rows.3, s32[12]{0:T(128)} %cols.3, f32[4,32,128]{2,1,0:T(8,128)S(1)} %get-tuple-element.37.own, bf16[4,32,128]{2,1,0:T(8,128)(2,1)S(1)} %get-tuple-element.38.ga, bf16[12,128,128]{2,1,0:T(8,128)(2,1)S(1)} %get-tuple-element.39.adj, ...), custom_call_target="tpu_custom_call" | custom-call | bytes 1048576 | tf_op jit(solution)/shard_map/pallas_call | solution.py:212
  52.0 6.1 %all-to-all-done.1.slots = bf16[16,32,128]{2,1,0:T(8,128)(2,1)S(1)} async-done(((bf16[16,32,128]{2,1,0:T(8,128)(2,1)}), bf16[16,32,128]{2,1,0:T(8,128)(2,1)S(1)}, u32[]{:S(2)}, u32[]{:S(2)}) %all-to-all-start.1) | async-done | bytes 131104 | tf_op jit(solution)/shard_map/all_to_all | solution.py:255
  58.1 0.6 shard_map.134
  58.7 3.3 %all-to-all-start.2 = ((f32[8,8,128]{2,1,0:T(8,128)}), f32[8,8,128]{2,1,0:T(8,128)S(1)}, u32[]{:S(2)}, u32[]{:S(2)}) async-start(f32[8,8,128]{2,1,0:T(8,128)} %shard_map.134), calls=%async_computation.2 | async-start | bytes 65536 | tf_op jit(solution)/shard_map/all_to_all | solution.py:265
  62.0 0.0 collective-permute-done.3.c2
  62.0 7.1 %all-to-all-done.2.terms = f32[8,8,128]{2,1,0:T(8,128)S(1)} async-done(((f32[8,8,128]{2,1,0:T(8,128)}), f32[8,8,128]{2,1,0:T(8,128)S(1)}, u32[]{:S(2)}, u32[]{:S(2)}) %all-to-all-start.2) | async-done | bytes 32800 | tf_op jit(solution)/shard_map/all_to_all | solution.py:265
  69.2 14.8 %all_to_all.21.slots = bf16[16,32,128]{2,1,0:T(8,128)(2,1)S(1)} all-to-all(bf16[16,32,128]{2,1,0:T(8,128)(2,1)S(1)} %shard_map.135), channel_id=1, replica_groups=mesh['y2'=2,'yl'=4,'z2'=2,'z1'=2,'z0'=2,'c'=2,'f'=4] {'z2','z1','z0','c'}, dimensions={0} | all-to-all | bytes 262144 | tf_op jit(solution)/shard_map/all_to_all | solution.py:268
  84.0 1.4 %shard_map.136 = (f32[32,512]{1,0:T(8,128)}, f32[32,256]{1,0:T(8,128)}, f32[32,256]{1,0:T(8,128)}) custom-call(s32[12]{0:T(128)} %send.3, bf16[16,32,128]{2,1,0:T(8,128)(2,1)S(1)} %all_to_all.21.slots, f32[32,512]{1,0:T(8,128)S(1)} %get-tuple-element.47.base, f32[32,512]{1,0:T(8,128)S(1)} %collective-permute-done.3.c2), custom_call_target="tpu_custom_call" | custom-call | bytes 1048576 | tf_op jit(solution)/shard_map/pallas_call | solution.py:212
  (1 shorter events, 0.0 us)
Async XLA Ops:
  1.4 24.1 %collective-permute-start = (bf16[32,512]{1,0:T(8,128)(2,1)S(1)}, bf16[32,512]{1,0:T(8,128)(2,1)S(1)}, u32[]{:S(2)}, u32[]{:S(2)}) collective-permute-start(bf16[32,512]{1,0:T(8,128)(2,1)S(1)} %get-tuple-element.28), channel_id=1, source_target_pairs={{0,256},{256,0},{1,257},{257,1},{2,258},{258,2},{3,259},{259,3},{4... | collective-permute-start | bytes 98312 | tf_op jit(solution)/shard_map/ppermute | solution.py:218
  9.7 15.8 %collective-permute-start.1 = (bf16[32,512]{1,0:T(8,128)(2,1)S(1)}, bf16[32,512]{1,0:T(8,128)(2,1)S(1)}, u32[]{:S(2)}, u32[]{:S(2)}) collective-permute-start(bf16[32,512]{1,0:T(8,128)(2,1)S(1)} %get-tuple-element.29), channel_id=1, source_target_pairs={{0,32},{32,0},{1,33},{33,1},{2,34},{34,2},{3,35},{35,3},{4,36},{36... | collective-permute-start | bytes 98312 | tf_op jit(solution)/shard_map/ppermute | solution.py:218
  20.4 5.2 %collective-permute-start.2 = (bf16[32,512]{1,0:T(8,128)(2,1)S(1)}, bf16[32,512]{1,0:T(8,128)(2,1)S(1)}, u32[]{:S(2)}, u32[]{:S(2)}) collective-permute-start(bf16[32,512]{1,0:T(8,128)(2,1)S(1)} %get-tuple-element.30), channel_id=1, source_target_pairs={{0,8},{8,0},{1,9},{9,1},{2,10},{10,2},{3,11},{11,3},{4,12},{12,4},... | collective-permute-start | bytes 98312 | tf_op jit(solution)/shard_map/ppermute | solution.py:218
  41.3 16.8 %all-to-all-start.1 = ((bf16[16,32,128]{2,1,0:T(8,128)(2,1)}), bf16[16,32,128]{2,1,0:T(8,128)(2,1)S(1)}, u32[]{:S(2)}, u32[]{:S(2)}) async-start(bf16[16,32,128]{2,1,0:T(8,128)(2,1)} %get-tuple-element.42), calls=%async_computation.1 | async-start | bytes 262144 | tf_op jit(solution)/shard_map/all_to_all | solution.py:255
  48.6 13.5 %collective-permute-start.3 = (f32[32,512]{1,0:T(8,128)S(1)}, f32[32,512]{1,0:T(8,128)S(1)}, u32[]{:S(2)}, u32[]{:S(2)}) collective-permute-start(f32[32,512]{1,0:T(8,128)S(1)} %get-tuple-element.45), channel_id=1, source_target_pairs={{0,256},{256,0},{1,257},{257,1},{2,258},{258,2},{3,259},{259,3},{4... | collective-permute-start | bytes 196616 | tf_op jit(solution)/shard_map/ppermute | solution.py:218
  58.7 10.5 %all-to-all-start.2 = ((f32[8,8,128]{2,1,0:T(8,128)}), f32[8,8,128]{2,1,0:T(8,128)S(1)}, u32[]{:S(2)}, u32[]{:S(2)}) async-start(f32[8,8,128]{2,1,0:T(8,128)} %shard_map.134), calls=%async_computation.2 | async-start | bytes 65536 | tf_op jit(solution)/shard_map/all_to_all | solution.py:265

commit v8 on v6

--- a/solution.py
+++ b/solution.py
@@ -30,7 +30,6 @@
 ZC = ("z2", "z1", "z0", "c")
 NZC = 16
 PAIRS = ("z0", "z2", "y2")
-FLIP = (2, 8)
 
 R_AGG, R_X, R_G, R_W = 0, FR, 2 * FR, 2 * FR + HR
 ROWS = R_W + FR
@@ -97,17 +96,7 @@
             give[i, R_AGG : R_AGG + FR, tile_of(t)] = part
 
 
-def split(w):
-    high = w.astype(bf16).astype(f32)
-    return jnp.concatenate([high, w - high], axis=0).astype(bf16)
-
-
-def whole(two):
-    both = two.astype(f32)
-    return both[:8] + both[8:]
-
-
-def node_kernel(brows, got, ws, wn, badj, y, acc, ga, b2, slots, lhs, rhs, act_all):
+def node_kernel(brows, got, ws, wn, badj, y, acc, ga, b0, b1, b2, slots, lhs, rhs, act_all):
     for i in range(NF):
         lhs[i * FR : (i + 1) * FR, :] = got[i, R_W : R_W + FR, :F_HID]
         lhs[F_IN + i * FR : F_IN + (i + 1) * FR, :] = got[i, R_W : R_W + FR, F_HID:]
@@ -131,21 +120,19 @@
         got[f, R_AGG : R_AGG + 2 * FR, :], grad, (((1,), (1,)), ((), ())), preferred_element_type=f32
     ) * (1.0 / math.sqrt(NODES))
     for j in range(NZC):
-        slots[j, :16, :] = split(w[j // 2 * 8 : j // 2 * 8 + 8, tile_of(j % 2)])
+        slots[j] = w[j // 2 * 8 : j // 2 * 8 + 8, tile_of(j % 2)]
     both = jnp.dot(
         jnp.concatenate([ws[...], wn[...]], axis=0), grad, preferred_element_type=f32
     )
     for t in range(TILES):
         acc[t] = both[:FR, tile_of(t)]
         ga[t] = both[FR:, tile_of(t)].astype(bf16)
+    outs = (b0, b1, b2)
     for s in range(ROUNDS * BT):
         r, b = divmod(s, BT)
-        back = jnp.dot(ga[brows[s]], badj[s], preferred_element_type=f32).astype(bf16)
-        if r == 2:
-            b2[:, tile_of(b)] = back
-        else:
-            slots[r * 8 + b, 16:, :] = back[:16]
-            slots[r * 8 + 4 + b, 16:, :] = back[16:]
+        outs[r][:, tile_of(b)] = jnp.dot(
+            ga[brows[s]], badj[s], preferred_element_type=f32
+        ).astype(outs[r].dtype)
 
 
 def back_kernel(rows, cols, own, ga, adj, y, base, out, acc):
@@ -157,37 +144,24 @@
         base[:, tile_of(t)] = acc[t]
 
 
-def first_sum_kernel(slots, out):
-    total = whole(slots[0, :16, :])
-    for j in range(1, NZC):
-        total += whole(slots[j, :16, :])
-    for j in range(NY):
-        out[j] = total
-
-
-def second_sum_kernel(terms, slots, out):
+def sum_kernel(terms, out):
     total = terms[0]
-    for j in range(1, NY):
+    for j in range(1, terms.shape[0]):
         total += terms[j]
-    done = split(total)
-    flip = jnp.where(lax.axis_index("z2") == 0, FLIP[0], FLIP[1])
-    for j in range(NZC):
-        out[j, :16, :] = done
-        out[j, 16:, :] = slots[j ^ flip, 16:, :]
-
-
-def join_kernel(send, slots, base, c2, gx, gws, gwn):
+    for j in range(out.shape[0]):
+        out[j] = total.astype(out.dtype)
+
+
+def grad_x_kernel(send, base, c0, c1, c2, out):
+    out[...] = base[...]
+    for s in range(ROUNDS * BT):
+        out[:, lanes(send[s])] += (c0, c1, c2)[s // BT][:, tile_of(s % BT)].astype(f32)
+
+
+def weights_kernel(slots, gws, gwn):
     for j in range(NZC):
         out, row = (gwn, j // 2 * 8) if j < 8 else (gws, j // 2 * 8 - FR)
-        out[row : row + 8, tile_of(j % 2)] = whole(slots[j, :16, :])
-    gx[...] = base[...]
-    for s in range(ROUNDS * BT):
-        r, b = divmod(s, BT)
-        if r == 2:
-            gx[:, lanes(send[s])] += c2[:, tile_of(b)].astype(f32)
-        else:
-            gx[:16, lanes(send[s])] += slots[r * 8 + b, 16:, :].astype(f32)
-            gx[16:, lanes(send[s])] += slots[r * 8 + 4 + b, 16:, :].astype(f32)
+        out[row : row + 8, tile_of(j % 2)] = slots[j].astype(f32)
 
 
 def call(kernel, ins, outs, scratch=(), flops=0, nbytes=1 << 20, aliases=()):
@@ -239,7 +213,7 @@
         aliases=((6, 0),),
     )(bnd_rows, *got, bnd_adj, acc, give)
     block = lax.all_to_all(give, "f", 0, 0, tiled=True)
-    y, own, ga, back, slots = call(
+    y, own, ga, b0, b1, b2, slots = call(
         node_kernel,
         (1,) + (0,) * 4,
         (
@@ -247,28 +221,30 @@
             V((TILES, FR, TILE), f32),
             V((TILES, FR, TILE), bf16),
             part,
-            S((NZC, 32, TILE), bf16),
+            *(V((FR, LOCAL), f32),) * 2,
+            S((NZC, 8, TILE), f32),
         ),
         (V((2 * F_IN, F_HID), bf16), V((2 * F_IN, LOCAL), bf16), V((F_HID, LOCAL), f32)),
     )(bnd_rows, block, ws, wn, bnd_adj)
     slots = lax.all_to_all(slots, ZC, 0, 0, tiled=True)
-    home = swap(back, PAIRS[2])
+    c2 = swap(b2, PAIRS[2])
     base, y = call(
         back_kernel,
         (1, 1) + (0,) * 4,
         (V((FR, LOCAL), f32), S((HR, LOCAL), bf16)),
         (V((TILES, FR, TILE), f32),),
     )(in_rows, in_cols, own, ga, in_adj, y)
-    slots, home, base = lax.optimization_barrier((slots, home, base))
-    terms = call(first_sum_kernel, (0,), V((NY, 8, TILE), f32))(slots)
+    slots, base, b1 = lax.optimization_barrier((slots, base, b1))
+    c1 = swap(b1, PAIRS[1])
+    terms = call(sum_kernel, (0,), S((NY, 8, TILE), f32))(slots)
     terms = lax.all_to_all(terms, Y, 0, 0, tiled=True)
-    slots = call(second_sum_kernel, (0, 0), V((NZC, 32, TILE), bf16))(terms, slots)
+    terms, c2, b0 = lax.optimization_barrier((terms, c2, b0))
+    c0 = swap(b0, PAIRS[0])
+    slots = call(sum_kernel, (0,), S((NZC, 8, TILE), bf16))(terms)
     slots = lax.all_to_all(slots, ZC, 0, 0, tiled=True)
-    gx, gws, gwn = call(
-        join_kernel,
-        (1, 0, 0, 0),
-        (S((FR, LOCAL), f32), S((FR, F_HID), f32), S((FR, F_HID), f32)),
-    )(bnd_send, slots, base, home)
+    gx = call(grad_x_kernel, (1, 0, 0, 0, 0), S((FR, LOCAL), f32))(bnd_send, base, c0, c1, c2)
+    half = S((FR, F_HID), f32)
+    gws, gwn = call(weights_kernel, (0,), (half, half))(slots)
     return y, gx, gws, gwn
 
 

time: 87.2 us -> 84.2 us (0.966)
  blocking collectives: 39.5 us -> 12.3 us
  starting transfers between devices: 31.3 us -> 51.8 us
  waiting for transfers between devices: 6.08 us -> 7.91 us
  Pallas kernels: 9.04 us -> 10.7 us
    all_to_all x2 -> x0, blocking collectives: 27.2 us -> none  [the longest x1 17.9 us: shards(): slots = lax.all_to_all(slots, ZC, 0, 0, tiled=True)]
    ppermute x4 -> x6, starting transfers between devices: 24 us -> 33.3 us  [swap(): return lax.ppermute(x, axis, [(0, 1), (1, 0)])]
    all_to_all x1 -> x2, starting transfers between devices: 7.32 us -> 15.2 us  [shards(): slots = lax.all_to_all(slots, ZC, 0, 0, tiled=True)]
    all_to_all x1 -> x2, waiting for transfers between devices: 0.71 us -> 5.39 us  [shards(): slots = lax.all_to_all(slots, ZC, 0, 0, tiled=True)]
    ppermute x4 -> x6, waiting for transfers between devices: 5.37 us -> 1.77 us  [swap(): return lax.ppermute(x, axis, [(0, 1), (1, 0)])]
    all_to_all x0 -> x1, starting transfers between devices: none -> 3.34 us  [shards(): terms = lax.all_to_all(terms, Y, 0, 0, tiled=True)]
    pallas_call x8 -> x9, Pallas kernels: 9.04 us -> 10.7 us  [apply(): return run(*near)]
  transfers between devices with their start and end apart: 5 -> 9, of which waited for: 2 -> 4; matrix products, arithmetic and copies ran while one was open for 0% -> 0% of each run, Pallas kernels for 4% -> 7%
where the time goes in v8:
time: 84.2 us; the launch traced here: 83.5 us
  starting transfers between devices  51.8 us (62%)
  blocking collectives  12.3 us (15%)
  Pallas kernels  10.7 us (13%)
  waiting for transfers between devices  7.91 us (9%)
    ppermute x6, starting transfers between devices, swap(): return lax.ppermute(x, axis, [(0, 1), (1, 0)])  33.3 us
    all_to_all x2, starting transfers between devices, shards(): slots = lax.all_to_all(slots, ZC, 0, 0, tiled=True)  15.2 us
    all_to_all x1, blocking collectives, shards(): block = lax.all_to_all(give, 'f', 0, 0, tiled=True)  12.3 us
    pallas_call x9, Pallas kernels, apply(): return run(*near)  10.7 us
    all_to_all x2, waiting for transfers between devices, shards(): slots = lax.all_to_all(slots, ZC, 0, 0, tiled=True)  5.39 us
    all_to_all x1, starting transfers between devices, shards(): terms = lax.all_to_all(terms, Y, 0, 0, tiled=True)  3.34 us
    ppermute x6, waiting for transfers between devices, swap(): return lax.ppermute(x, axis, [(0, 1), (1, 0)])  1.77 us
  transfers between devices with their start and end apart: 9, of which 4 were waited for; matrix products, arithmetic and copies ran while one was open for 0% of the time, Pallas kernels for 7%

profile of v8, /device:TPU:1, one launch (start us, length us, event | category | flops | bytes accessed | tf_op | source)
XLA Modules:
  0.0 83.5 jit_solution(4403086101003100715)
XLA Ops:
  0.6 0.8 shard_map.129
  1.4 8.3 %collective-permute-start = (bf16[32,512]{1,0:T(8,128)(2,1)S(1)}, bf16[32,512]{1,0:T(8,128)(2,1)S(1)}, u32[]{:S(2)}, u32[]{:S(2)}) collective-permute-start(bf16[32,512]{1,0:T(8,128)(2,1)S(1)} %get-tuple-element.31), channel_id=1, source_target_pairs={{0,256},{256,0},{1,257},{257,1},{2,258},{258,2},{3,259},{259,3},{4... | collective-permute-start | bytes 98312 | tf_op jit(solution)/shard_map/ppermute | solution.py:191
  9.7 10.6 %collective-permute-start.1 = (bf16[32,512]{1,0:T(8,128)(2,1)S(1)}, bf16[32,512]{1,0:T(8,128)(2,1)S(1)}, u32[]{:S(2)}, u32[]{:S(2)}) collective-permute-start(bf16[32,512]{1,0:T(8,128)(2,1)S(1)} %get-tuple-element.32), channel_id=1, source_target_pairs={{0,32},{32,0},{1,33},{33,1},{2,34},{34,2},{3,35},{35,3},{4,36},{36... | collective-permute-start | bytes 98312 | tf_op jit(solution)/shard_map/ppermute | solution.py:191
  20.4 3.1 %collective-permute-start.2 = (bf16[32,512]{1,0:T(8,128)(2,1)S(1)}, bf16[32,512]{1,0:T(8,128)(2,1)S(1)}, u32[]{:S(2)}, u32[]{:S(2)}) collective-permute-start(bf16[32,512]{1,0:T(8,128)(2,1)S(1)} %get-tuple-element.33), channel_id=1, source_target_pairs={{0,8},{8,0},{1,9},{9,1},{2,10},{10,2},{3,11},{11,3},{4,12},{12,4},... | collective-permute-start | bytes 98312 | tf_op jit(solution)/shard_map/ppermute | solution.py:191
  23.5 2.1 %shard_map.130 = (bf16[12,128,128]{2,1,0:T(8,128)(2,1)S(1)}, bf16[12,128,128]{2,1,0:T(8,128)(2,1)S(1)}, bf16[32,256]{1,0:T(8,128)(2,1)S(1)}, bf16[32,256]{1,0:T(...) custom-call(s32[12]{0:T(128)} %rows.3, s32[12]{0:T(128)} %cols.3, ...), custom_call_target="tpu_custom_call" | custom-call | bytes 1048576 | tf_op jit(solution)/shard_map/pallas_call | solution.py:185
  25.6 0.0 collective-permute-done.r2
  25.6 0.0 collective-permute-done.1.r1
  25.6 0.0 collective-permute-done.2.r0
  25.6 1.0 %shard_map.131 = bf16[4,160,512]{2,1,0:T(8,128)(2,1)S(1)} custom-call(s32[12]{0:T(128)} %brows.3, bf16[32,512]{1,0:T(8,128)(2,1)S(1)} %collective-permute-done.r2, bf16[32,512]{1,0:T(8,128)(2,1)S(1)} %collective-permute-done.1.r1, bf16[32,512]{1,0:T(8,128)(2,1)S(1)} %collective-permute-done.2.r0, ...), custom_call_target="tpu_custom_call", output_to_operand_aliasing={{}: (6, {})} | custom-call | bytes 1048576 | tf_op jit(solution)/shard_map/pallas_call | solution.py:185
  26.6 12.3 %all_to_all.20.got = bf16[4,160,512]{2,1,0:T(8,128)(2,1)S(1)} all-to-all(bf16[4,160,512]{2,1,0:T(8,128)(2,1)S(1)} %shard_map.131), channel_id=1, replica_groups=mesh['y2'=2,'yl'=4,'z2'=2,'z1'=2,'z0'=2,'c'=2,'f'=4] {'f'}, dimensions={0} | all-to-all | bytes 1310720 | tf_op jit(solution)/shard_map/all_to_all | solution.py:215
  39.0 2.2 %shard_map.132 = (bf16[64,512]{1,0:T(8,128)(2,1)S(1)}, f32[4,32,128]{2,1,0:T(8,128)S(1)}, bf16[4,32,128]{2,1,0:T(8,128)(2,1)S(1)}, bf16[32,512]{1,0:T(8,128)(2,1...) custom-call(s32[12]{0:T(128)} %brows.3, bf16[4,160,512]{2,1,0:T(8,128)(2,1)S(1)} %all_to_all.20.got, ...), custom_call_target="tpu_custom_call" | custom-call | bytes 1048576 | tf_op jit(solution)/shard_map/pallas_call | solution.py:185
  41.1 7.3 %all-to-all-start.1 = ((f32[16,8,128]{2,1,0:T(8,128)}), f32[16,8,128]{2,1,0:T(8,128)S(1)}, u32[]{:S(2)}, u32[]{:S(2)}) async-start(f32[16,8,128]{2,1,0:T(8,128)} %get-tuple-element.45), calls=%async_computation.1 | async-start | bytes 131072 | tf_op jit(solution)/shard_map/all_to_all | solution.py:229
  48.5 1.9 %collective-permute-start.3 = (f32[32,512]{1,0:T(8,128)S(1)}, f32[32,512]{1,0:T(8,128)S(1)}, u32[]{:S(2)}, u32[]{:S(2)}) collective-permute-start(f32[32,512]{1,0:T(8,128)S(1)} %get-tuple-element.50), channel_id=1, source_target_pairs={{0,256},{256,0},{1,257},{257,1},{2,258},{258,2},{3,259},{259,3},{4... | collective-permute-start | bytes 196616 | tf_op jit(solution)/shard_map/ppermute | solution.py:191
  50.4 1.4 %shard_map.133 = (f32[32,512]{1,0:T(8,128)S(1)}, bf16[64,512]{1,0:T(8,128)(2,1)}) custom-call(s32[12]{0:T(128)} %rows.3, s32[12]{0:T(128)} %cols.3, f32[4,32,128]{2,1,0:T(8,128)S(1)} %get-tuple-element.40.own, bf16[4,32,128]{2,1,0:T(8,128)(2,1)S(1)} %get-tuple-element.41.ga, bf16[12,128,128]{2,1,0:T(8,128)(2,1)S(1)} %get-tuple-element.42.adj, ...), custom_call_target="tpu_custom_call" | custom-call | bytes 1048576 | tf_op jit(solution)/shard_map/pallas_call | solution.py:185
  51.8 4.4 %all-to-all-done.1.terms = f32[16,8,128]{2,1,0:T(8,128)S(1)} async-done(((f32[16,8,128]{2,1,0:T(8,128)}), f32[16,8,128]{2,1,0:T(8,128)S(1)}, u32[]{:S(2)}, u32[]{:S(2)}) %all-to-all-start.1) | async-done | bytes 65568 | tf_op jit(solution)/shard_map/all_to_all | solution.py:229
  56.3 0.6 shard_map.134
  56.9 3.3 %all-to-all-start.2 = ((f32[8,8,128]{2,1,0:T(8,128)}), f32[8,8,128]{2,1,0:T(8,128)S(1)}, u32[]{:S(2)}, u32[]{:S(2)}) async-start(f32[8,8,128]{2,1,0:T(8,128)} %shard_map.134), calls=%async_computation.2 | async-start | bytes 65536 | tf_op jit(solution)/shard_map/all_to_all | solution.py:240
  60.2 6.0 %collective-permute-start.5 = (f32[32,512]{1,0:T(8,128)S(1)}, f32[32,512]{1,0:T(8,128)S(1)}, u32[]{:S(2)}, u32[]{:S(2)}) collective-permute-start(f32[32,512]{1,0:T(8,128)S(1)} %get-tuple-element.53), channel_id=1, source_target_pairs={{0,32},{32,0},{1,33},{33,1},{2,34},{34,2},{3,35},{35,3},{4,36},{36... | collective-permute-start | bytes 196616 | tf_op jit(solution)/shard_map/ppermute | solution.py:191
  66.3 0.0 collective-permute-done.3.c2
  66.3 0.7 all-to-all-done.2.terms
  67.0 0.6 shard_map.136
  67.7 7.9 %all-to-all-start.3 = ((bf16[16,8,128]{2,1,0:T(8,128)(2,1)}), bf16[16,8,128]{2,1,0:T(8,128)(2,1)S(1)}, u32[]{:S(2)}, u32[]{:S(2)}) async-start(bf16[16,8,128]{2,1,0:T(8,128)(2,1)} %shard_map.136), calls=%async_computation.3 | async-start | bytes 65536 | tf_op jit(solution)/shard_map/all_to_all | solution.py:244
  75.5 3.3 %collective-permute-start.4 = (bf16[32,512]{1,0:T(8,128)(2,1)S(1)}, bf16[32,512]{1,0:T(8,128)(2,1)S(1)}, u32[]{:S(2)}, u32[]{:S(2)}) collective-permute-start(bf16[32,512]{1,0:T(8,128)(2,1)S(1)} %get-tuple-element.52), channel_id=1, source_target_pairs={{0,8},{8,0},{1,9},{9,1},{2,10},{10,2},{3,11},{11,3},{4,12},{12,4},... | collective-permute-start | bytes 98312 | tf_op jit(solution)/shard_map/ppermute | solution.py:191
  78.8 0.0 collective-permute-done.5.c1
  78.8 1.8 %collective-permute-done.4.c0 = bf16[32,512]{1,0:T(8,128)(2,1)S(1)} collective-permute-done((bf16[32,512]{1,0:T(8,128)(2,1)S(1)}, bf16[32,512]{1,0:T(8,128)(2,1)S(1)}, u32[]{:S(2)}, u32[]{:S(2)}) %collective-permute-start.4) | collective-permute-done | bytes 32800 | tf_op jit(solution)/shard_map/ppermute | solution.py:191
  80.6 1.4 %shard_map.135 = f32[32,512]{1,0:T(8,128)} custom-call(s32[12]{0:T(128)} %send.3, f32[32,512]{1,0:T(8,128)S(1)} %get-tuple-element.48.base, bf16[32,512]{1,0:T(8,128)(2,1)S(1)} %collective-permute-done.4.c0, f32[32,512]{1,0:T(8,128)S(1)} %collective-permute-done.5.c1, f32[32,512]{1,0:T(8,128)S(1)} %collective-permute-done.3.c2), custom_call_target="tpu_custom_call" | custom-call | bytes 1048576 | tf_op jit(solution)/shard_map/pallas_call | solution.py:185
  81.9 1.0 %all-to-all-done.3.slots = bf16[16,8,128]{2,1,0:T(8,128)(2,1)S(1)} async-done(((bf16[16,8,128]{2,1,0:T(8,128)(2,1)}), bf16[16,8,128]{2,1,0:T(8,128)(2,1)S(1)}, u32[]{:S(2)}, u32[]{:S(2)}) %all-to-all-start.3) | async-done | bytes 32800 | tf_op jit(solution)/shard_map/all_to_all | solution.py:244
  82.9 0.6 shard_map.137
Async XLA Ops:
  1.4 24.1 %collective-permute-start = (bf16[32,512]{1,0:T(8,128)(2,1)S(1)}, bf16[32,512]{1,0:T(8,128)(2,1)S(1)}, u32[]{:S(2)}, u32[]{:S(2)}) collective-permute-start(bf16[32,512]{1,0:T(8,128)(2,1)S(1)} %get-tuple-element.31), channel_id=1, source_target_pairs={{0,256},{256,0},{1,257},{257,1},{2,258},{258,2},{3,259},{259,3},{4... | collective-permute-start | bytes 98312 | tf_op jit(solution)/shard_map/ppermute | solution.py:191
  9.7 15.8 %collective-permute-start.1 = (bf16[32,512]{1,0:T(8,128)(2,1)S(1)}, bf16[32,512]{1,0:T(8,128)(2,1)S(1)}, u32[]{:S(2)}, u32[]{:S(2)}) collective-permute-start(bf16[32,512]{1,0:T(8,128)(2,1)S(1)} %get-tuple-element.32), channel_id=1, source_target_pairs={{0,32},{32,0},{1,33},{33,1},{2,34},{34,2},{3,35},{35,3},{4,36},{36... | collective-permute-start | bytes 98312 | tf_op jit(solution)/shard_map/ppermute | solution.py:191
  20.4 5.2 %collective-permute-start.2 = (bf16[32,512]{1,0:T(8,128)(2,1)S(1)}, bf16[32,512]{1,0:T(8,128)(2,1)S(1)}, u32[]{:S(2)}, u32[]{:S(2)}) collective-permute-start(bf16[32,512]{1,0:T(8,128)(2,1)S(1)} %get-tuple-element.33), channel_id=1, source_target_pairs={{0,8},{8,0},{1,9},{9,1},{2,10},{10,2},{3,11},{11,3},{4,12},{12,4},... | collective-permute-start | bytes 98312 | tf_op jit(solution)/shard_map/ppermute | solution.py:191
  41.1 15.1 %all-to-all-start.1 = ((f32[16,8,128]{2,1,0:T(8,128)}), f32[16,8,128]{2,1,0:T(8,128)S(1)}, u32[]{:S(2)}, u32[]{:S(2)}) async-start(f32[16,8,128]{2,1,0:T(8,128)} %get-tuple-element.45), calls=%async_computation.1 | async-start | bytes 131072 | tf_op jit(solution)/shard_map/all_to_all | solution.py:229
  48.5 17.8 %collective-permute-start.3 = (f32[32,512]{1,0:T(8,128)S(1)}, f32[32,512]{1,0:T(8,128)S(1)}, u32[]{:S(2)}, u32[]{:S(2)}) collective-permute-start(f32[32,512]{1,0:T(8,128)S(1)} %get-tuple-element.50), channel_id=1, source_target_pairs={{0,256},{256,0},{1,257},{257,1},{2,258},{258,2},{3,259},{259,3},{4... | collective-permute-start | bytes 196616 | tf_op jit(solution)/shard_map/ppermute | solution.py:191
  56.9 10.1 %all-to-all-start.2 = ((f32[8,8,128]{2,1,0:T(8,128)}), f32[8,8,128]{2,1,0:T(8,128)S(1)}, u32[]{:S(2)}, u32[]{:S(2)}) async-start(f32[8,8,128]{2,1,0:T(8,128)} %shard_map.134), calls=%async_computation.2 | async-start | bytes 65536 | tf_op jit(solution)/shard_map/all_to_all | solution.py:240
  60.2 18.6 %collective-permute-start.5 = (f32[32,512]{1,0:T(8,128)S(1)}, f32[32,512]{1,0:T(8,128)S(1)}, u32[]{:S(2)}, u32[]{:S(2)}) collective-permute-start(f32[32,512]{1,0:T(8,128)S(1)} %get-tuple-element.53), channel_id=1, source_target_pairs={{0,32},{32,0},{1,33},{33,1},{2,34},{34,2},{3,35},{35,3},{4,36},{36... | collective-permute-start | bytes 196616 | tf_op jit(solution)/shard_map/ppermute | solution.py:191
  67.7 15.2 %all-to-all-start.3 = ((bf16[16,8,128]{2,1,0:T(8,128)(2,1)}), bf16[16,8,128]{2,1,0:T(8,128)(2,1)S(1)}, u32[]{:S(2)}, u32[]{:S(2)}) async-start(bf16[16,8,128]{2,1,0:T(8,128)(2,1)} %shard_map.136), calls=%async_computation.3 | async-start | bytes 65536 | tf_op jit(solution)/shard_map/all_to_all | solution.py:244
  75.5 5.1 %collective-permute-start.4 = (bf16[32,512]{1,0:T(8,128)(2,1)S(1)}, bf16[32,512]{1,0:T(8,128)(2,1)S(1)}, u32[]{:S(2)}, u32[]{:S(2)}) collective-permute-start(bf16[32,512]{1,0:T(8,128)(2,1)S(1)} %get-tuple-element.52), channel_id=1, source_target_pairs={{0,8},{8,0},{1,9},{9,1},{2,10},{10,2},{3,11},{11,3},{4,12},{12,4},... | collective-permute-start | bytes 98312 | tf_op jit(solution)/shard_map/ppermute | solution.py:191

commit v9 on v8

--- a/solution.py
+++ b/solution.py
@@ -130,18 +130,7 @@
     outs = (b0, b1, b2)
     for s in range(ROUNDS * BT):
         r, b = divmod(s, BT)
-        outs[r][:, tile_of(b)] = jnp.dot(
-            ga[brows[s]], badj[s], preferred_element_type=f32
-        ).astype(outs[r].dtype)
-
-
-def back_kernel(rows, cols, own, ga, adj, y, base, out, acc):
-    out[...] = y[...]
-    acc[...] = own[...]
-    for k in range(KIN):
-        acc[cols[k]] += jnp.dot(ga[rows[k]], adj[k], preferred_element_type=f32)
-    for t in range(TILES):
-        base[:, tile_of(t)] = acc[t]
+        outs[r][:, tile_of(b)] = jnp.dot(ga[brows[s]], badj[s], preferred_element_type=f32)
 
 
 def sum_kernel(terms, out):
@@ -152,10 +141,15 @@
         out[j] = total.astype(out.dtype)
 
 
-def grad_x_kernel(send, base, c0, c1, c2, out):
-    out[...] = base[...]
+def grad_x_kernel(rows, cols, send, own, ga, adj, c0, c1, c2, y, out, y_out, acc):
+    y_out[...] = y[...]
+    acc[...] = own[...]
+    for k in range(KIN):
+        acc[cols[k]] += jnp.dot(ga[rows[k]], adj[k], preferred_element_type=f32)
     for s in range(ROUNDS * BT):
-        out[:, lanes(send[s])] += (c0, c1, c2)[s // BT][:, tile_of(s % BT)].astype(f32)
+        acc[send[s]] += (c0, c1, c2)[s // BT][:, tile_of(s % BT)]
+    for t in range(TILES):
+        out[:, tile_of(t)] = acc[t]
 
 
 def weights_kernel(slots, gws, gwn):
@@ -220,29 +214,27 @@
             V((HR, LOCAL), bf16),
             V((TILES, FR, TILE), f32),
             V((TILES, FR, TILE), bf16),
-            part,
-            *(V((FR, LOCAL), f32),) * 2,
+            *(V((FR, LOCAL), f32),) * 3,
             S((NZC, 8, TILE), f32),
         ),
         (V((2 * F_IN, F_HID), bf16), V((2 * F_IN, LOCAL), bf16), V((F_HID, LOCAL), f32)),
     )(bnd_rows, block, ws, wn, bnd_adj)
     slots = lax.all_to_all(slots, ZC, 0, 0, tiled=True)
     c2 = swap(b2, PAIRS[2])
-    base, y = call(
-        back_kernel,
-        (1, 1) + (0,) * 4,
-        (V((FR, LOCAL), f32), S((HR, LOCAL), bf16)),
-        (V((TILES, FR, TILE), f32),),
-    )(in_rows, in_cols, own, ga, in_adj, y)
-    slots, base, b1 = lax.optimization_barrier((slots, base, b1))
+    c0 = swap(b0, PAIRS[0])
+    slots, b1 = lax.optimization_barrier((slots, b1))
     c1 = swap(b1, PAIRS[1])
     terms = call(sum_kernel, (0,), S((NY, 8, TILE), f32))(slots)
     terms = lax.all_to_all(terms, Y, 0, 0, tiled=True)
-    terms, c2, b0 = lax.optimization_barrier((terms, c2, b0))
-    c0 = swap(b0, PAIRS[0])
+    terms, c2, c0, own = lax.optimization_barrier((terms, c2, c0, own))
     slots = call(sum_kernel, (0,), S((NZC, 8, TILE), bf16))(terms)
     slots = lax.all_to_all(slots, ZC, 0, 0, tiled=True)
-    gx = call(grad_x_kernel, (1, 0, 0, 0, 0), S((FR, LOCAL), f32))(bnd_send, base, c0, c1, c2)
+    gx, y = call(
+        grad_x_kernel,
+        (1, 1, 1) + (0,) * 7,
+        (S((FR, LOCAL), f32), S((HR, LOCAL), bf16)),
+        (V((TILES, FR, TILE), f32),),
+    )(in_rows, in_cols, bnd_send, own, ga, in_adj, c0, c1, c2, y)
     half = S((FR, F_HID), f32)
     gws, gwn = call(weights_kernel, (0,), (half, half))(slots)
     return y, gx, gws, gwn

time: 84.2 us -> 85.2 us (1.012)
  waiting for transfers between devices: 7.91 us -> 9.14 us
  Pallas kernels: 10.7 us -> 9.55 us
  starting transfers between devices: 51.8 us -> 52.8 us
    all_to_all x2, waiting for transfers between devices: 5.39 us -> 8.37 us  [shards(): slots = lax.all_to_all(slots, ZC, 0, 0, tiled=True)]
    ppermute x6, waiting for transfers between devices: 1.77 us -> 0.02 us  [swap(): return lax.ppermute(x, axis, [(0, 1), (1, 0)])]
    pallas_call x9 -> x8, Pallas kernels: 10.7 us -> 9.55 us  [apply(): return run(*near)]
  transfers between devices with their start and end apart: 9 -> 9, of which waited for: 4 -> 3; matrix products, arithmetic and copies ran while one was open for 0% -> 0% of each run, Pallas kernels for 7% -> 6%
where the time goes in v9:
time: 85.2 us; the launch traced here: 84.6 us
  starting transfers between devices  52.8 us (62%)
  blocking collectives  12.3 us (14%)
  Pallas kernels  9.55 us (11%)
  waiting for transfers between devices  9.14 us (11%)
    ppermute x6, starting transfers between devices, swap(): return lax.ppermute(x, axis, [(0, 1), (1, 0)])  33.3 us
    all_to_all x2, starting transfers between devices, shards(): slots = lax.all_to_all(slots, ZC, 0, 0, tiled=True)  15.4 us
    all_to_all x1, blocking collectives, shards(): block = lax.all_to_all(give, 'f', 0, 0, tiled=True)  12.3 us
    pallas_call x8, Pallas kernels, apply(): return run(*near)  9.55 us
    all_to_all x2, waiting for transfers between devices, shards(): slots = lax.all_to_all(slots, ZC, 0, 0, tiled=True)  8.37 us
    all_to_all x1, starting transfers between devices, shards(): terms = lax.all_to_all(terms, Y, 0, 0, tiled=True)  4.06 us
  transfers between devices with their start and end apart: 9, of which 3 were waited for; matrix products, arithmetic and copies ran while one was open for 0% of the time, Pallas kernels for 6%

profile of v9, /device:TPU:1, one launch (start us, length us, event | category | flops | bytes accessed | tf_op | source)
XLA Modules:
  0.0 84.6 jit_solution(2981901829980867031)
XLA Ops:
  0.6 0.8 shard_map.129
  1.4 8.3 %collective-permute-start = (bf16[32,512]{1,0:T(8,128)(2,1)S(1)}, bf16[32,512]{1,0:T(8,128)(2,1)S(1)}, u32[]{:S(2)}, u32[]{:S(2)}) collective-permute-start(bf16[32,512]{1,0:T(8,128)(2,1)S(1)} %get-tuple-element.31), channel_id=1, source_target_pairs={{0,256},{256,0},{1,257},{257,1},{2,258},{258,2},{3,259},{259,3},{4... | collective-permute-start | bytes 98312 | tf_op jit(solution)/shard_map/ppermute | solution.py:185
  9.7 10.6 %collective-permute-start.1 = (bf16[32,512]{1,0:T(8,128)(2,1)S(1)}, bf16[32,512]{1,0:T(8,128)(2,1)S(1)}, u32[]{:S(2)}, u32[]{:S(2)}) collective-permute-start(bf16[32,512]{1,0:T(8,128)(2,1)S(1)} %get-tuple-element.32), channel_id=1, source_target_pairs={{0,32},{32,0},{1,33},{33,1},{2,34},{34,2},{3,35},{35,3},{4,36},{36... | collective-permute-start | bytes 98312 | tf_op jit(solution)/shard_map/ppermute | solution.py:185
  20.4 3.1 %collective-permute-start.2 = (bf16[32,512]{1,0:T(8,128)(2,1)S(1)}, bf16[32,512]{1,0:T(8,128)(2,1)S(1)}, u32[]{:S(2)}, u32[]{:S(2)}) collective-permute-start(bf16[32,512]{1,0:T(8,128)(2,1)S(1)} %get-tuple-element.33), channel_id=1, source_target_pairs={{0,8},{8,0},{1,9},{9,1},{2,10},{10,2},{3,11},{11,3},{4,12},{12,4},... | collective-permute-start | bytes 98312 | tf_op jit(solution)/shard_map/ppermute | solution.py:185
  23.5 2.1 %shard_map.130 = (bf16[12,128,128]{2,1,0:T(8,128)(2,1)S(1)}, bf16[12,128,128]{2,1,0:T(8,128)(2,1)S(1)}, bf16[32,256]{1,0:T(8,128)(2,1)S(1)}, bf16[32,256]{1,0:T(...) custom-call(s32[12]{0:T(128)} %rows.3, s32[12]{0:T(128)} %cols.3, ...), custom_call_target="tpu_custom_call" | custom-call | bytes 1048576 | tf_op jit(solution)/shard_map/pallas_call | solution.py:179
  25.6 0.0 collective-permute-done.r2
  25.6 0.0 collective-permute-done.1.r1
  25.6 0.0 collective-permute-done.2.r0
  25.6 1.0 %shard_map.131 = bf16[4,160,512]{2,1,0:T(8,128)(2,1)S(1)} custom-call(s32[12]{0:T(128)} %brows.3, bf16[32,512]{1,0:T(8,128)(2,1)S(1)} %collective-permute-done.r2, bf16[32,512]{1,0:T(8,128)(2,1)S(1)} %collective-permute-done.1.r1, bf16[32,512]{1,0:T(8,128)(2,1)S(1)} %collective-permute-done.2.r0, ...), custom_call_target="tpu_custom_call", output_to_operand_aliasing={{}: (6, {})} | custom-call | bytes 1048576 | tf_op jit(solution)/shard_map/pallas_call | solution.py:179
  26.6 12.3 %all_to_all.20.got = bf16[4,160,512]{2,1,0:T(8,128)(2,1)S(1)} all-to-all(bf16[4,160,512]{2,1,0:T(8,128)(2,1)S(1)} %shard_map.131), channel_id=1, replica_groups=mesh['y2'=2,'yl'=4,'z2'=2,'z1'=2,'z0'=2,'c'=2,'f'=4] {'f'}, dimensions={0} | all-to-all | bytes 1310720 | tf_op jit(solution)/shard_map/all_to_all | solution.py:209
  39.0 2.2 %shard_map.132 = (bf16[64,512]{1,0:T(8,128)(2,1)S(1)}, f32[4,32,128]{2,1,0:T(8,128)S(1)}, bf16[4,32,128]{2,1,0:T(8,128)(2,1)S(1)}, f32[32,512]{1,0:T(8,128)S(1)}...) custom-call(s32[12]{0:T(128)} %brows.3, bf16[4,160,512]{2,1,0:T(8,128)(2,1)S(1)} %all_to_all.20.got, ...), custom_call_target="tpu_custom_call" | custom-call | bytes 1048576 | tf_op jit(solution)/shard_map/pallas_call | solution.py:179
  41.1 7.3 %all-to-all-start.1 = ((f32[16,8,128]{2,1,0:T(8,128)}), f32[16,8,128]{2,1,0:T(8,128)S(1)}, u32[]{:S(2)}, u32[]{:S(2)}) async-start(f32[16,8,128]{2,1,0:T(8,128)} %get-tuple-element.40), calls=%async_computation.1 | async-start | bytes 131072 | tf_op jit(solution)/shard_map/all_to_all | solution.py:222
  48.4 1.9 %collective-permute-start.3 = (f32[32,512]{1,0:T(8,128)S(1)}, f32[32,512]{1,0:T(8,128)S(1)}, u32[]{:S(2)}, u32[]{:S(2)}) collective-permute-start(f32[32,512]{1,0:T(8,128)S(1)} %get-tuple-element.43), channel_id=1, source_target_pairs={{0,256},{256,0},{1,257},{257,1},{2,258},{258,2},{3,259},{259,3},{4... | collective-permute-start | bytes 196616 | tf_op jit(solution)/shard_map/ppermute | solution.py:185
  50.4 3.3 %collective-permute-start.4 = (f32[32,512]{1,0:T(8,128)S(1)}, f32[32,512]{1,0:T(8,128)S(1)}, u32[]{:S(2)}, u32[]{:S(2)}) collective-permute-start(f32[32,512]{1,0:T(8,128)S(1)} %get-tuple-element.44), channel_id=1, source_target_pairs={{0,8},{8,0},{1,9},{9,1},{2,10},{10,2},{3,11},{11,3},{4,12},{12,4},... | collective-permute-start | bytes 196616 | tf_op jit(solution)/shard_map/ppermute | solution.py:185
  53.7 2.6 %all-to-all-done.1.terms = f32[16,8,128]{2,1,0:T(8,128)S(1)} async-done(((f32[16,8,128]{2,1,0:T(8,128)}), f32[16,8,128]{2,1,0:T(8,128)S(1)}, u32[]{:S(2)}, u32[]{:S(2)}) %all-to-all-start.1) | async-done | bytes 65568 | tf_op jit(solution)/shard_map/all_to_all | solution.py:222
  56.3 0.6 shard_map.133
  56.9 4.1 %all-to-all-start.2 = ((f32[8,8,128]{2,1,0:T(8,128)}), f32[8,8,128]{2,1,0:T(8,128)S(1)}, u32[]{:S(2)}, u32[]{:S(2)}) async-start(f32[8,8,128]{2,1,0:T(8,128)} %shard_map.133), calls=%async_computation.2 | async-start | bytes 65536 | tf_op jit(solution)/shard_map/all_to_all | solution.py:228
  60.9 6.1 %collective-permute-start.5 = (f32[32,512]{1,0:T(8,128)S(1)}, f32[32,512]{1,0:T(8,128)S(1)}, u32[]{:S(2)}, u32[]{:S(2)}) collective-permute-start(f32[32,512]{1,0:T(8,128)S(1)} %get-tuple-element.50), channel_id=1, source_target_pairs={{0,32},{32,0},{1,33},{33,1},{2,34},{34,2},{3,35},{35,3},{4,36},{36... | collective-permute-start | bytes 196616 | tf_op jit(solution)/shard_map/ppermute | solution.py:185
  67.0 0.0 collective-permute-done.3.c2
  67.1 0.0 collective-permute-done.4.c0
  67.1 0.8 all-to-all-done.2.terms
  67.8 0.6 shard_map.135
  68.5 8.1 %all-to-all-start.3 = ((bf16[16,8,128]{2,1,0:T(8,128)(2,1)}), bf16[16,8,128]{2,1,0:T(8,128)(2,1)S(1)}, u32[]{:S(2)}, u32[]{:S(2)}) async-start(bf16[16,8,128]{2,1,0:T(8,128)(2,1)} %shard_map.135), calls=%async_computation.3 | async-start | bytes 65536 | tf_op jit(solution)/shard_map/all_to_all | solution.py:231
  76.6 0.0 collective-permute-done.5.c1
  76.6 1.6 %shard_map.134 = (f32[32,512]{1,0:T(8,128)}, bf16[64,512]{1,0:T(8,128)(2,1)}) custom-call(s32[12]{0:T(128)} %rows.3, s32[12]{0:T(128)} %cols.3, s32[12]{0:T(128)} %send.3, f32[4,32,128]{2,1,0:T(8,128)S(1)} %get-tuple-element.46.own, bf16[4,32,128]{2,1,0:T(8,128)(2,1)S(1)} %get-tuple-element.47.ga, bf16[12,128,128]{2,1,0:T(8,128)(2,1)S(1)} %get-tuple-element.48.adj, ...), custom_call_target="tpu_custom_call" | custom-call | bytes 1048576 | tf_op jit(solution)/shard_map/pallas_call | solution.py:179
  78.2 5.8 %all-to-all-done.3.slots = bf16[16,8,128]{2,1,0:T(8,128)(2,1)S(1)} async-done(((bf16[16,8,128]{2,1,0:T(8,128)(2,1)}), bf16[16,8,128]{2,1,0:T(8,128)(2,1)S(1)}, u32[]{:S(2)}, u32[]{:S(2)}) %all-to-all-start.3) | async-done | bytes 32800 | tf_op jit(solution)/shard_map/all_to_all | solution.py:231
  84.0 0.6 shard_map.136
Async XLA Ops:
  1.4 24.1 %collective-permute-start = (bf16[32,512]{1,0:T(8,128)(2,1)S(1)}, bf16[32,512]{1,0:T(8,128)(2,1)S(1)}, u32[]{:S(2)}, u32[]{:S(2)}) collective-permute-start(bf16[32,512]{1,0:T(8,128)(2,1)S(1)} %get-tuple-element.31), channel_id=1, source_target_pairs={{0,256},{256,0},{1,257},{257,1},{2,258},{258,2},{3,259},{259,3},{4... | collective-permute-start | bytes 98312 | tf_op jit(solution)/shard_map/ppermute | solution.py:185
  9.7 15.8 %collective-permute-start.1 = (bf16[32,512]{1,0:T(8,128)(2,1)S(1)}, bf16[32,512]{1,0:T(8,128)(2,1)S(1)}, u32[]{:S(2)}, u32[]{:S(2)}) collective-permute-start(bf16[32,512]{1,0:T(8,128)(2,1)S(1)} %get-tuple-element.32), channel_id=1, source_target_pairs={{0,32},{32,0},{1,33},{33,1},{2,34},{34,2},{3,35},{35,3},{4,36},{36... | collective-permute-start | bytes 98312 | tf_op jit(solution)/shard_map/ppermute | solution.py:185
  20.4 5.2 %collective-permute-start.2 = (bf16[32,512]{1,0:T(8,128)(2,1)S(1)}, bf16[32,512]{1,0:T(8,128)(2,1)S(1)}, u32[]{:S(2)}, u32[]{:S(2)}) collective-permute-start(bf16[32,512]{1,0:T(8,128)(2,1)S(1)} %get-tuple-element.33), channel_id=1, source_target_pairs={{0,8},{8,0},{1,9},{9,1},{2,10},{10,2},{3,11},{11,3},{4,12},{12,4},... | collective-permute-start | bytes 98312 | tf_op jit(solution)/shard_map/ppermute | solution.py:185
  41.1 15.1 %all-to-all-start.1 = ((f32[16,8,128]{2,1,0:T(8,128)}), f32[16,8,128]{2,1,0:T(8,128)S(1)}, u32[]{:S(2)}, u32[]{:S(2)}) async-start(f32[16,8,128]{2,1,0:T(8,128)} %get-tuple-element.40), calls=%async_computation.1 | async-start | bytes 131072 | tf_op jit(solution)/shard_map/all_to_all | solution.py:222
  48.4 18.6 %collective-permute-start.3 = (f32[32,512]{1,0:T(8,128)S(1)}, f32[32,512]{1,0:T(8,128)S(1)}, u32[]{:S(2)}, u32[]{:S(2)}) collective-permute-start(f32[32,512]{1,0:T(8,128)S(1)} %get-tuple-element.43), channel_id=1, source_target_pairs={{0,256},{256,0},{1,257},{257,1},{2,258},{258,2},{3,259},{259,3},{4... | collective-permute-start | bytes 196616 | tf_op jit(solution)/shard_map/ppermute | solution.py:185
  50.4 16.7 %collective-permute-start.4 = (f32[32,512]{1,0:T(8,128)S(1)}, f32[32,512]{1,0:T(8,128)S(1)}, u32[]{:S(2)}, u32[]{:S(2)}) collective-permute-start(f32[32,512]{1,0:T(8,128)S(1)} %get-tuple-element.44), channel_id=1, source_target_pairs={{0,8},{8,0},{1,9},{9,1},{2,10},{10,2},{3,11},{11,3},{4,12},{12,4},... | collective-permute-start | bytes 196616 | tf_op jit(solution)/shard_map/ppermute | solution.py:185
  56.9 10.9 %all-to-all-start.2 = ((f32[8,8,128]{2,1,0:T(8,128)}), f32[8,8,128]{2,1,0:T(8,128)S(1)}, u32[]{:S(2)}, u32[]{:S(2)}) async-start(f32[8,8,128]{2,1,0:T(8,128)} %shard_map.133), calls=%async_computation.2 | async-start | bytes 65536 | tf_op jit(solution)/shard_map/all_to_all | solution.py:228
  60.9 15.6 %collective-permute-start.5 = (f32[32,512]{1,0:T(8,128)S(1)}, f32[32,512]{1,0:T(8,128)S(1)}, u32[]{:S(2)}, u32[]{:S(2)}) collective-permute-start(f32[32,512]{1,0:T(8,128)S(1)} %get-tuple-element.50), channel_id=1, source_target_pairs={{0,32},{32,0},{1,33},{33,1},{2,34},{34,2},{3,35},{35,3},{4,36},{36... | collective-permute-start | bytes 196616 | tf_op jit(solution)/shard_map/ppermute | solution.py:185
  68.5 15.5 %all-to-all-start.3 = ((bf16[16,8,128]{2,1,0:T(8,128)(2,1)}), bf16[16,8,128]{2,1,0:T(8,128)(2,1)S(1)}, u32[]{:S(2)}, u32[]{:S(2)}) async-start(bf16[16,8,128]{2,1,0:T(8,128)(2,1)} %shard_map.135), calls=%async_computation.3 | async-start | bytes 65536 | tf_op jit(solution)/shard_map/all_to_all | solution.py:231

commit v10 on v8

--- a/solution.py
+++ b/solution.py
@@ -140,8 +140,7 @@
     acc[...] = own[...]
     for k in range(KIN):
         acc[cols[k]] += jnp.dot(ga[rows[k]], adj[k], preferred_element_type=f32)
-    for t in range(TILES):
-        base[:, tile_of(t)] = acc[t]
+    base[...] = acc[...]
 
 
 def sum_kernel(terms, out):
@@ -152,16 +151,21 @@
         out[j] = total.astype(out.dtype)
 
 
-def grad_x_kernel(send, base, c0, c1, c2, out):
+def far_kernel(send, base, c1, c2, out):
     out[...] = base[...]
-    for s in range(ROUNDS * BT):
-        out[:, lanes(send[s])] += (c0, c1, c2)[s // BT][:, tile_of(s % BT)].astype(f32)
-
-
-def weights_kernel(slots, gws, gwn):
+    for s in range(BT, ROUNDS * BT):
+        out[send[s]] += (c1, c2)[s // BT - 1][:, tile_of(s % BT)].astype(f32)
+
+
+def last_kernel(send, base, c0, slots, gx, gws, gwn, acc):
     for j in range(NZC):
         out, row = (gwn, j // 2 * 8) if j < 8 else (gws, j // 2 * 8 - FR)
         out[row : row + 8, tile_of(j % 2)] = slots[j].astype(f32)
+    acc[...] = base[...]
+    for s in range(BT):
+        acc[send[s]] += c0[:, tile_of(s)].astype(f32)
+    for t in range(TILES):
+        gx[:, tile_of(t)] = acc[t]
 
 
 def call(kernel, ins, outs, scratch=(), flops=0, nbytes=1 << 20, aliases=()):
@@ -231,7 +235,7 @@
     base, y = call(
         back_kernel,
         (1, 1) + (0,) * 4,
-        (V((FR, LOCAL), f32), S((HR, LOCAL), bf16)),
+        (V((TILES, FR, TILE), f32), S((HR, LOCAL), bf16)),
         (V((TILES, FR, TILE), f32),),
     )(in_rows, in_cols, own, ga, in_adj, y)
     slots, base, b1 = lax.optimization_barrier((slots, base, b1))
@@ -242,9 +246,14 @@
     c0 = swap(b0, PAIRS[0])
     slots = call(sum_kernel, (0,), S((NZC, 8, TILE), bf16))(terms)
     slots = lax.all_to_all(slots, ZC, 0, 0, tiled=True)
-    gx = call(grad_x_kernel, (1, 0, 0, 0, 0), S((FR, LOCAL), f32))(bnd_send, base, c0, c1, c2)
+    base = call(far_kernel, (1, 0, 0, 0), V((TILES, FR, TILE), f32))(bnd_send, base, c1, c2)
     half = S((FR, F_HID), f32)
-    gws, gwn = call(weights_kernel, (0,), (half, half))(slots)
+    gx, gws, gwn = call(
+        last_kernel,
+        (1, 0, 0, 0),
+        (S((FR, LOCAL), f32), half, half),
+        (V((TILES, FR, TILE), f32),),
+    )(bnd_send, base, c0, slots)
     return y, gx, gws, gwn
 
 

time: 84.2 us -> 84.9 us (level)
    all_to_all x2, waiting for transfers between devices: 5.39 us -> 6.74 us  [shards(): slots = lax.all_to_all(slots, ZC, 0, 0, tiled=True)]
where the time goes in v10:
time: 84.9 us; the launch traced here: 84.2 us
  starting transfers between devices  51.8 us (61%)
  blocking collectives  12.3 us (14%)
  Pallas kernels  10.8 us (13%)
  waiting for transfers between devices  8.54 us (10%)
    ppermute x6, starting transfers between devices, swap(): return lax.ppermute(x, axis, [(0, 1), (1, 0)])  33.3 us
    all_to_all x2, starting transfers between devices, shards(): slots = lax.all_to_all(slots, ZC, 0, 0, tiled=True)  15.2 us
    all_to_all x1, blocking collectives, shards(): block = lax.all_to_all(give, 'f', 0, 0, tiled=True)  12.3 us
    pallas_call x9, Pallas kernels, apply(): return run(*near)  10.8 us
    all_to_all x2, waiting for transfers between devices, shards(): slots = lax.all_to_all(slots, ZC, 0, 0, tiled=True)  6.74 us
    all_to_all x1, starting transfers between devices, shards(): terms = lax.all_to_all(terms, Y, 0, 0, tiled=True)  3.34 us
  transfers between devices with their start and end apart: 9, of which 4 were waited for; matrix products, arithmetic and copies ran while one was open for 0% of the time, Pallas kernels for 7%

profile of v10, /device:TPU:1, one launch (start us, length us, event | category | flops | bytes accessed | tf_op | source)
XLA Modules:
  0.0 84.2 jit_solution(13920012274315541415)
XLA Ops:
  0.6 0.8 shard_map.129
  1.4 8.3 %collective-permute-start = (bf16[32,512]{1,0:T(8,128)(2,1)S(1)}, bf16[32,512]{1,0:T(8,128)(2,1)S(1)}, u32[]{:S(2)}, u32[]{:S(2)}) collective-permute-start(bf16[32,512]{1,0:T(8,128)(2,1)S(1)} %get-tuple-element.32), channel_id=1, source_target_pairs={{0,256},{256,0},{1,257},{257,1},{2,258},{258,2},{3,259},{259,3},{4... | collective-permute-start | bytes 98312 | tf_op jit(solution)/shard_map/ppermute | solution.py:195
  9.7 10.6 %collective-permute-start.1 = (bf16[32,512]{1,0:T(8,128)(2,1)S(1)}, bf16[32,512]{1,0:T(8,128)(2,1)S(1)}, u32[]{:S(2)}, u32[]{:S(2)}) collective-permute-start(bf16[32,512]{1,0:T(8,128)(2,1)S(1)} %get-tuple-element.33), channel_id=1, source_target_pairs={{0,32},{32,0},{1,33},{33,1},{2,34},{34,2},{3,35},{35,3},{4,36},{36... | collective-permute-start | bytes 98312 | tf_op jit(solution)/shard_map/ppermute | solution.py:195
  20.4 3.1 %collective-permute-start.2 = (bf16[32,512]{1,0:T(8,128)(2,1)S(1)}, bf16[32,512]{1,0:T(8,128)(2,1)S(1)}, u32[]{:S(2)}, u32[]{:S(2)}) collective-permute-start(bf16[32,512]{1,0:T(8,128)(2,1)S(1)} %get-tuple-element.34), channel_id=1, source_target_pairs={{0,8},{8,0},{1,9},{9,1},{2,10},{10,2},{3,11},{11,3},{4,12},{12,4},... | collective-permute-start | bytes 98312 | tf_op jit(solution)/shard_map/ppermute | solution.py:195
  23.5 2.1 %shard_map.130 = (bf16[12,128,128]{2,1,0:T(8,128)(2,1)S(1)}, bf16[12,128,128]{2,1,0:T(8,128)(2,1)S(1)}, bf16[32,256]{1,0:T(8,128)(2,1)S(1)}, bf16[32,256]{1,0:T(...) custom-call(s32[12]{0:T(128)} %rows.3, s32[12]{0:T(128)} %cols.3, ...), custom_call_target="tpu_custom_call" | custom-call | bytes 1048576 | tf_op jit(solution)/shard_map/pallas_call | solution.py:189
  25.6 0.0 collective-permute-done.r2
  25.6 0.0 collective-permute-done.1.r1
  25.6 0.0 collective-permute-done.2.r0
  25.6 1.0 %shard_map.131 = bf16[4,160,512]{2,1,0:T(8,128)(2,1)S(1)} custom-call(s32[12]{0:T(128)} %brows.3, bf16[32,512]{1,0:T(8,128)(2,1)S(1)} %collective-permute-done.r2, bf16[32,512]{1,0:T(8,128)(2,1)S(1)} %collective-permute-done.1.r1, bf16[32,512]{1,0:T(8,128)(2,1)S(1)} %collective-permute-done.2.r0, ...), custom_call_target="tpu_custom_call", output_to_operand_aliasing={{}: (6, {})} | custom-call | bytes 1048576 | tf_op jit(solution)/shard_map/pallas_call | solution.py:189
  26.6 12.3 %all_to_all.20.got = bf16[4,160,512]{2,1,0:T(8,128)(2,1)S(1)} all-to-all(bf16[4,160,512]{2,1,0:T(8,128)(2,1)S(1)} %shard_map.131), channel_id=1, replica_groups=mesh['y2'=2,'yl'=4,'z2'=2,'z1'=2,'z0'=2,'c'=2,'f'=4] {'f'}, dimensions={0} | all-to-all | bytes 1310720 | tf_op jit(solution)/shard_map/all_to_all | solution.py:219
  39.0 2.2 %shard_map.132 = (bf16[64,512]{1,0:T(8,128)(2,1)S(1)}, f32[4,32,128]{2,1,0:T(8,128)S(1)}, bf16[4,32,128]{2,1,0:T(8,128)(2,1)S(1)}, bf16[32,512]{1,0:T(8,128)(2,1...) custom-call(s32[12]{0:T(128)} %brows.3, bf16[4,160,512]{2,1,0:T(8,128)(2,1)S(1)} %all_to_all.20.got, ...), custom_call_target="tpu_custom_call" | custom-call | bytes 1048576 | tf_op jit(solution)/shard_map/pallas_call | solution.py:189
  41.1 7.3 %all-to-all-start.1 = ((f32[16,8,128]{2,1,0:T(8,128)}), f32[16,8,128]{2,1,0:T(8,128)S(1)}, u32[]{:S(2)}, u32[]{:S(2)}) async-start(f32[16,8,128]{2,1,0:T(8,128)} %get-tuple-element.46), calls=%async_computation.1 | async-start | bytes 131072 | tf_op jit(solution)/shard_map/all_to_all | solution.py:233
  48.4 1.9 %collective-permute-start.4 = (f32[32,512]{1,0:T(8,128)S(1)}, f32[32,512]{1,0:T(8,128)S(1)}, u32[]{:S(2)}, u32[]{:S(2)}) collective-permute-start(f32[32,512]{1,0:T(8,128)S(1)} %get-tuple-element.52), channel_id=1, source_target_pairs={{0,256},{256,0},{1,257},{257,1},{2,258},{258,2},{3,259},{259,3},{4... | collective-permute-start | bytes 196616 | tf_op jit(solution)/shard_map/ppermute | solution.py:195
  50.4 1.4 %shard_map.133 = (f32[4,32,128]{2,1,0:T(8,128)S(1)}, bf16[64,512]{1,0:T(8,128)(2,1)}) custom-call(s32[12]{0:T(128)} %rows.3, s32[12]{0:T(128)} %cols.3, f32[4,32,128]{2,1,0:T(8,128)S(1)} %get-tuple-element.41.own, bf16[4,32,128]{2,1,0:T(8,128)(2,1)S(1)} %get-tuple-element.42.ga, bf16[12,128,128]{2,1,0:T(8,128)(2,1)S(1)} %get-tuple-element.43.adj, ...), custom_call_target="tpu_custom_call" | custom-call | bytes 1048576 | tf_op jit(solution)/shard_map/pallas_call | solution.py:189
  51.8 4.4 %all-to-all-done.1.terms = f32[16,8,128]{2,1,0:T(8,128)S(1)} async-done(((f32[16,8,128]{2,1,0:T(8,128)}), f32[16,8,128]{2,1,0:T(8,128)S(1)}, u32[]{:S(2)}, u32[]{:S(2)}) %all-to-all-start.1) | async-done | bytes 65568 | tf_op jit(solution)/shard_map/all_to_all | solution.py:233
  56.3 0.6 shard_map.134
  56.9 3.3 %all-to-all-start.2 = ((f32[8,8,128]{2,1,0:T(8,128)}), f32[8,8,128]{2,1,0:T(8,128)S(1)}, u32[]{:S(2)}, u32[]{:S(2)}) async-start(f32[8,8,128]{2,1,0:T(8,128)} %shard_map.134), calls=%async_computation.2 | async-start | bytes 65536 | tf_op jit(solution)/shard_map/all_to_all | solution.py:244
  60.2 6.0 %collective-permute-start.3 = (f32[32,512]{1,0:T(8,128)S(1)}, f32[32,512]{1,0:T(8,128)S(1)}, u32[]{:S(2)}, u32[]{:S(2)}) collective-permute-start(f32[32,512]{1,0:T(8,128)S(1)} %get-tuple-element.50), channel_id=1, source_target_pairs={{0,32},{32,0},{1,33},{33,1},{2,34},{34,2},{3,35},{35,3},{4,36},{36... | collective-permute-start | bytes 196616 | tf_op jit(solution)/shard_map/ppermute | solution.py:195
  66.3 0.0 collective-permute-done.4.c2
  66.3 0.7 all-to-all-done.2.terms
  67.0 0.6 shard_map.136
  67.7 7.9 %all-to-all-start.3 = ((bf16[16,8,128]{2,1,0:T(8,128)(2,1)}), bf16[16,8,128]{2,1,0:T(8,128)(2,1)S(1)}, u32[]{:S(2)}, u32[]{:S(2)}) async-start(bf16[16,8,128]{2,1,0:T(8,128)(2,1)} %shard_map.136), calls=%async_computation.3 | async-start | bytes 65536 | tf_op jit(solution)/shard_map/all_to_all | solution.py:248
  75.5 3.3 %collective-permute-start.5 = (bf16[32,512]{1,0:T(8,128)(2,1)S(1)}, bf16[32,512]{1,0:T(8,128)(2,1)S(1)}, u32[]{:S(2)}, u32[]{:S(2)}) collective-permute-start(bf16[32,512]{1,0:T(8,128)(2,1)S(1)} %get-tuple-element.55), channel_id=1, source_target_pairs={{0,8},{8,0},{1,9},{9,1},{2,10},{10,2},{3,11},{11,3},{4,12},{12,4},... | collective-permute-start | bytes 98312 | tf_op jit(solution)/shard_map/ppermute | solution.py:195
  78.8 0.0 collective-permute-done.3.c1
  78.8 0.7 shard_map.135.base
  79.5 1.0 %collective-permute-done.5.c0 = bf16[32,512]{1,0:T(8,128)(2,1)S(1)} collective-permute-done((bf16[32,512]{1,0:T(8,128)(2,1)S(1)}, bf16[32,512]{1,0:T(8,128)(2,1)S(1)}, u32[]{:S(2)}, u32[]{:S(2)}) %collective-permute-start.5) | collective-permute-done | bytes 32800 | tf_op jit(solution)/shard_map/ppermute | solution.py:195
  80.6 2.3 %all-to-all-done.3.slots = bf16[16,8,128]{2,1,0:T(8,128)(2,1)S(1)} async-done(((bf16[16,8,128]{2,1,0:T(8,128)(2,1)}), bf16[16,8,128]{2,1,0:T(8,128)(2,1)S(1)}, u32[]{:S(2)}, u32[]{:S(2)}) %all-to-all-start.3) | async-done | bytes 32800 | tf_op jit(solution)/shard_map/all_to_all | solution.py:248
  82.9 1.3 %shard_map.137 = (f32[32,512]{1,0:T(8,128)}, f32[32,256]{1,0:T(8,128)}, f32[32,256]{1,0:T(8,128)}) custom-call(s32[12]{0:T(128)} %send.5, f32[4,32,128]{2,1,0:T(8,128)S(1)} %shard_map.135.base, bf16[32,512]{1,0:T(8,128)(2,1)S(1)} %collective-permute-done.5.c0, bf16[16,8,128]{2,1,0:T(8,128)(2,1)S(1)} %all-to-all-done.3.slots), custom_call_target="tpu_custom_call" | custom-call | bytes 1048576 | tf_op jit(solution)/shard_map/pallas_call | solution.py:189
Async XLA Ops:
  1.4 24.1 %collective-permute-start = (bf16[32,512]{1,0:T(8,128)(2,1)S(1)}, bf16[32,512]{1,0:T(8,128)(2,1)S(1)}, u32[]{:S(2)}, u32[]{:S(2)}) collective-permute-start(bf16[32,512]{1,0:T(8,128)(2,1)S(1)} %get-tuple-element.32), channel_id=1, source_target_pairs={{0,256},{256,0},{1,257},{257,1},{2,258},{258,2},{3,259},{259,3},{4... | collective-permute-start | bytes 98312 | tf_op jit(solution)/shard_map/ppermute | solution.py:195
  9.7 15.9 %collective-permute-start.1 = (bf16[32,512]{1,0:T(8,128)(2,1)S(1)}, bf16[32,512]{1,0:T(8,128)(2,1)S(1)}, u32[]{:S(2)}, u32[]{:S(2)}) collective-permute-start(bf16[32,512]{1,0:T(8,128)(2,1)S(1)} %get-tuple-element.33), channel_id=1, source_target_pairs={{0,32},{32,0},{1,33},{33,1},{2,34},{34,2},{3,35},{35,3},{4,36},{36... | collective-permute-start | bytes 98312 | tf_op jit(solution)/shard_map/ppermute | solution.py:195
  20.4 5.2 %collective-permute-start.2 = (bf16[32,512]{1,0:T(8,128)(2,1)S(1)}, bf16[32,512]{1,0:T(8,128)(2,1)S(1)}, u32[]{:S(2)}, u32[]{:S(2)}) collective-permute-start(bf16[32,512]{1,0:T(8,128)(2,1)S(1)} %get-tuple-element.34), channel_id=1, source_target_pairs={{0,8},{8,0},{1,9},{9,1},{2,10},{10,2},{3,11},{11,3},{4,12},{12,4},... | collective-permute-start | bytes 98312 | tf_op jit(solution)/shard_map/ppermute | solution.py:195
  41.1 15.1 %all-to-all-start.1 = ((f32[16,8,128]{2,1,0:T(8,128)}), f32[16,8,128]{2,1,0:T(8,128)S(1)}, u32[]{:S(2)}, u32[]{:S(2)}) async-start(f32[16,8,128]{2,1,0:T(8,128)} %get-tuple-element.46), calls=%async_computation.1 | async-start | bytes 131072 | tf_op jit(solution)/shard_map/all_to_all | solution.py:233
  48.4 17.8 %collective-permute-start.4 = (f32[32,512]{1,0:T(8,128)S(1)}, f32[32,512]{1,0:T(8,128)S(1)}, u32[]{:S(2)}, u32[]{:S(2)}) collective-permute-start(f32[32,512]{1,0:T(8,128)S(1)} %get-tuple-element.52), channel_id=1, source_target_pairs={{0,256},{256,0},{1,257},{257,1},{2,258},{258,2},{3,259},{259,3},{4... | collective-permute-start | bytes 196616 | tf_op jit(solution)/shard_map/ppermute | solution.py:195
  56.9 10.1 %all-to-all-start.2 = ((f32[8,8,128]{2,1,0:T(8,128)}), f32[8,8,128]{2,1,0:T(8,128)S(1)}, u32[]{:S(2)}, u32[]{:S(2)}) async-start(f32[8,8,128]{2,1,0:T(8,128)} %shard_map.134), calls=%async_computation.2 | async-start | bytes 65536 | tf_op jit(solution)/shard_map/all_to_all | solution.py:244
  60.2 18.6 %collective-permute-start.3 = (f32[32,512]{1,0:T(8,128)S(1)}, f32[32,512]{1,0:T(8,128)S(1)}, u32[]{:S(2)}, u32[]{:S(2)}) collective-permute-start(f32[32,512]{1,0:T(8,128)S(1)} %get-tuple-element.50), channel_id=1, source_target_pairs={{0,32},{32,0},{1,33},{33,1},{2,34},{34,2},{3,35},{35,3},{4,36},{36... | collective-permute-start | bytes 196616 | tf_op jit(solution)/shard_map/ppermute | solution.py:195
  67.7 15.2 %all-to-all-start.3 = ((bf16[16,8,128]{2,1,0:T(8,128)(2,1)}), bf16[16,8,128]{2,1,0:T(8,128)(2,1)S(1)}, u32[]{:S(2)}, u32[]{:S(2)}) async-start(bf16[16,8,128]{2,1,0:T(8,128)(2,1)} %shard_map.136), calls=%async_computation.3 | async-start | bytes 65536 | tf_op jit(solution)/shard_map/all_to_all | solution.py:248
  75.5 5.1 %collective-permute-start.5 = (bf16[32,512]{1,0:T(8,128)(2,1)S(1)}, bf16[32,512]{1,0:T(8,128)(2,1)S(1)}, u32[]{:S(2)}, u32[]{:S(2)}) collective-permute-start(bf16[32,512]{1,0:T(8,128)(2,1)S(1)} %get-tuple-element.55), channel_id=1, source_target_pairs={{0,8},{8,0},{1,9},{9,1},{2,10},{10,2},{3,11},{11,3},{4,12},{12,4},... | collective-permute-start | bytes 98312 | tf_op jit(solution)/shard_map/ppermute | solution.py:195

commit v11 on v8

--- a/solution.py
+++ b/solution.py
@@ -25,9 +25,9 @@
 AXES = ("y2", "yl", "z2", "z1", "z0", "c", "f")
 SIZES = (2, 4, 2, 2, 2, 2, 4)
 DOM = AXES[:6]
-Y = ("y2", "yl")
+Y = ("yl", "y2")
 NY = 8
-ZC = ("z2", "z1", "z0", "c")
+ZC = ("c", "z2", "z1", "z0")
 NZC = 16
 PAIRS = ("z0", "z2", "y2")
 

time: 84.2 us -> 83.5 us (level)
  waiting for transfers between devices: 7.91 us -> 6.19 us
  starting transfers between devices: 51.8 us -> 52.8 us
    all_to_all x2, waiting for transfers between devices: 5.39 us -> 4.41 us  [shards(): slots = lax.all_to_all(slots, ZC, 0, 0, tiled=True)]
  transfers between devices with their start and end apart: 9 -> 9, of which waited for: 4 -> 3; matrix products, arithmetic and copies ran while one was open for 0% -> 0% of each run, Pallas kernels for 7% -> 7%
where the time goes in v11:
time: 83.5 us; the launch traced here: 82.9 us
  starting transfers between devices  52.8 us (63%)
  blocking collectives  12.3 us (15%)
  Pallas kernels  10.8 us (13%)
  waiting for transfers between devices  6.19 us (7%)
    ppermute x6, starting transfers between devices, swap(): return lax.ppermute(x, axis, [(0, 1), (1, 0)])  33.9 us
    all_to_all x2, starting transfers between devices, shards(): slots = lax.all_to_all(slots, ZC, 0, 0, tiled=True)  15.6 us
    all_to_all x1, blocking collectives, shards(): block = lax.all_to_all(give, 'f', 0, 0, tiled=True)  12.3 us
    pallas_call x9, Pallas kernels, apply(): return run(*near)  10.8 us
    all_to_all x2, waiting for transfers between devices, shards(): slots = lax.all_to_all(slots, ZC, 0, 0, tiled=True)  4.41 us
    all_to_all x1, starting transfers between devices, shards(): terms = lax.all_to_all(terms, Y, 0, 0, tiled=True)  3.34 us
    ppermute x6, waiting for transfers between devices, swap(): return lax.ppermute(x, axis, [(0, 1), (1, 0)])  1.77 us
  transfers between devices with their start and end apart: 9, of which 3 were waited for; matrix products, arithmetic and copies ran while one was open for 0% of the time, Pallas kernels for 7%

profile of v11, /device:TPU:1, one launch (start us, length us, event | category | flops | bytes accessed | tf_op | source)
XLA Modules:
  0.0 82.9 jit_solution(17398063390231579429)
XLA Ops:
  0.6 0.8 shard_map.129
  1.4 8.3 %collective-permute-start = (bf16[32,512]{1,0:T(8,128)(2,1)S(1)}, bf16[32,512]{1,0:T(8,128)(2,1)S(1)}, u32[]{:S(2)}, u32[]{:S(2)}) collective-permute-start(bf16[32,512]{1,0:T(8,128)(2,1)S(1)} %get-tuple-element.31), channel_id=1, source_target_pairs={{0,256},{256,0},{1,257},{257,1},{2,258},{258,2},{3,259},{259,3},{4... | collective-permute-start | bytes 98312 | tf_op jit(solution)/shard_map/ppermute | solution.py:191
  9.7 10.6 %collective-permute-start.1 = (bf16[32,512]{1,0:T(8,128)(2,1)S(1)}, bf16[32,512]{1,0:T(8,128)(2,1)S(1)}, u32[]{:S(2)}, u32[]{:S(2)}) collective-permute-start(bf16[32,512]{1,0:T(8,128)(2,1)S(1)} %get-tuple-element.32), channel_id=1, source_target_pairs={{0,32},{32,0},{1,33},{33,1},{2,34},{34,2},{3,35},{35,3},{4,36},{36... | collective-permute-start | bytes 98312 | tf_op jit(solution)/shard_map/ppermute | solution.py:191
  20.4 3.1 %collective-permute-start.2 = (bf16[32,512]{1,0:T(8,128)(2,1)S(1)}, bf16[32,512]{1,0:T(8,128)(2,1)S(1)}, u32[]{:S(2)}, u32[]{:S(2)}) collective-permute-start(bf16[32,512]{1,0:T(8,128)(2,1)S(1)} %get-tuple-element.33), channel_id=1, source_target_pairs={{0,8},{8,0},{1,9},{9,1},{2,10},{10,2},{3,11},{11,3},{4,12},{12,4},... | collective-permute-start | bytes 98312 | tf_op jit(solution)/shard_map/ppermute | solution.py:191
  23.5 2.1 %shard_map.130 = (bf16[12,128,128]{2,1,0:T(8,128)(2,1)S(1)}, bf16[12,128,128]{2,1,0:T(8,128)(2,1)S(1)}, bf16[32,256]{1,0:T(8,128)(2,1)S(1)}, bf16[32,256]{1,0:T(...) custom-call(s32[12]{0:T(128)} %rows.3, s32[12]{0:T(128)} %cols.3, ...), custom_call_target="tpu_custom_call" | custom-call | bytes 1048576 | tf_op jit(solution)/shard_map/pallas_call | solution.py:185
  25.6 0.0 collective-permute-done.r2
  25.6 0.0 collective-permute-done.1.r1
  25.6 0.0 collective-permute-done.2.r0
  25.6 1.0 %shard_map.131 = bf16[4,160,512]{2,1,0:T(8,128)(2,1)S(1)} custom-call(s32[12]{0:T(128)} %brows.3, bf16[32,512]{1,0:T(8,128)(2,1)S(1)} %collective-permute-done.r2, bf16[32,512]{1,0:T(8,128)(2,1)S(1)} %collective-permute-done.1.r1, bf16[32,512]{1,0:T(8,128)(2,1)S(1)} %collective-permute-done.2.r0, ...), custom_call_target="tpu_custom_call", output_to_operand_aliasing={{}: (6, {})} | custom-call | bytes 1048576 | tf_op jit(solution)/shard_map/pallas_call | solution.py:185
  26.6 12.3 %all_to_all.20.got = bf16[4,160,512]{2,1,0:T(8,128)(2,1)S(1)} all-to-all(bf16[4,160,512]{2,1,0:T(8,128)(2,1)S(1)} %shard_map.131), channel_id=1, replica_groups=mesh['y2'=2,'yl'=4,'z2'=2,'z1'=2,'z0'=2,'c'=2,'f'=4] {'f'}, dimensions={0} | all-to-all | bytes 1310720 | tf_op jit(solution)/shard_map/all_to_all | solution.py:215
  39.0 2.2 %shard_map.132 = (bf16[64,512]{1,0:T(8,128)(2,1)S(1)}, f32[4,32,128]{2,1,0:T(8,128)S(1)}, bf16[4,32,128]{2,1,0:T(8,128)(2,1)S(1)}, bf16[32,512]{1,0:T(8,128)(2,1...) custom-call(s32[12]{0:T(128)} %brows.3, bf16[4,160,512]{2,1,0:T(8,128)(2,1)S(1)} %all_to_all.20.got, ...), custom_call_target="tpu_custom_call" | custom-call | bytes 1048576 | tf_op jit(solution)/shard_map/pallas_call | solution.py:185
  41.1 7.3 %all-to-all-start.1 = ((f32[16,8,128]{2,1,0:T(8,128)}), f32[16,8,128]{2,1,0:T(8,128)S(1)}, u32[]{:S(2)}, u32[]{:S(2)}) async-start(f32[16,8,128]{2,1,0:T(8,128)} %get-tuple-element.45), calls=%async_computation.1 | async-start | bytes 131072 | tf_op jit(solution)/shard_map/all_to_all | solution.py:229
  48.5 1.9 %collective-permute-start.3 = (f32[32,512]{1,0:T(8,128)S(1)}, f32[32,512]{1,0:T(8,128)S(1)}, u32[]{:S(2)}, u32[]{:S(2)}) collective-permute-start(f32[32,512]{1,0:T(8,128)S(1)} %get-tuple-element.50), channel_id=1, source_target_pairs={{0,256},{256,0},{1,257},{257,1},{2,258},{258,2},{3,259},{259,3},{4... | collective-permute-start | bytes 196616 | tf_op jit(solution)/shard_map/ppermute | solution.py:191
  50.4 1.4 %shard_map.133 = (f32[32,512]{1,0:T(8,128)S(1)}, bf16[64,512]{1,0:T(8,128)(2,1)}) custom-call(s32[12]{0:T(128)} %rows.3, s32[12]{0:T(128)} %cols.3, f32[4,32,128]{2,1,0:T(8,128)S(1)} %get-tuple-element.40.own, bf16[4,32,128]{2,1,0:T(8,128)(2,1)S(1)} %get-tuple-element.41.ga, bf16[12,128,128]{2,1,0:T(8,128)(2,1)S(1)} %get-tuple-element.42.adj, ...), custom_call_target="tpu_custom_call" | custom-call | bytes 1048576 | tf_op jit(solution)/shard_map/pallas_call | solution.py:185
  51.8 3.8 %all-to-all-done.1.terms = f32[16,8,128]{2,1,0:T(8,128)S(1)} async-done(((f32[16,8,128]{2,1,0:T(8,128)}), f32[16,8,128]{2,1,0:T(8,128)S(1)}, u32[]{:S(2)}, u32[]{:S(2)}) %all-to-all-start.1) | async-done | bytes 65568 | tf_op jit(solution)/shard_map/all_to_all | solution.py:229
  55.6 0.6 shard_map.134
  56.2 3.3 %all-to-all-start.2 = ((f32[8,8,128]{2,1,0:T(8,128)}), f32[8,8,128]{2,1,0:T(8,128)S(1)}, u32[]{:S(2)}, u32[]{:S(2)}) async-start(f32[8,8,128]{2,1,0:T(8,128)} %shard_map.134), calls=%async_computation.2 | async-start | bytes 65536 | tf_op jit(solution)/shard_map/all_to_all | solution.py:240
  59.6 6.7 %collective-permute-start.5 = (f32[32,512]{1,0:T(8,128)S(1)}, f32[32,512]{1,0:T(8,128)S(1)}, u32[]{:S(2)}, u32[]{:S(2)}) collective-permute-start(f32[32,512]{1,0:T(8,128)S(1)} %get-tuple-element.53), channel_id=1, source_target_pairs={{0,32},{32,0},{1,33},{33,1},{2,34},{34,2},{3,35},{35,3},{4,36},{36... | collective-permute-start | bytes 196616 | tf_op jit(solution)/shard_map/ppermute | solution.py:191
  66.3 0.0 collective-permute-done.3.c2
  66.3 0.0 all-to-all-done.2.terms
  66.3 0.6 shard_map.136
  66.9 8.3 %all-to-all-start.3 = ((bf16[16,8,128]{2,1,0:T(8,128)(2,1)}), bf16[16,8,128]{2,1,0:T(8,128)(2,1)S(1)}, u32[]{:S(2)}, u32[]{:S(2)}) async-start(bf16[16,8,128]{2,1,0:T(8,128)(2,1)} %shard_map.136), calls=%async_computation.3 | async-start | bytes 65536 | tf_op jit(solution)/shard_map/all_to_all | solution.py:244
  75.2 3.3 %collective-permute-start.4 = (bf16[32,512]{1,0:T(8,128)(2,1)S(1)}, bf16[32,512]{1,0:T(8,128)(2,1)S(1)}, u32[]{:S(2)}, u32[]{:S(2)}) collective-permute-start(bf16[32,512]{1,0:T(8,128)(2,1)S(1)} %get-tuple-element.52), channel_id=1, source_target_pairs={{0,8},{8,0},{1,9},{9,1},{2,10},{10,2},{3,11},{11,3},{4,12},{12,4},... | collective-permute-start | bytes 98312 | tf_op jit(solution)/shard_map/ppermute | solution.py:191
  78.5 0.0 collective-permute-done.5.c1
  78.5 1.8 %collective-permute-done.4.c0 = bf16[32,512]{1,0:T(8,128)(2,1)S(1)} collective-permute-done((bf16[32,512]{1,0:T(8,128)(2,1)S(1)}, bf16[32,512]{1,0:T(8,128)(2,1)S(1)}, u32[]{:S(2)}, u32[]{:S(2)}) %collective-permute-start.4) | collective-permute-done | bytes 32800 | tf_op jit(solution)/shard_map/ppermute | solution.py:191
  80.3 1.4 %shard_map.135 = f32[32,512]{1,0:T(8,128)} custom-call(s32[12]{0:T(128)} %send.3, f32[32,512]{1,0:T(8,128)S(1)} %get-tuple-element.48.base, bf16[32,512]{1,0:T(8,128)(2,1)S(1)} %collective-permute-done.4.c0, f32[32,512]{1,0:T(8,128)S(1)} %collective-permute-done.5.c1, f32[32,512]{1,0:T(8,128)S(1)} %collective-permute-done.3.c2), custom_call_target="tpu_custom_call" | custom-call | bytes 1048576 | tf_op jit(solution)/shard_map/pallas_call | solution.py:185
  81.6 0.6 all-to-all-done.3.slots
  82.3 0.6 shard_map.137
Async XLA Ops:
  1.4 24.1 %collective-permute-start = (bf16[32,512]{1,0:T(8,128)(2,1)S(1)}, bf16[32,512]{1,0:T(8,128)(2,1)S(1)}, u32[]{:S(2)}, u32[]{:S(2)}) collective-permute-start(bf16[32,512]{1,0:T(8,128)(2,1)S(1)} %get-tuple-element.31), channel_id=1, source_target_pairs={{0,256},{256,0},{1,257},{257,1},{2,258},{258,2},{3,259},{259,3},{4... | collective-permute-start | bytes 98312 | tf_op jit(solution)/shard_map/ppermute | solution.py:191
  9.7 15.9 %collective-permute-start.1 = (bf16[32,512]{1,0:T(8,128)(2,1)S(1)}, bf16[32,512]{1,0:T(8,128)(2,1)S(1)}, u32[]{:S(2)}, u32[]{:S(2)}) collective-permute-start(bf16[32,512]{1,0:T(8,128)(2,1)S(1)} %get-tuple-element.32), channel_id=1, source_target_pairs={{0,32},{32,0},{1,33},{33,1},{2,34},{34,2},{3,35},{35,3},{4,36},{36... | collective-permute-start | bytes 98312 | tf_op jit(solution)/shard_map/ppermute | solution.py:191
  20.4 5.2 %collective-permute-start.2 = (bf16[32,512]{1,0:T(8,128)(2,1)S(1)}, bf16[32,512]{1,0:T(8,128)(2,1)S(1)}, u32[]{:S(2)}, u32[]{:S(2)}) collective-permute-start(bf16[32,512]{1,0:T(8,128)(2,1)S(1)} %get-tuple-element.33), channel_id=1, source_target_pairs={{0,8},{8,0},{1,9},{9,1},{2,10},{10,2},{3,11},{11,3},{4,12},{12,4},... | collective-permute-start | bytes 98312 | tf_op jit(solution)/shard_map/ppermute | solution.py:191
  41.1 14.5 %all-to-all-start.1 = ((f32[16,8,128]{2,1,0:T(8,128)}), f32[16,8,128]{2,1,0:T(8,128)S(1)}, u32[]{:S(2)}, u32[]{:S(2)}) async-start(f32[16,8,128]{2,1,0:T(8,128)} %get-tuple-element.45), calls=%async_computation.1 | async-start | bytes 131072 | tf_op jit(solution)/shard_map/all_to_all | solution.py:229
  48.5 17.8 %collective-permute-start.3 = (f32[32,512]{1,0:T(8,128)S(1)}, f32[32,512]{1,0:T(8,128)S(1)}, u32[]{:S(2)}, u32[]{:S(2)}) collective-permute-start(f32[32,512]{1,0:T(8,128)S(1)} %get-tuple-element.50), channel_id=1, source_target_pairs={{0,256},{256,0},{1,257},{257,1},{2,258},{258,2},{3,259},{259,3},{4... | collective-permute-start | bytes 196616 | tf_op jit(solution)/shard_map/ppermute | solution.py:191
  56.2 10.0 %all-to-all-start.2 = ((f32[8,8,128]{2,1,0:T(8,128)}), f32[8,8,128]{2,1,0:T(8,128)S(1)}, u32[]{:S(2)}, u32[]{:S(2)}) async-start(f32[8,8,128]{2,1,0:T(8,128)} %shard_map.134), calls=%async_computation.2 | async-start | bytes 65536 | tf_op jit(solution)/shard_map/all_to_all | solution.py:240
  59.6 18.9 %collective-permute-start.5 = (f32[32,512]{1,0:T(8,128)S(1)}, f32[32,512]{1,0:T(8,128)S(1)}, u32[]{:S(2)}, u32[]{:S(2)}) collective-permute-start(f32[32,512]{1,0:T(8,128)S(1)} %get-tuple-element.53), channel_id=1, source_target_pairs={{0,32},{32,0},{1,33},{33,1},{2,34},{34,2},{3,35},{35,3},{4,36},{36... | collective-permute-start | bytes 196616 | tf_op jit(solution)/shard_map/ppermute | solution.py:191
  66.9 15.3 %all-to-all-start.3 = ((bf16[16,8,128]{2,1,0:T(8,128)(2,1)}), bf16[16,8,128]{2,1,0:T(8,128)(2,1)S(1)}, u32[]{:S(2)}, u32[]{:S(2)}) async-start(bf16[16,8,128]{2,1,0:T(8,128)(2,1)} %shard_map.136), calls=%async_computation.3 | async-start | bytes 65536 | tf_op jit(solution)/shard_map/all_to_all | solution.py:244
  75.2 5.1 %collective-permute-start.4 = (bf16[32,512]{1,0:T(8,128)(2,1)S(1)}, bf16[32,512]{1,0:T(8,128)(2,1)S(1)}, u32[]{:S(2)}, u32[]{:S(2)}) collective-permute-start(bf16[32,512]{1,0:T(8,128)(2,1)S(1)} %get-tuple-element.52), channel_id=1, source_target_pairs={{0,8},{8,0},{1,9},{9,1},{2,10},{10,2},{3,11},{11,3},{4,12},{12,4},... | collective-permute-start | bytes 98312 | tf_op jit(solution)/shard_map/ppermute | solution.py:191
